TPU v7x, 32 devices: a whole 2x2x4 slice. The times are simulated.
32 devices in a mesh: seq: 32 (over z, y, x, core).
Axes of the slice: x: 2, y: 2, z: 4, core: 2. Of those that a mesh axis runs over, the one named last changes fastest.
Arguments:
- tokens: bfloat16 [4096, 1600], P('seq'), may hold values from -6 to 6
- seg_ids: int32 [4096], P('seq'), may hold values from 0 to 8, as said below
- meta_index: int32 [4096], P('seq'), may hold values from 0 to 128, as said below
- meta_table: bfloat16 [128, 1600], replicated, may hold values from -6 to 6
- mixer_gain: float32 [1600], replicated, may hold values from 0.5 to 1.5
- attn_weight: bfloat16 [1600, 3840], replicated, may hold values from -0.15625 to 0.15625
- ssm_weight: bfloat16 [1600, 6400], replicated, may hold values from -0.15625 to 0.15625
- select_weight: bfloat16 [1600, 82], replicated, may hold values from -0.15625 to 0.15625
- conv_weight: float32 [4, 3200], replicated, may hold values from -4 to 4
- step_bias: float32 [50], replicated, may hold values from -1 to 1
- decay_log: float32 [50], replicated, may hold values from -9 to -3
- skip_gain: float32 [50], replicated, may hold values from 0.5 to 1.5
- ssm_down: bfloat16 [3200, 1600], replicated, may hold values from -0.109375 to 0.109375
- attn_beta: float32 [1600], replicated, may hold values from 0.5 to 1.5
- ssm_beta: float32 [1600], replicated, may hold values from 0.5 to 1.5
- ffn_gain: float32 [1600], replicated, may hold values from 0.5 to 1.5
- gate_up: bfloat16 [1600, 11008], replicated, may hold values from -0.15625 to 0.15625
- ffn_down: bfloat16 [5504, 1600], replicated, may hold values from -0.078125 to 0.078125
- cotangent: bfloat16 [4096, 1600], P('seq'), may hold values from -6 to 6
Outputs:
- layer_out: bfloat16 [4096, 1600], P('seq')
- grad_tokens: bfloat16 [4096, 1600], P('seq')
- grad_meta: float32 [128, 1600], replicated
- grad_mixer_gain: float32 [1600], replicated
- grad_attn: float32 [1600, 3840], P(None, 'seq')
- grad_ssm: float32 [1600, 6400], P(None, 'seq')
- grad_select: float32 [1600, 82], replicated
- grad_conv: float32 [4, 3200], replicated
- grad_step_bias: float32 [50], replicated
- grad_decay: float32 [50], replicated
- grad_skip: float32 [50], replicated
- grad_ssm_down: float32 [3200, 1600], P('seq')
- grad_attn_beta: float32 [1600], replicated
- grad_ssm_beta: float32 [1600], replicated
- grad_ffn_gain: float32 [1600], replicated
- grad_gate_up: float32 [1600, 11008], P(None, 'seq')
- grad_ffn_down: float32 [5504, 1600], P('seq')
Inputs may be any that keep to these rules, and one draw needn't show every extreme that they name: `seg_ids`: item numbers never fall along the tokens. Tokens 4 * 128 up to 2560 hold items of exactly 2048 tokens, each starting 2048 tokens after the one before; every other item holds more than 128 tokens and fewer than 384. No token lies 2048 or more positions after the first token of its item. `meta_index`: A token's place in its item where that is below 128, else 128.
All inputs are finite; a program needn't handle non-finite values.
Results may differ from a plain program's by a relative error of at most 0.018.
Values may be sent and summed in bfloat16 or wider, within the bound.
A program may use at most 512 MiB of HBM per device.

v0:
```python
from functools import partial
import math

import jax
import jax.numpy as jnp
from jax import lax
from jax.sharding import PartitionSpec as P

HEADS = 25
GROUPS = 5
HEAD = 64
INNER = 3200
STATE = 16
CONV = 4
FF = 5504
META = 128
SHEAD = 64
SPAN = 16
LEAST_DEV = 64


eps = 1e-05
highest = lax.Precision.HIGHEST


def from_behind(x, axis, by):
    count = lax.axis_size(axis)
    pairs = [(i, i + by) for i in range(count) if 0 <= i + by < count]
    return lax.ppermute(x, axis, pairs)


def carried_in_2(x, axis, combine, identity, reverse):
    count, place = (lax.axis_size(axis), lax.axis_index(axis))
    everything = jax.tree.map(
        lambda part, kind: lax.all_gather(part.astype(kind), axis),
        x,
        jax.tree.map(lambda a: jnp.bfloat16 if a.dtype == jnp.float32 else a.dtype, x),
    )
    start = jax.tree.map(
        lambda part, zero: jnp.broadcast_to(jnp.asarray(zero, part.dtype), part.shape), x, identity
    )

    def hop(k, before):
        at = count - 1 - k if reverse else k
        reached = at > place if reverse else at < place
        new = combine(
            before, jax.tree.map(lambda part, own: part[at].astype(own.dtype), everything, x)
        )
        return jax.tree.map(lambda a, b: jnp.where(reached, a, b), new, before)

    return lax.fori_loop(0, count, hop, start)


def passed_along(x, axis, by):
    count = lax.axis_size(axis)
    return lax.ppermute(x, axis, [(i, (i + by) % count) for i in range(count)])


def as_sent(x):
    return jax.tree.map(lambda a: a.astype(jnp.bfloat16) if a.dtype == jnp.float32 else a, x)


def rms_scale(entries):
    return entries * lax.rsqrt(jnp.mean(entries * entries, axis=-1, keepdims=True) + eps)


def scaled_norm(entries, gain):
    return rms_scale(entries) * gain


def branch_mix(attn_proj, ssm_proj_out, attn_beta, ssm_beta):
    return attn_beta * rms_scale(attn_proj) + ssm_beta * rms_scale(ssm_proj_out)


def silu_slope(entries):
    sigma = jax.nn.sigmoid(entries)
    return sigma * (1.0 + entries * (1.0 - sigma))


def conv_local(conv_in, tail_x, conv_weight, seg_ids, tail_seg):
    row_count = conv_in.shape[0]
    tap_count = conv_weight.shape[0]
    extended = jnp.concatenate([tail_x, conv_in], 0)
    ext_seg = jnp.concatenate([tail_seg, seg_ids], 0)
    summed = conv_weight[0] * conv_in
    for tap_lag in range(1, tap_count):
        first_row = tap_count - 1 - tap_lag
        lagged = extended[first_row : first_row + row_count]
        same_item = (ext_seg[first_row : first_row + row_count] == seg_ids)[:, None]
        summed = summed + conv_weight[tap_lag] * jnp.where(same_item, lagged, 0.0)
    return jax.nn.silu(summed)


def ssm_parts(conv_in, select, tail_x, conv_weight, step_bias, decay_log, seg_ids, tail_seg):
    row_count = conv_in.shape[0]
    conv_out = conv_local(conv_in, tail_x, conv_weight, seg_ids, tail_seg)
    heads_x = conv_out.reshape(row_count, -1, SHEAD)
    b_proj = select[:, :STATE]
    c_proj = select[:, STATE : 2 * STATE]
    step_size = jax.nn.softplus(select[:, 2 * STATE :] + step_bias)
    log_decay = -step_size * jnp.exp(decay_log)
    lower_tri = (jnp.arange(row_count)[:, None] >= jnp.arange(row_count)[None, :]).astype(
        jnp.float32
    )
    cum_decay = jnp.dot(lower_tri, log_decay, precision=highest)
    scaled_x = heads_x * step_size[:, :, None]
    return (heads_x, b_proj, c_proj, cum_decay, scaled_x, lower_tri)


def ssm_output(
    conv_in,
    select,
    tail_x,
    conv_weight,
    step_bias,
    decay_log,
    skip_gain,
    held_in,
    seg_ids,
    tail_seg,
):
    heads_x, b_proj, c_proj, cum_decay, scaled_x, lower_tri = ssm_parts(
        conv_in, select, tail_x, conv_weight, step_bias, decay_log, seg_ids, tail_seg
    )
    seg_prev = tail_seg[-1]
    same_item = (seg_ids[:, None] == seg_ids[None, :]) & (lower_tri > 0)
    exponent = jnp.where(same_item[None], cum_decay.T[:, :, None] - cum_decay.T[:, None, :], -1e30)
    weights = jnp.exp(exponent) * jnp.dot(c_proj, b_proj.T, precision=highest)[None]
    local_part = jnp.einsum("htr,rhp->thp", weights, scaled_x, precision=highest)
    follow = (seg_ids == seg_prev).astype(jnp.float32)
    carry_weight = jnp.exp(cum_decay) * follow[:, None]
    carried = jnp.einsum("th,hpn,tn->thp", carry_weight, held_in, c_proj, precision=highest)
    outputs = local_part + carried + skip_gain[None, :, None] * heads_x
    return outputs.reshape(conv_in.shape[0], -1)


def ssm_state(conv_in, select, tail_x, conv_weight, step_bias, decay_log, seg_ids, tail_seg):
    heads_x, b_proj, c_proj, cum_decay, scaled_x, lower_tri = ssm_parts(
        conv_in, select, tail_x, conv_weight, step_bias, decay_log, seg_ids, tail_seg
    )
    seg_prev = tail_seg[-1]
    last_same = (seg_ids == seg_ids[-1]).astype(jnp.float32)
    last_weight = jnp.exp(cum_decay[-1][None, :] - cum_decay) * last_same[:, None]
    fresh_state = jnp.einsum("rh,rhp,rn->hpn", last_weight, scaled_x, b_proj, precision=highest)
    through = (seg_ids[-1] == seg_prev).astype(jnp.float32)
    return (fresh_state, jnp.exp(cum_decay[-1]) * through)


def chain_forward(earlier, later):
    return (earlier[0] * later[0], later[0][:, None, None] * earlier[1] + later[1])


def chain_backward(earlier, later):
    return (later[0] * earlier[0], later[1] + later[0][:, None, None] * earlier[1])


def block_allowed(seg_ids, key_seg, source, row_count, device_index):
    query_pos = device_index * row_count + jnp.arange(row_count, dtype=jnp.int32)
    key_pos = source * row_count + jnp.arange(row_count, dtype=jnp.int32)
    return (seg_ids[:, None] == key_seg[None, :]) & (key_pos[None, :] <= query_pos[:, None])


def attend_block(carried_in, queries, key_rows, value_rows, allowed, score_scale):
    run_max, run_sum, run_acc = carried_in
    scores = (
        jnp.einsum("tgjd,rgd->gjtr", queries, key_rows, preferred_element_type=jnp.float32)
        * score_scale
    )
    scores = jnp.where(allowed, scores, -1e30)
    new_max = jnp.maximum(run_max, jnp.max(scores, axis=-1))
    probs = jnp.where(allowed, jnp.exp(scores - new_max[..., None]), 0.0)
    fade = jnp.exp(run_max - new_max)
    run_sum = run_sum * fade + jnp.sum(probs, axis=-1)
    run_acc = run_acc * fade[..., None] + jnp.einsum(
        "gjtr,rgd->gjtd", probs.astype(jnp.bfloat16), value_rows, preferred_element_type=jnp.float32
    )
    return (new_max, run_sum, run_acc)


def attend_back(
    grads_in, queries, key_rows, value_rows, allowed, score_scale, log_sum, out_grad, row_dot
):
    grad_q, grad_k, grad_v = grads_in
    scores = (
        jnp.einsum("tgjd,rgd->gjtr", queries, key_rows, preferred_element_type=jnp.float32)
        * score_scale
    )
    probs = jnp.where(allowed, jnp.exp(scores - log_sum[..., None]), 0.0)
    grad_v = grad_v + jnp.einsum(
        "gjtr,tgjd->rgd", probs.astype(jnp.bfloat16), out_grad, preferred_element_type=jnp.float32
    )
    grad_probs = jnp.einsum(
        "tgjd,rgd->gjtr", out_grad, value_rows, preferred_element_type=jnp.float32
    )
    grad_scores = (probs * (grad_probs - row_dot[..., None])).astype(jnp.bfloat16)
    grad_q = (
        grad_q
        + jnp.einsum("gjtr,rgd->tgjd", grad_scores, key_rows, preferred_element_type=jnp.float32)
        * score_scale
    )
    grad_k = (
        grad_k
        + jnp.einsum("gjtr,tgjd->rgd", grad_scores, queries, preferred_element_type=jnp.float32)
        * score_scale
    )
    return (grad_q, grad_k, grad_v)


def per_device(
    tokens,
    seg_ids,
    meta_index,
    meta_table,
    mixer_gain,
    attn_weight,
    ssm_weight,
    select_weight,
    conv_weight,
    step_bias,
    decay_log,
    skip_gain,
    ssm_down,
    attn_beta,
    ssm_beta,
    ffn_gain,
    gate_up,
    ffn_down,
    cotangent,
):
    row_count = tokens.shape[0]
    model_width = tokens.shape[1]
    kv_width = GROUPS * HEAD
    per_group = HEADS // GROUPS
    qkv_cols = model_width + 2 * kv_width
    score_scale = 1.0 / math.sqrt(HEAD)
    devices = lax.axis_size("seq")
    device_index = lax.axis_index("seq")
    hop_count = min(devices // 2, max(SPAN, LEAST_DEV * devices // row_count))
    one_hot = (meta_index[:, None] == jnp.arange(META, dtype=jnp.int32)[None, :]).astype(
        jnp.float32
    )
    is_meta = (meta_index < META)[:, None]
    layer_in = jnp.where(
        is_meta,
        jnp.dot(one_hot.astype(jnp.bfloat16), meta_table, preferred_element_type=jnp.float32),
        tokens.astype(jnp.float32),
    )
    normed = scaled_norm(layer_in, mixer_gain).astype(jnp.bfloat16)
    proj_qkv = jnp.dot(
        normed, attn_weight[:, :qkv_cols], preferred_element_type=jnp.float32
    ).astype(jnp.bfloat16)
    queries = proj_qkv[:, :model_width].reshape(row_count, GROUPS, per_group, HEAD)
    keys = proj_qkv[:, model_width : model_width + kv_width].reshape(row_count, GROUPS, HEAD)
    values = proj_qkv[:, model_width + kv_width :].reshape(row_count, GROUPS, HEAD)

    def visit_forward(carried_in, key_rows, value_rows, key_seg, hop):
        source = (device_index - hop) % devices
        allowed = block_allowed(seg_ids, key_seg, source, row_count, device_index)
        return attend_block(carried_in, queries, key_rows, value_rows, allowed, score_scale)

    start_carry = (
        jnp.full((GROUPS, per_group, row_count), -1e30, jnp.float32),
        jnp.zeros((GROUPS, per_group, row_count), jnp.float32),
        jnp.zeros((GROUPS, per_group, row_count, HEAD), jnp.float32),
    )
    first_carry = visit_forward(start_carry, keys, values, seg_ids, 0)

    def forward_step(hop, loop_state):
        key_rows, value_rows, key_seg, carried_in = loop_state
        key_rows, value_rows, key_seg = from_behind((key_rows, value_rows, key_seg), "seq", 1)
        return (
            key_rows,
            value_rows,
            key_seg,
            visit_forward(carried_in, key_rows, value_rows, key_seg, hop),
        )

    loop_out = lax.fori_loop(1, hop_count, forward_step, (keys, values, seg_ids, first_carry))
    run_max, run_sum, run_acc = loop_out[3]
    log_sum = run_max + jnp.log(run_sum)
    attn_full = run_acc / run_sum[..., None]
    attended = (
        jnp.transpose(attn_full, (2, 0, 1, 3)).reshape(row_count, model_width).astype(jnp.bfloat16)
    )
    out_weight = attn_weight[:, qkv_cols:]
    attn_proj = jnp.dot(attended, out_weight.T, preferred_element_type=jnp.float32)
    ssm_proj = jnp.dot(normed, ssm_weight, preferred_element_type=jnp.float32)
    conv_in = ssm_proj[:, :INNER]
    z_gate = ssm_proj[:, INNER:]
    select = jnp.dot(normed, select_weight, preferred_element_type=jnp.float32)
    tail_x, tail_seg = (
        from_behind(conv_in[row_count - CONV + 1 :].astype(jnp.bfloat16), "seq", 1).astype(
            jnp.float32
        ),
        from_behind(seg_ids[row_count - CONV + 1 :], "seq", 1),
    )
    (fresh_state, decay_all), state_pull = jax.vjp(
        partial(ssm_state, seg_ids=seg_ids, tail_seg=tail_seg),
        conv_in,
        select,
        tail_x,
        conv_weight,
        step_bias,
        decay_log,
    )
    carry_identity = (jnp.ones_like(decay_all), jnp.zeros_like(fresh_state))
    held_in = carried_in_2((decay_all, fresh_state), "seq", chain_forward, carry_identity, False)[1]
    scanned, output_pull = jax.vjp(
        partial(ssm_output, seg_ids=seg_ids, tail_seg=tail_seg),
        conv_in,
        select,
        tail_x,
        conv_weight,
        step_bias,
        decay_log,
        skip_gain,
        held_in,
    )
    gated = (scanned * jax.nn.silu(z_gate)).astype(jnp.bfloat16)
    ssm_proj_out = jnp.dot(gated, ssm_down, preferred_element_type=jnp.float32)
    mixed_terms, mix_pull = jax.vjp(branch_mix, attn_proj, ssm_proj_out, attn_beta, ssm_beta)
    hidden1 = layer_in + mixed_terms
    ffn_in_f, ffn_norm_pull = jax.vjp(scaled_norm, hidden1, ffn_gain)
    ffn_in = ffn_in_f.astype(jnp.bfloat16)
    gate_vals = jnp.dot(ffn_in, gate_up, preferred_element_type=jnp.float32)
    gate_part = gate_vals[:, :FF]
    up_part = gate_vals[:, FF:]
    hidden = (jax.nn.silu(gate_part) * up_part).astype(jnp.bfloat16)
    layer_out = (hidden1 + jnp.dot(hidden, ffn_down, preferred_element_type=jnp.float32)).astype(
        jnp.bfloat16
    )
    grad_hidden = (
        jnp.dot(cotangent, ffn_down.T, preferred_element_type=jnp.float32)
        .astype(jnp.bfloat16)
        .astype(jnp.float32)
    )
    grad_ffn_down = jnp.dot(hidden.T, cotangent, preferred_element_type=jnp.float32)
    grad_gate_vals = jnp.concatenate(
        [grad_hidden * up_part * silu_slope(gate_part), grad_hidden * jax.nn.silu(gate_part)], 1
    ).astype(jnp.bfloat16)
    grad_gate_up = jnp.dot(ffn_in.T, grad_gate_vals, preferred_element_type=jnp.float32)
    grad_ffn_in = jnp.dot(grad_gate_vals, gate_up.T, preferred_element_type=jnp.float32)
    grad_from_ffn, grad_ffn_gain = ffn_norm_pull(grad_ffn_in)
    grad_hidden1 = cotangent.astype(jnp.float32) + grad_from_ffn
    grad_attn_proj, grad_ssm_proj_out, grad_attn_beta, grad_ssm_beta = mix_pull(grad_hidden1)
    attn_grad_low = grad_attn_proj.astype(jnp.bfloat16)
    ssm_grad_low = grad_ssm_proj_out.astype(jnp.bfloat16)
    out_grad = (
        jnp.dot(attn_grad_low, out_weight, preferred_element_type=jnp.float32)
        .astype(jnp.bfloat16)
        .reshape(row_count, GROUPS, per_group, HEAD)
    )
    grad_out_weight = jnp.dot(attn_grad_low.T, attended, preferred_element_type=jnp.float32)
    row_dot = jnp.einsum("tgjd,gjtd->gjt", out_grad.astype(jnp.float32), attn_full)

    def visit_backward(grads_in, key_rows, value_rows, key_seg, hop):
        source = (device_index - hop) % devices
        allowed = block_allowed(seg_ids, key_seg, source, row_count, device_index)
        return attend_back(
            grads_in,
            queries,
            key_rows,
            value_rows,
            allowed,
            score_scale,
            log_sum,
            out_grad,
            row_dot,
        )

    grad_start = (
        jnp.zeros((row_count, GROUPS, per_group, HEAD), jnp.float32),
        jnp.zeros((row_count, GROUPS, HEAD), jnp.float32),
        jnp.zeros((row_count, GROUPS, HEAD), jnp.float32),
    )
    first_grads = visit_backward(grad_start, keys, values, seg_ids, 0)

    def backward_step(hop, loop_state):
        key_rows, value_rows, key_seg, grad_q, grad_k, grad_v = loop_state
        key_rows, value_rows, key_seg = from_behind((key_rows, value_rows, key_seg), "seq", 1)
        grad_k, grad_v = (
            passed_along(grad_k.astype(jnp.bfloat16), "seq", 1).astype(grad_k.dtype),
            passed_along(grad_v.astype(jnp.bfloat16), "seq", 1).astype(grad_v.dtype),
        )
        grad_q, grad_k, grad_v = visit_backward(
            (grad_q, grad_k, grad_v), key_rows, value_rows, key_seg, hop
        )
        return (key_rows, value_rows, key_seg, grad_q, grad_k, grad_v)

    back_out = lax.fori_loop(
        1, hop_count, backward_step, (keys, values, seg_ids) + tuple(first_grads)
    )
    grad_queries = back_out[3]
    grad_keys, grad_values = (
        passed_along(back_out[4].astype(jnp.bfloat16), "seq", 1 - hop_count).astype(jnp.float32),
        passed_along(back_out[5].astype(jnp.bfloat16), "seq", 1 - hop_count).astype(jnp.float32),
    )
    grad_gated = (
        jnp.dot(ssm_grad_low, ssm_down.T, preferred_element_type=jnp.float32)
        .astype(jnp.bfloat16)
        .astype(jnp.float32)
    )
    grad_ssm_down = jnp.dot(gated.T, ssm_grad_low, preferred_element_type=jnp.float32)
    grad_scanned = grad_gated * jax.nn.silu(z_gate)
    grad_z_gate = grad_gated * scanned * silu_slope(z_gate)
    output_grads = output_pull(grad_scanned)
    later_grad = carried_in_2(
        (decay_all, output_grads[7]), "seq", chain_backward, carry_identity, True
    )[1]
    grad_decay_all = jnp.sum(later_grad * held_in, axis=(1, 2))
    state_grads = state_pull((later_grad, grad_decay_all))
    grad_tail = output_grads[2] + state_grads[2]
    tail_back = from_behind(as_sent(grad_tail), "seq", -1).astype(grad_tail.dtype)
    grad_conv_in = output_grads[0] + state_grads[0]
    grad_conv_in = jnp.concatenate(
        [grad_conv_in[: row_count - CONV + 1], grad_conv_in[row_count - CONV + 1 :] + tail_back], 0
    )
    grad_select_in = (output_grads[1] + state_grads[1]).astype(jnp.bfloat16)
    grad_conv = output_grads[3] + state_grads[3]
    grad_step_bias = output_grads[4] + state_grads[4]
    grad_decay = output_grads[5] + state_grads[5]
    grad_skip = output_grads[6]
    proj_grad = jnp.concatenate([grad_conv_in, grad_z_gate], 1).astype(jnp.bfloat16)
    qkv_grad = jnp.concatenate(
        [
            grad_queries.reshape(row_count, model_width),
            grad_keys.reshape(row_count, kv_width),
            grad_values.reshape(row_count, kv_width),
        ],
        1,
    ).astype(jnp.bfloat16)
    grad_normed = jnp.dot(qkv_grad, attn_weight[:, :qkv_cols].T, preferred_element_type=jnp.float32)
    grad_normed = grad_normed + jnp.dot(proj_grad, ssm_weight.T, preferred_element_type=jnp.float32)
    grad_normed = grad_normed + jnp.dot(
        grad_select_in, select_weight.T, preferred_element_type=jnp.float32
    )
    grad_attn = jnp.concatenate(
        [jnp.dot(normed.T, qkv_grad, preferred_element_type=jnp.float32), grad_out_weight], 1
    )
    grad_ssm = jnp.dot(normed.T, proj_grad, preferred_element_type=jnp.float32)
    grad_select = jnp.dot(normed.T, grad_select_in, preferred_element_type=jnp.float32)
    mixer_norm_pull = jax.vjp(scaled_norm, layer_in, mixer_gain)[1]
    grad_from_mixer, grad_mixer_gain = mixer_norm_pull(grad_normed)
    grad_layer_in = grad_hidden1 + grad_from_mixer
    grad_tokens = jnp.where(is_meta, 0.0, grad_layer_in).astype(jnp.bfloat16)
    grad_meta = jnp.dot(one_hot.T, jnp.where(is_meta, grad_layer_in, 0.0), precision=highest)
    small = lax.psum(
        (
            grad_meta,
            grad_mixer_gain,
            grad_select,
            grad_conv,
            grad_step_bias,
            grad_decay,
            grad_skip,
            grad_attn_beta,
            grad_ssm_beta,
            grad_ffn_gain,
        ),
        "seq",
    )
    shares = (
        lax.psum_scatter(grad_attn, "seq", scatter_dimension=1, tiled=True),
        lax.psum_scatter(grad_ssm, "seq", scatter_dimension=1, tiled=True),
        lax.psum_scatter(grad_ssm_down, "seq", scatter_dimension=0, tiled=True),
        lax.psum_scatter(grad_gate_up, "seq", scatter_dimension=1, tiled=True),
        lax.psum_scatter(grad_ffn_down, "seq", scatter_dimension=0, tiled=True),
    )
    return (
        layer_out,
        grad_tokens,
        small[0],
        small[1],
        shares[0],
        shares[1],
        small[2],
        small[3],
        small[4],
        small[5],
        small[6],
        shares[2],
        small[7],
        small[8],
        small[9],
        shares[3],
        shares[4],
    )


def solution(mesh):
    placed = (
        P("seq", None),
        P("seq"),
        P("seq"),
        P(),
        P(),
        P(),
        P(),
        P(),
        P(),
        P(),
        P(),
        P(),
        P(),
        P(),
        P(),
        P(),
        P(),
        P(),
        P("seq", None),
    )
    return jax.shard_map(
        per_device,
        mesh=mesh,
        in_specs=placed,
        out_specs=(
            P("seq", None),
            P("seq", None),
            P(),
            P(),
            P(None, "seq"),
            P(None, "seq"),
            P(),
            P(),
            P(),
            P(),
            P(),
            P("seq", None),
            P(),
            P(),
            P(),
            P(None, "seq"),
            P("seq", None),
        ),
        check_vma=False,
    )
```

profile of v0, /device:TPU:0, one launch (start us, length us, event | category | flops | bytes accessed | tf_op | source)
XLA Modules:
  0.0 3152.3 jit_solution(7972990455240345579)
XLA Ops:
  13.7 8.7 fusion.218
  64.4 221.6 %while.80 = (s32[]{:T(128)}, bf16[128,5,64]{0,2,1:T(8,128)(2,1)}, bf16[128,5,64]{0,2,1:T(8,128)(2,1)}, s32[128]{0:T(128)}, f32[5,5,128]{2,1,0:T(8,128)S(1)}, /*i...) while((s32[]{:T(128)}, bf16[128,5,64]{0,2,1:T(8,128)(2,1)}, ...), condition=%wide.region_6.7_spmd, body=%wide.region_3.6_spmd.sunk | while | flops 109009424 | bytes 8386970 | solution.py:278
  294.4 40.7 %all-gather.2 = bf16[32,1,50]{2,1,0:T(2,128)(2,1)S(1)} all-gather(bf16[1,1,50]{2,1,0:T(2,128)(2,1)S(1)} %bitcast.354), channel_id=1, replica_groups=mesh['seq'=32] {'seq'}, dimensions={0}, use_global_device_ids=true | all-gather | bytes 3300 | tf_op jit(solution)/shard_map/all_gather | solution.py:35
  335.8 84.1 %while.82 = (s32[]{:T(128)}, f32[50,64,16]{1,2,0:T(8,128)}, s32[]{:T(128)}, bf16[32,50]{1,0:T(8,128)(2,1)}, bf16[32,50,64,16]{2,3,1,0:T(8,128)(2,1)}, /*index=5*/s32[]{:T(128)}, s32[]{:T(128)}) while((s32[]{:T(128)}, f32[50,64,16]{1,2,0:T(8,128)}, s32[]{:T(128)}, bf16[32,50]{1,0:T(8,128)(2,1)}, ...), condition=%wide.region_9.11_spmd.clone, body=%wide.region_8.10_spmd.clone.sunk | while | flops 256054 | bytes 512613 | solution.py:51
  443.1 17.1 fusion.207
  460.2 12.8 multiply_convert_fusion.1
  473.0 18.1 multiply_reduce_fusion.10
  518.6 313.1 %while.81 = (s32[]{:T(128)}, bf16[128,5,64]{0,2,1:T(8,128)(2,1)}, bf16[128,5,64]{0,2,1:T(8,128)(2,1)}, s32[128]{0:T(128)S(1)}, f32[128,5,5,64]{0,3,2,1:T(8,128)S...) while((s32[]{:T(128)}, bf16[128,5,64]{0,2,1:T(8,128)(2,1)}, ...), condition=%wide.region_15.17_spmd, body=%wide.region_14.16_spmd.sunk | while | flops 266985728 | bytes 14696534 | solution.py:390
  855.6 9.9 pad_maximum_fusion
  865.5 58.7 %while.83 = (s32[]{:T(128)}, f32[50,64,16]{1,2,0:T(8,128)S(1)}, s32[]{:T(128)}, bf16[32,50,64,16]{2,3,1,0:T(8,128)(2,1)}, bf16[32,50]{1,0:T(8,128)(2,1)}, /*index=5*/s32[]{:T(128)}, s32[]{:T(128)}, s32[]{:T(128)}, s32[]{:T(128)}) while((s32[]{:T(128)}, f32[50,64,16]{1,2,0:T(8,128)S(1)}, s32[]{:T(128)}, ...), condition=%wide.region_18.20_spmd.clone, body=%wide.region_17.19_spmd.clone.sunk | while | flops 256058 | bytes 512675 | solution.py:51
  960.5 9.8 fusion.133
  979.4 18.0 fusion.132
  999.1 28.4 fusion.65
  1028.8 11.3 fusion.223
  1040.1 317.4 %fusion = f32[112,1600]{1,0:T(8,128)S(1)} fusion(f32[3200,1600]{1,0:T(8,128)} %fusion.223), kind=kCustom, calls=%all-reduce-scatter | all-reduce-scatter fusion | flops 5734401 | bytes 21196800
  1358.2 9.2 collective-permute-start.15
  1367.3 10.6 collective-permute-start.14
  1382.9 14.5 fusion.224
  1397.4 571.8 %fusion.1 = f32[176,1600]{1,0:T(8,128)} fusion(f32[5504,1600]{1,0:T(8,128)} %fusion.224), kind=kCustom, calls=%all-reduce-scatter.1 | all-reduce-scatter fusion | flops 9011201 | bytes 36352000
  1971.3 9.8 collective-permute-start.17
  1981.1 9.8 fusion.59
  1991.0 14.8 concatenate.34
  2020.7 302.4 %reduce-scatter.14.cloned.1.call-done = f32[1600,200]{0,1:T(8,128)} async-done(((f32[1600,6400]{0,1:T(8,128)}), f32[1600,200]{0,1:T(8,128)}) %reduce-scatter.14.cloned.1.call-update) | async-done | bytes 1280016
  2323.1 815.6 %reduce-scatter.16.cloned.1.call-done = f32[1600,344]{0,1:T(8,128)} async-done(((f32[1600,11008]{0,1:T(8,128)}), f32[1600,344]{0,1:T(8,128)}) %reduce-scatter.16.cloned.1.call-update) | async-done | bytes 2201616
  (1247 shorter events, 878.0 us)
Async XLA Ops:
  7.2 328.6 %all-gather.6.cloned.1.call-start = ((), (), s32[]{:S(2)}) async-start(), calls=%async_computation.2 | async-start | bytes 6758400 | tf_op jit(solution)/shard_map/all_gather | solution.py:35
  8.0 42.6 %collective-permute-start.8 = (s32[3]{0:T(128)S(1)}, s32[3]{0:T(128)S(1)}, u32[]{:S(2)}, u32[]{:S(2)}) collective-permute-start(s32[3]{0:T(128)S(1)} %slice.114), channel_id=1, source_target_pairs={{0,1},{1,2},{2,3},{3,4},{4,5},{5,6},{6,7},{7,8},{8,9},{9,10},{10,1... | collective-permute-start | bytes 44 | tf_op jit(solution)/shard_map/ppermute | solution.py:29
  24.9 29.8 collective-permute-start.9
  64.2 801.3 %all-gather.8.cloned.1.call-start = ((), (), s32[]{:S(2)}) async-start(), calls=%async_computation.3 | async-start | bytes 6758400 | tf_op jit(solution)/shard_map/all_gather | solution.py:35
  518.5 1499.1 %all-reduce.35.cloned.1.call-start = ((), (), s32[]{:S(2)}) async-start(), calls=%async_computation.7 | async-start | bytes 51961856 | tf_op jit(solution)/shard_map/psum | solution.py:447
  616.1 15.1 collective-permute-start.5
  618.7 15.3 collective-permute-start.7
  621.0 16.3 collective-permute-start.6
  639.7 18.3 collective-permute-start.5
  642.8 17.9 collective-permute-start.7
  646.1 18.0 collective-permute-start.6
  686.4 19.5 collective-permute-start.5
  690.7 17.9 collective-permute-start.7
  694.0 18.0 collective-permute-start.6
  831.7 21.0 collective-permute-start.11
  838.0 14.8 collective-permute-start.10
  976.0 1044.7 %all-reduce.33.cloned.1.call-start = ((), (), s32[]{:S(2)}) async-start(), calls=%async_computation.6 | async-start | bytes 171008 | tf_op jit(solution)/shard_map/psum | solution.py:447
  979.3 1343.8 %reduce-scatter.14.cloned.1.call-start = ((), (), s32[]{:S(2)}) async-start(), calls=%async_computation.4 | async-start | bytes 43929600
  997.4 2141.2 %reduce-scatter.16.cloned.1.call-start = ((), (), s32[]{:S(2)}) async-start(), calls=%async_computation.5 | async-start | bytes 75558912
  1358.2 632.8 %collective-permute-start.15 = (f32[112,1600]{1,0:T(8,128)S(1)}, f32[112,1600]{1,0:T(8,128)}, u32[]{:S(2)}, u32[]{:S(2)}) collective-permute-start(f32[112,1600]{1,0:T(8,128)S(1)} %fusion), channel_id=1, source_target_pairs={{0,3},{1,4},{2,5},{3,6},{4,7},{5,8},{6,9},{7,10},{8,11},{9,12},{10... | collective-permute-start | bytes 2150408
  1367.3 623.6 %collective-permute-start.14 = (f32[112,1600]{1,0:T(8,128)S(1)}, f32[112,1600]{1,0:T(8,128)}, u32[]{:S(2)}, u32[]{:S(2)}) collective-permute-start(f32[112,1600]{1,0:T(8,128)S(1)} %fusion), channel_id=1, source_target_pairs={{0,2},{1,3},{2,4},{3,5},{4,6},{5,7},{6,8},{7,9},{8,10},{9,11},{10,... | collective-permute-start | bytes 2150408
  1377.9 613.0 %collective-permute-start.13 = (f32[112,1600]{1,0:T(8,128)S(1)}, f32[112,1600]{1,0:T(8,128)}, u32[]{:S(2)}, u32[]{:S(2)}) collective-permute-start(f32[112,1600]{1,0:T(8,128)S(1)} %fusion), channel_id=1, source_target_pairs={{0,1},{1,2},{2,3},{3,4},{4,5},{5,6},{6,7},{7,8},{8,9},{9,10},{10,1... | collective-permute-start | bytes 2150408
  1380.9 610.0 %collective-permute-start.16 = (f32[36,1600]{1,0:T(8,128)}, f32[36,1600]{1,0:T(8,128)}, u32[]{:S(2)}, u32[]{:S(2)}) collective-permute-start(f32[36,1600]{1,0:T(8,128)} %slice.153), channel_id=1, source_target_pairs={{0,4},{1,5},{2,6},{3,7},{4,8},{5,9},{6,10},{7,11},{8,12},{9,13},{1... | collective-permute-start | bytes 691208
  1971.3 36.5 %collective-permute-start.17 = (f32[124,1600]{1,0:T(8,128)}, f32[124,1600]{1,0:T(8,128)}, u32[]{:S(2)}, u32[]{:S(2)}) collective-permute-start(f32[124,1600]{1,0:T(8,128)} %slice.154), channel_id=1, source_target_pairs={{0,1},{1,2},{2,3},{3,4},{4,5},{5,6},{6,7},{7,8},{8,9},{9,10},{10,1... | collective-permute-start | bytes 2380808
  (301 other events, 15625.1 us)
Sparse Core Ops, SparseCore 0:
  64.3 73.0 all-gather.5
  518.6 70.7 all-gather.7
  976.1 598.1 all-reduce.34
  1582.8 178.5 all-reduce.32
  1764.2 558.9 reduce-scatter.13
  2325.9 812.7 reduce-scatter.15
where the time goes:
time: 3180 us; the launch traced here: 3150 us
  waiting for transfers between devices  1120 us (35%)
  blocking collectives  930 us (29%)
  starting transfers between devices  386 us (12%)
  matrix products  349 us (11%)
  other arithmetic  213 us (7%)
  local copies, waits for them, and re-layouts  128 us (4%)
    unnamed x13, waiting for transfers between devices  1120 us
    unnamed x2, blocking collectives  889 us
    ppermute x93, starting transfers between devices, from_behind(): return lax.ppermute(x, axis, pairs)  296 us
    select_n x64, other arithmetic, hop(): return jax.tree.map(lambda a, b: jnp.where(reached, a, b), new, before)  97.1 us
  transfers between devices with their start and end apart: 136, of which 18 were waited for; matrix products, arithmetic and copies ran while one was open for 40% of the time, Pallas kernels for 0%

commit v1 on v0

--- a/solution.py
+++ b/solution.py
@@ -4,6 +4,8 @@
 import jax
 import jax.numpy as jnp
 from jax import lax
+from jax.experimental import pallas as pl
+from jax.experimental.pallas import tpu as pltpu
 from jax.sharding import PartitionSpec as P
 
 HEADS = 25
@@ -15,12 +17,394 @@
 FF = 5504
 META = 128
 SHEAD = 64
-SPAN = 16
-LEAST_DEV = 64
 
 
 eps = 1e-05
 highest = lax.Precision.HIGHEST
+
+
+MESH = pl.DeviceIdType.MESH
+MIB = 2**20
+
+
+def flipped(v, k):
+    bit = 1 << k
+    return jnp.where(lax.rem(v // bit, 2) == 0, v + bit, v - bit)
+
+
+def flips_of(v, bits):
+    out = [v]
+    for k in bits:
+        out = out + [flipped(o, k) for o in out]
+    return out
+
+
+def thirds(rows):
+    most = (rows // 3 + 15) // 16 * 16
+    return [(0, most), (most, most), (2 * most, rows - 2 * most)]
+
+
+def greet(partners):
+    barrier = pltpu.get_barrier_semaphore()
+    for partner in partners:
+        pl.semaphore_signal(barrier, inc=1, device_id=(partner,), device_id_type=MESH)
+    pl.semaphore_wait(barrier, len(partners))
+
+
+def remote(src, dst, send, recv, device):
+    return pltpu.make_async_remote_copy(
+        src_ref=src,
+        dst_ref=dst,
+        send_sem=send,
+        recv_sem=recv,
+        device_id=(device,),
+        device_id_type=MESH,
+    )
+
+
+def gather_kernel(arrays, half, *refs):
+    ins, out = refs[:arrays], refs[arrays]
+    send, recv, core_send, core_recv, local_sem = refs[arrays + 1 :]
+    me = lax.axis_index("seq")
+    place = lax.rem(me, half)
+    bits = half.bit_length() - 1
+    greet([flipped(me, k) for k in range(bits)])
+    parts = thirds(ins[0].shape[0])
+    links = bits - 1
+    orders = [[1 + (c + s) % links for s in range(links)] for c in range(3)]
+    local = [
+        pltpu.make_async_copy(ins[a], out.at[a * half + place], local_sem.at[a])
+        for a in range(arrays)
+    ]
+    for copy in local:
+        copy.start()
+    sent, handed = [], []
+    for step in range(links + 1):
+        arriving = []
+        for c, (first, count) in enumerate(parts):
+            rows = pl.ds(first, count)
+            held = flips_of(place, orders[c][:step])
+            for a in range(arrays):
+                if step < links:
+                    for i, b in enumerate(held):
+                        place_at = out.at[a * half + b, rows]
+                        at = (1 << step) - 1 + i
+                        copy = remote(
+                            ins[a].at[rows] if i == 0 else place_at,
+                            place_at,
+                            send.at[a, c, at],
+                            recv.at[a, c, at],
+                            flipped(me, orders[c][step]),
+                        )
+                        copy.start()
+                        arriving.append(copy)
+                new = held if step == 0 else held[len(held) // 2 :]
+                for i, b in enumerate(new):
+                    place_at = out.at[a * half + b, rows]
+                    at = 0 if step == 0 else (1 << (step - 1)) + i
+                    copy = remote(
+                        ins[a].at[rows] if step == 0 else place_at,
+                        place_at,
+                        core_send.at[a, c, at],
+                        core_recv.at[a, c, at],
+                        flipped(me, 0),
+                    )
+                    copy.start()
+                    handed.append(copy)
+        for copy in arriving:
+            copy.wait_recv()
+        sent += arriving
+    for copy in sent:
+        copy.wait_send()
+    for copy in handed:
+        copy.wait()
+    for copy in local:
+        copy.wait()
+
+
+def gather_half(arrays, half, collective_id):
+    count = len(arrays)
+    shape = arrays[0].shape
+    semaphores = pltpu.SemaphoreType.DMA((count, 3, half // 2))
+    return pl.pallas_call(
+        partial(gather_kernel, count, half),
+        out_shape=jax.ShapeDtypeStruct((count * half,) + shape, arrays[0].dtype),
+        in_specs=[pl.BlockSpec(memory_space=pl.ANY)] * count,
+        out_specs=pl.BlockSpec(memory_space=pl.ANY),
+        scratch_shapes=[semaphores] * 4 + [pltpu.SemaphoreType.DMA((count,))],
+        compiler_params=pltpu.CompilerParams(collective_id=collective_id, has_side_effects=True),
+        name="gather_half",
+    )(*arrays)
+
+
+def sum_kernel(arrays, half, *refs):
+    terms, outs = refs[0], refs[1 : 1 + arrays]
+    mine, core_in, link_in, load_sem, send, recv, core_send, core_recv = refs[1 + arrays :]
+    me = lax.axis_index("seq")
+    place = lax.rem(me, half)
+    bits = half.bit_length() - 1
+    greet([flipped(me, k) for k in range(bits)])
+    parts = thirds(terms.shape[1])
+    links = bits - 1
+    orders = [[1 + (c + s) % links for s in range(links)] for c in range(3)]
+    loads = []
+    pairs = half // 2
+    for a in range(arrays):
+        for i in range(pairs):
+            block = 2 * i + lax.rem(place, 2)
+            copy = pltpu.make_async_copy(
+                terms.at[a * half + block], mine.at[a, i], load_sem.at[a, i]
+            )
+            copy.start()
+            loads.append(copy)
+    handed = {}
+    for wanted in range(2):
+        for c, (first, count) in enumerate(parts):
+            rows = pl.ds(first, count)
+            kept = flips_of(place, orders[c][1:])
+            blocks = kept if wanted else [flipped(b, orders[c][0]) for b in kept]
+            for a in range(arrays):
+                for i, b in enumerate(blocks):
+                    at = wanted * (pairs // 2) + i
+                    copy = remote(
+                        terms.at[a * half + flipped(b, 0), rows],
+                        core_in.at[a, at, rows],
+                        core_send.at[a, c, at],
+                        core_recv.at[a, c, at],
+                        flipped(me, 0),
+                    )
+                    copy.start()
+                    handed[a, c, at] = copy
+    for copy in loads:
+        copy.wait()
+    sent = []
+    arriving = {}
+
+    def add(ref, slot, rows, other):
+        ref[slot, rows] = (
+            ref[slot, rows].astype(jnp.float32) + other[...].astype(jnp.float32)
+        ).astype(ref.dtype)
+
+    for step in range(links):
+        for c, (first, count) in enumerate(parts):
+            rows = pl.ds(first, count)
+            kept = flips_of(place, orders[c][step + 1 :])
+            for a in range(arrays):
+                for i, b in enumerate(kept):
+                    out_block = flipped(b, orders[c][step])
+                    if step == 0:
+                        handed[a, c, i].wait_recv()
+                        add(mine.at[a], out_block // 2, rows, core_in.at[a, i, rows])
+                    at = pairs - (pairs >> step) + i
+                    copy = remote(
+                        mine.at[a, out_block // 2, rows],
+                        link_in.at[a, at, rows],
+                        send.at[a, c, at],
+                        recv.at[a, c, at],
+                        flipped(me, orders[c][step]),
+                    )
+                    copy.start()
+                    arriving[a, c, at] = copy
+                    sent.append(copy)
+        if step == 0:
+            for c, (first, count) in enumerate(parts):
+                rows = pl.ds(first, count)
+                for a in range(arrays):
+                    for i, b in enumerate(flips_of(place, orders[c][1:])):
+                        at = pairs // 2 + i
+                        handed[a, c, at].wait_recv()
+                        add(mine.at[a], b // 2, rows, core_in.at[a, at, rows])
+        for c, (first, count) in enumerate(parts):
+            rows = pl.ds(first, count)
+            kept = flips_of(place, orders[c][step + 1 :])
+            for a in range(arrays):
+                for i, b in enumerate(kept):
+                    at = pairs - (pairs >> step) + i
+                    arriving[a, c, at].wait_recv()
+                    add(mine.at[a], b // 2, rows, link_in.at[a, at, rows])
+    for a in range(arrays):
+        outs[a][...] = mine[a, place // 2]
+    for copy in sent:
+        copy.wait_send()
+    for copy in handed.values():
+        copy.wait_send()
+
+
+def sum_half(terms, arrays, half, collective_id):
+    rows, columns = terms.shape[1:]
+    pairs = half // 2
+    block = (rows, columns)
+    semaphores = pltpu.SemaphoreType.DMA((arrays, 3, pairs))
+    return pl.pallas_call(
+        partial(sum_kernel, arrays, half),
+        out_shape=[jax.ShapeDtypeStruct(block, terms.dtype)] * arrays,
+        in_specs=[pl.BlockSpec(memory_space=pl.ANY)],
+        out_specs=[pl.BlockSpec(memory_space=pltpu.VMEM)] * arrays,
+        scratch_shapes=[
+            pltpu.VMEM((arrays, pairs) + block, terms.dtype),
+            pltpu.VMEM((arrays, pairs) + block, terms.dtype),
+            pltpu.VMEM((arrays, pairs) + block, terms.dtype),
+            pltpu.SemaphoreType.DMA((arrays, pairs)),
+        ]
+        + [semaphores] * 4,
+        compiler_params=pltpu.CompilerParams(
+            collective_id=collective_id, has_side_effects=True, vmem_limit_bytes=60 * MIB
+        ),
+        name="sum_half",
+    )(terms)
+
+
+def masked_block(at, first_ref, device_index, rows):
+    key = lax.broadcasted_iota(jnp.int32, (rows, rows), 0) + at * rows
+    query = lax.broadcasted_iota(jnp.int32, (rows, rows), 1) + device_index * rows
+    seen = ((key >= first_ref[...]) & (key <= query)).astype(jnp.float32)
+    return jnp.concatenate([seen] * (HEADS // GROUPS), 1) > 0.0
+
+
+def side_by_side(ref, g):
+    return jnp.concatenate([ref[g, j] for j in range(HEADS // GROUPS)], 1)
+
+
+def over_shards(steps_ref, body):
+    body(0)
+
+    @pl.loop(1, steps_ref[1] + 1)
+    def _(hop):
+        body(hop)
+
+
+def attend_kernel(half, steps_ref, q_ref, kv_ref, first_ref, out_ref, log_ref, top, total, acc):
+    device_index, newest = steps_ref[0], half + lax.rem(steps_ref[0], half)
+    rows = kv_ref.shape[1]
+    top[...] = jnp.full_like(top, -1e30)
+    total[...] = jnp.zeros_like(total)
+    acc[...] = jnp.zeros_like(acc)
+
+    def body(hop):
+        block = kv_ref[newest - hop]
+        seen = masked_block(device_index - hop, first_ref, device_index, rows)
+        for g in range(GROUPS):
+            keys = block[:, g * HEAD : (g + 1) * HEAD]
+            values = block[:, (GROUPS + g) * HEAD : (GROUPS + g + 1) * HEAD]
+            scores = jnp.dot(keys, side_by_side(q_ref, g), preferred_element_type=jnp.float32)
+            scores = jnp.where(seen, scores, -1e30)
+            now = jnp.maximum(top[g], jnp.max(scores, axis=0, keepdims=True))
+            probs = jnp.exp(scores - now)
+            fade = jnp.exp(top[g] - now)
+            top[g] = now
+            total[g] = total[g] * fade + jnp.sum(probs, axis=0, keepdims=True)
+            acc[g] = acc[g] * fade + lax.dot_general(
+                values,
+                probs.astype(jnp.bfloat16),
+                (((0,), (0,)), ((), ())),
+                preferred_element_type=jnp.float32,
+            )
+
+    over_shards(steps_ref, body)
+    for g in range(GROUPS):
+        done = acc[g] / total[g]
+        for j in range(HEADS // GROUPS):
+            out_ref[g, j] = done[:, j * rows : (j + 1) * rows]
+        log_ref[g] = top[g] + jnp.log(total[g])
+
+
+def attend(steps, queries, kv, first, half):
+    rows = kv.shape[1]
+    per_group = HEADS // GROUPS
+    wide = per_group * rows
+    return pl.pallas_call(
+        partial(attend_kernel, half),
+        out_shape=[
+            jax.ShapeDtypeStruct((GROUPS, per_group, HEAD, rows), jnp.float32),
+            jax.ShapeDtypeStruct((GROUPS, 1, wide), jnp.float32),
+        ],
+        in_specs=[pl.BlockSpec(memory_space=pltpu.SMEM)]
+        + [pl.BlockSpec(memory_space=pltpu.VMEM)] * 3,
+        out_specs=[pl.BlockSpec(memory_space=pltpu.VMEM)] * 2,
+        scratch_shapes=[
+            pltpu.VMEM((GROUPS, 1, wide), jnp.float32),
+            pltpu.VMEM((GROUPS, 1, wide), jnp.float32),
+            pltpu.VMEM((GROUPS, HEAD, wide), jnp.float32),
+        ],
+        compiler_params=pltpu.CompilerParams(vmem_limit_bytes=56 * MIB),
+        name="attend",
+    )(steps, queries, kv, first)
+
+
+def attend_back_kernel(
+    half,
+    steps_ref,
+    q_ref,
+    kv_ref,
+    first_ref,
+    out_ref,
+    log_ref,
+    grad_ref,
+    grad_q_ref,
+    grad_kv_ref,
+    dots,
+    acc,
+):
+    device_index, newest = steps_ref[0], half + lax.rem(steps_ref[0], half)
+    rows = kv_ref.shape[1]
+    contract = lambda a, b, i: lax.dot_general(
+        a, b, (((i,), (i,)), ((), ())), preferred_element_type=jnp.float32
+    )
+    for g in range(GROUPS):
+        product = side_by_side(out_ref, g) * side_by_side(grad_ref, g).astype(jnp.float32)
+        dots[g] = jnp.sum(product, axis=0, keepdims=True)
+    acc[...] = jnp.zeros_like(acc)
+
+    @pl.loop(0, 2 * half)
+    def _(i):
+        grad_kv_ref[i] = jnp.zeros(grad_kv_ref.shape[1:], grad_kv_ref.dtype)
+
+    def body(hop):
+        block = kv_ref[newest - hop]
+        seen = masked_block(device_index - hop, first_ref, device_index, rows)
+        grad_keys, grad_values = [], []
+        for g in range(GROUPS):
+            keys = block[:, g * HEAD : (g + 1) * HEAD]
+            values = block[:, (GROUPS + g) * HEAD : (GROUPS + g + 1) * HEAD]
+            queries, grads = side_by_side(q_ref, g), side_by_side(grad_ref, g)
+            scores = jnp.dot(keys, queries, preferred_element_type=jnp.float32)
+            probs = jnp.where(seen, jnp.exp(scores - log_ref[g]), 0.0)
+            grad_probs = jnp.dot(values, grads, preferred_element_type=jnp.float32)
+            grad_values.append(contract(probs.astype(jnp.bfloat16), grads, 1))
+            grad_scores = (probs * (grad_probs - dots[g])).astype(jnp.bfloat16)
+            grad_keys.append(contract(grad_scores, queries, 1))
+            acc[g] += contract(keys, grad_scores, 0)
+        grad_kv_ref[newest - hop] = jnp.concatenate(grad_keys + grad_values, 1).astype(
+            grad_kv_ref.dtype
+        )
+
+    over_shards(steps_ref, body)
+    for g in range(GROUPS):
+        for j in range(HEADS // GROUPS):
+            grad_q_ref[g, j] = (acc[g, :, j * rows : (j + 1) * rows] * (HEAD**-0.5)).astype(
+                grad_q_ref.dtype
+            )
+
+
+def attend_back(steps, queries, kv, first, out, log_sum, grads, half):
+    rows = kv.shape[1]
+    wide = HEADS // GROUPS * rows
+    return pl.pallas_call(
+        partial(attend_back_kernel, half),
+        out_shape=[
+            jax.ShapeDtypeStruct(queries.shape, jnp.bfloat16),
+            jax.ShapeDtypeStruct(kv.shape, jnp.bfloat16),
+        ],
+        in_specs=[pl.BlockSpec(memory_space=pltpu.SMEM)]
+        + [pl.BlockSpec(memory_space=pltpu.VMEM)] * 6,
+        out_specs=[pl.BlockSpec(memory_space=pltpu.VMEM)] * 2,
+        scratch_shapes=[
+            pltpu.VMEM((GROUPS, 1, wide), jnp.float32),
+            pltpu.VMEM((GROUPS, HEAD, wide), jnp.float32),
+        ],
+        compiler_params=pltpu.CompilerParams(vmem_limit_bytes=60 * MIB),
+        name="attend_back",
+    )(steps, queries, kv, first, out, log_sum, grads)
 
 
 def from_behind(x, axis, by):
@@ -51,13 +435,38 @@
     return lax.fori_loop(0, count, hop, start)
 
 
-def passed_along(x, axis, by):
-    count = lax.axis_size(axis)
-    return lax.ppermute(x, axis, [(i, (i + by) % count) for i in range(count)])
-
-
 def as_sent(x):
     return jax.tree.map(lambda a: a.astype(jnp.bfloat16) if a.dtype == jnp.float32 else a, x)
+
+
+def gathered(x, groups):
+    return lax.all_gather(x, "seq", axis_index_groups=groups, tiled=True)
+
+
+def summed_rows(x, groups):
+    return lax.psum_scatter(x, "seq", scatter_dimension=0, axis_index_groups=groups, tiled=True)
+
+
+def halves_summed(first, second, side, half):
+    send = jnp.where(side == 0, second, first).astype(jnp.bfloat16)
+    keep = jnp.where(side == 0, first, second)
+    return keep + lax.ppermute(
+        send, "seq", [(d, (d + half) % (2 * half)) for d in range(2 * half)]
+    ).astype(jnp.float32)
+
+
+def swapped(arrays, half, groups):
+    widths = [a.shape[1] // (2 * half) for a in arrays]
+    rows = arrays[0].shape[0]
+    packed = jnp.concatenate([a.reshape(rows, 2, half, -1) for a in arrays], 3)
+    packed = jnp.transpose(packed, (2, 0, 1, 3))
+    packed = lax.all_to_all(packed, "seq", 0, 0, axis_index_groups=groups, tiled=True)
+    packed = packed.reshape(half * rows, 2, -1)
+    out, at = [], 0
+    for width in widths:
+        out.append([packed[:, k, at : at + width] for k in range(2)])
+        at += width
+    return out
 
 
 def rms_scale(entries):
@@ -152,58 +561,6 @@
 
 def chain_backward(earlier, later):
     return (later[0] * earlier[0], later[1] + later[0][:, None, None] * earlier[1])
-
-
-def block_allowed(seg_ids, key_seg, source, row_count, device_index):
-    query_pos = device_index * row_count + jnp.arange(row_count, dtype=jnp.int32)
-    key_pos = source * row_count + jnp.arange(row_count, dtype=jnp.int32)
-    return (seg_ids[:, None] == key_seg[None, :]) & (key_pos[None, :] <= query_pos[:, None])
-
-
-def attend_block(carried_in, queries, key_rows, value_rows, allowed, score_scale):
-    run_max, run_sum, run_acc = carried_in
-    scores = (
-        jnp.einsum("tgjd,rgd->gjtr", queries, key_rows, preferred_element_type=jnp.float32)
-        * score_scale
-    )
-    scores = jnp.where(allowed, scores, -1e30)
-    new_max = jnp.maximum(run_max, jnp.max(scores, axis=-1))
-    probs = jnp.where(allowed, jnp.exp(scores - new_max[..., None]), 0.0)
-    fade = jnp.exp(run_max - new_max)
-    run_sum = run_sum * fade + jnp.sum(probs, axis=-1)
-    run_acc = run_acc * fade[..., None] + jnp.einsum(
-        "gjtr,rgd->gjtd", probs.astype(jnp.bfloat16), value_rows, preferred_element_type=jnp.float32
-    )
-    return (new_max, run_sum, run_acc)
-
-
-def attend_back(
-    grads_in, queries, key_rows, value_rows, allowed, score_scale, log_sum, out_grad, row_dot
-):
-    grad_q, grad_k, grad_v = grads_in
-    scores = (
-        jnp.einsum("tgjd,rgd->gjtr", queries, key_rows, preferred_element_type=jnp.float32)
-        * score_scale
-    )
-    probs = jnp.where(allowed, jnp.exp(scores - log_sum[..., None]), 0.0)
-    grad_v = grad_v + jnp.einsum(
-        "gjtr,tgjd->rgd", probs.astype(jnp.bfloat16), out_grad, preferred_element_type=jnp.float32
-    )
-    grad_probs = jnp.einsum(
-        "tgjd,rgd->gjtr", out_grad, value_rows, preferred_element_type=jnp.float32
-    )
-    grad_scores = (probs * (grad_probs - row_dot[..., None])).astype(jnp.bfloat16)
-    grad_q = (
-        grad_q
-        + jnp.einsum("gjtr,rgd->tgjd", grad_scores, key_rows, preferred_element_type=jnp.float32)
-        * score_scale
-    )
-    grad_k = (
-        grad_k
-        + jnp.einsum("gjtr,tgjd->rgd", grad_scores, queries, preferred_element_type=jnp.float32)
-        * score_scale
-    )
-    return (grad_q, grad_k, grad_v)
 
 
 def per_device(
@@ -235,7 +592,9 @@
     score_scale = 1.0 / math.sqrt(HEAD)
     devices = lax.axis_size("seq")
     device_index = lax.axis_index("seq")
-    hop_count = min(devices // 2, max(SPAN, LEAST_DEV * devices // row_count))
+    half = devices // 2
+    side, place = device_index // half, device_index % half
+    groups = [[h * half + q for q in range(half)] for h in range(2)]
     one_hot = (meta_index[:, None] == jnp.arange(META, dtype=jnp.int32)[None, :]).astype(
         jnp.float32
     )
@@ -246,42 +605,22 @@
         tokens.astype(jnp.float32),
     )
     normed = scaled_norm(layer_in, mixer_gain).astype(jnp.bfloat16)
-    proj_qkv = jnp.dot(
-        normed, attn_weight[:, :qkv_cols], preferred_element_type=jnp.float32
-    ).astype(jnp.bfloat16)
-    queries = proj_qkv[:, :model_width].reshape(row_count, GROUPS, per_group, HEAD)
-    keys = proj_qkv[:, model_width : model_width + kv_width].reshape(row_count, GROUPS, HEAD)
-    values = proj_qkv[:, model_width + kv_width :].reshape(row_count, GROUPS, HEAD)
-
-    def visit_forward(carried_in, key_rows, value_rows, key_seg, hop):
-        source = (device_index - hop) % devices
-        allowed = block_allowed(seg_ids, key_seg, source, row_count, device_index)
-        return attend_block(carried_in, queries, key_rows, value_rows, allowed, score_scale)
-
-    start_carry = (
-        jnp.full((GROUPS, per_group, row_count), -1e30, jnp.float32),
-        jnp.zeros((GROUPS, per_group, row_count), jnp.float32),
-        jnp.zeros((GROUPS, per_group, row_count, HEAD), jnp.float32),
-    )
-    first_carry = visit_forward(start_carry, keys, values, seg_ids, 0)
-
-    def forward_step(hop, loop_state):
-        key_rows, value_rows, key_seg, carried_in = loop_state
-        key_rows, value_rows, key_seg = from_behind((key_rows, value_rows, key_seg), "seq", 1)
-        return (
-            key_rows,
-            value_rows,
-            key_seg,
-            visit_forward(carried_in, key_rows, value_rows, key_seg, hop),
-        )
-
-    loop_out = lax.fori_loop(1, hop_count, forward_step, (keys, values, seg_ids, first_carry))
-    run_max, run_sum, run_acc = loop_out[3]
-    log_sum = run_max + jnp.log(run_sum)
-    attn_full = run_acc / run_sum[..., None]
-    attended = (
-        jnp.transpose(attn_full, (2, 0, 1, 3)).reshape(row_count, model_width).astype(jnp.bfloat16)
-    )
+    query_weight = attn_weight[:, :model_width]
+    kv_weight = attn_weight[:, model_width:qkv_cols]
+    flip = [(d, (d + half) % devices) for d in range(devices)]
+    kv = jnp.dot(normed, kv_weight, preferred_element_type=jnp.float32).astype(jnp.bfloat16)
+    kv_all = gather_half([lax.ppermute(kv, "seq", flip), kv], half, 0)
+    queries = lax.dot_general(
+        query_weight, normed, (((0,), (1,)), ((), ())), preferred_element_type=jnp.float32
+    )
+    queries = (queries.astype(jnp.bfloat16) * score_scale).reshape(
+        GROUPS, per_group, HEAD, row_count
+    )
+    seg_all = lax.all_gather(seg_ids, "seq", tiled=True)
+    first = jnp.sum((seg_all[:, None] < seg_ids[None, :]).astype(jnp.int32), axis=0)
+    steps = jnp.stack([device_index, device_index - first[0] // row_count])
+    attn_full, log_sum = attend(steps, queries, kv_all, first[None, :], half)
+    attended = attn_full.reshape(model_width, row_count).astype(jnp.bfloat16).T
     out_weight = attn_weight[:, qkv_cols:]
     attn_proj = jnp.dot(attended, out_weight.T, preferred_element_type=jnp.float32)
     ssm_proj = jnp.dot(normed, ssm_weight, preferred_element_type=jnp.float32)
@@ -322,85 +661,63 @@
     hidden1 = layer_in + mixed_terms
     ffn_in_f, ffn_norm_pull = jax.vjp(scaled_norm, hidden1, ffn_gain)
     ffn_in = ffn_in_f.astype(jnp.bfloat16)
-    gate_vals = jnp.dot(ffn_in, gate_up, preferred_element_type=jnp.float32)
-    gate_part = gate_vals[:, :FF]
-    up_part = gate_vals[:, FF:]
+    ffn_rows = gather_half([ffn_in], half, 2).reshape(half * row_count, model_width)
+    cot_rows = gathered(cotangent, groups)
+    units = FF // half
+    gate_w = lax.dynamic_slice_in_dim(gate_up, place * units, units, 1)
+    up_w = lax.dynamic_slice_in_dim(gate_up, FF + place * units, units, 1)
+    down_w = lax.dynamic_slice_in_dim(ffn_down, place * units, units, 0)
+    gate_part = jnp.dot(ffn_rows, gate_w, preferred_element_type=jnp.float32)
+    up_part = jnp.dot(ffn_rows, up_w, preferred_element_type=jnp.float32)
     hidden = (jax.nn.silu(gate_part) * up_part).astype(jnp.bfloat16)
-    layer_out = (hidden1 + jnp.dot(hidden, ffn_down, preferred_element_type=jnp.float32)).astype(
-        jnp.bfloat16
-    )
+    out_terms = jnp.dot(hidden, down_w, preferred_element_type=jnp.float32).astype(jnp.bfloat16)
+    layer_out = (hidden1 + summed_rows(out_terms, groups).astype(jnp.float32)).astype(jnp.bfloat16)
     grad_hidden = (
-        jnp.dot(cotangent, ffn_down.T, preferred_element_type=jnp.float32)
+        jnp.dot(cot_rows, down_w.T, preferred_element_type=jnp.float32)
         .astype(jnp.bfloat16)
         .astype(jnp.float32)
     )
-    grad_ffn_down = jnp.dot(hidden.T, cotangent, preferred_element_type=jnp.float32)
-    grad_gate_vals = jnp.concatenate(
-        [grad_hidden * up_part * silu_slope(gate_part), grad_hidden * jax.nn.silu(gate_part)], 1
-    ).astype(jnp.bfloat16)
-    grad_gate_up = jnp.dot(ffn_in.T, grad_gate_vals, preferred_element_type=jnp.float32)
-    grad_ffn_in = jnp.dot(grad_gate_vals, gate_up.T, preferred_element_type=jnp.float32)
+    down_terms = jnp.dot(hidden.T, cot_rows, preferred_element_type=jnp.float32)
+    grad_gate = (grad_hidden * up_part * silu_slope(gate_part)).astype(jnp.bfloat16)
+    grad_up = (grad_hidden * jax.nn.silu(gate_part)).astype(jnp.bfloat16)
+    gate_terms = jnp.dot(ffn_rows.T, grad_gate, preferred_element_type=jnp.float32)
+    up_terms = jnp.dot(ffn_rows.T, grad_up, preferred_element_type=jnp.float32)
+    grad_gate_up = halves_summed(gate_terms, up_terms, side, half)
+    own_down = halves_summed(down_terms[: units // 2], down_terms[units // 2 :], side, half)
+    grad_ffn_down = lax.ppermute(
+        own_down.astype(jnp.bfloat16),
+        "seq",
+        [(h * half + q, 2 * q + h) for h in range(2) for q in range(half)],
+    ).astype(jnp.float32)
+    in_terms = jnp.dot(grad_gate, gate_w.T, preferred_element_type=jnp.float32) + jnp.dot(
+        grad_up, up_w.T, preferred_element_type=jnp.float32
+    )
+    in_terms = in_terms.astype(jnp.bfloat16).reshape(half, row_count, model_width)
+    grad_ffn_in = sum_half(in_terms, 1, half, 3)[0].astype(jnp.float32)
     grad_from_ffn, grad_ffn_gain = ffn_norm_pull(grad_ffn_in)
     grad_hidden1 = cotangent.astype(jnp.float32) + grad_from_ffn
     grad_attn_proj, grad_ssm_proj_out, grad_attn_beta, grad_ssm_beta = mix_pull(grad_hidden1)
     attn_grad_low = grad_attn_proj.astype(jnp.bfloat16)
     ssm_grad_low = grad_ssm_proj_out.astype(jnp.bfloat16)
     out_grad = (
-        jnp.dot(attn_grad_low, out_weight, preferred_element_type=jnp.float32)
+        lax.dot_general(
+            out_weight, attn_grad_low, (((0,), (1,)), ((), ())), preferred_element_type=jnp.float32
+        )
         .astype(jnp.bfloat16)
-        .reshape(row_count, GROUPS, per_group, HEAD)
-    )
-    grad_out_weight = jnp.dot(attn_grad_low.T, attended, preferred_element_type=jnp.float32)
-    row_dot = jnp.einsum("tgjd,gjtd->gjt", out_grad.astype(jnp.float32), attn_full)
-
-    def visit_backward(grads_in, key_rows, value_rows, key_seg, hop):
-        source = (device_index - hop) % devices
-        allowed = block_allowed(seg_ids, key_seg, source, row_count, device_index)
-        return attend_back(
-            grads_in,
-            queries,
-            key_rows,
-            value_rows,
-            allowed,
-            score_scale,
-            log_sum,
-            out_grad,
-            row_dot,
-        )
-
-    grad_start = (
-        jnp.zeros((row_count, GROUPS, per_group, HEAD), jnp.float32),
-        jnp.zeros((row_count, GROUPS, HEAD), jnp.float32),
-        jnp.zeros((row_count, GROUPS, HEAD), jnp.float32),
-    )
-    first_grads = visit_backward(grad_start, keys, values, seg_ids, 0)
-
-    def backward_step(hop, loop_state):
-        key_rows, value_rows, key_seg, grad_q, grad_k, grad_v = loop_state
-        key_rows, value_rows, key_seg = from_behind((key_rows, value_rows, key_seg), "seq", 1)
-        grad_k, grad_v = (
-            passed_along(grad_k.astype(jnp.bfloat16), "seq", 1).astype(grad_k.dtype),
-            passed_along(grad_v.astype(jnp.bfloat16), "seq", 1).astype(grad_v.dtype),
-        )
-        grad_q, grad_k, grad_v = visit_backward(
-            (grad_q, grad_k, grad_v), key_rows, value_rows, key_seg, hop
-        )
-        return (key_rows, value_rows, key_seg, grad_q, grad_k, grad_v)
-
-    back_out = lax.fori_loop(
-        1, hop_count, backward_step, (keys, values, seg_ids) + tuple(first_grads)
-    )
-    grad_queries = back_out[3]
-    grad_keys, grad_values = (
-        passed_along(back_out[4].astype(jnp.bfloat16), "seq", 1 - hop_count).astype(jnp.float32),
-        passed_along(back_out[5].astype(jnp.bfloat16), "seq", 1 - hop_count).astype(jnp.float32),
+        .reshape(GROUPS, per_group, HEAD, row_count)
+    )
+    grad_queries, kv_terms = attend_back(
+        steps, queries, kv_all, first[None, :], attn_full, log_sum, out_grad, half
+    )
+    grad_kv_other, grad_kv = sum_half(kv_terms, 2, half, 1)
+    grad_kv = grad_kv.astype(jnp.float32) + lax.ppermute(grad_kv_other, "seq", flip).astype(
+        jnp.float32
     )
     grad_gated = (
         jnp.dot(ssm_grad_low, ssm_down.T, preferred_element_type=jnp.float32)
         .astype(jnp.bfloat16)
         .astype(jnp.float32)
     )
-    grad_ssm_down = jnp.dot(gated.T, ssm_grad_low, preferred_element_type=jnp.float32)
     grad_scanned = grad_gated * jax.nn.silu(z_gate)
     grad_z_gate = grad_gated * scanned * silu_slope(z_gate)
     output_grads = output_pull(grad_scanned)
@@ -422,22 +739,40 @@
     grad_skip = output_grads[6]
     proj_grad = jnp.concatenate([grad_conv_in, grad_z_gate], 1).astype(jnp.bfloat16)
     qkv_grad = jnp.concatenate(
-        [
-            grad_queries.reshape(row_count, model_width),
-            grad_keys.reshape(row_count, kv_width),
-            grad_values.reshape(row_count, kv_width),
-        ],
-        1,
-    ).astype(jnp.bfloat16)
+        [grad_queries.reshape(model_width, row_count).T, grad_kv.astype(jnp.bfloat16)], 1
+    )
     grad_normed = jnp.dot(qkv_grad, attn_weight[:, :qkv_cols].T, preferred_element_type=jnp.float32)
     grad_normed = grad_normed + jnp.dot(proj_grad, ssm_weight.T, preferred_element_type=jnp.float32)
     grad_normed = grad_normed + jnp.dot(
         grad_select_in, select_weight.T, preferred_element_type=jnp.float32
     )
-    grad_attn = jnp.concatenate(
-        [jnp.dot(normed.T, qkv_grad, preferred_element_type=jnp.float32), grad_out_weight], 1
-    )
-    grad_ssm = jnp.dot(normed.T, proj_grad, preferred_element_type=jnp.float32)
+    columns = swapped(
+        [jnp.concatenate([qkv_grad, attended], 1), proj_grad, gated], half, groups
+    )
+    normed_rows = gathered(normed, groups)
+    attn_grad_rows = gathered(attn_grad_low, groups)
+    ssm_grad_rows = gathered(ssm_grad_low, groups)
+    grad_attn, grad_ssm = [], []
+    for k in range(2):
+        block = columns[0][k]
+        width = block.shape[1]
+        column = (k * half + place) * width + jnp.arange(width, dtype=jnp.int32)
+        grad_attn.append(
+            jnp.where(
+                (column < qkv_cols)[None, :],
+                jnp.dot(normed_rows.T, block, preferred_element_type=jnp.float32),
+                jnp.dot(attn_grad_rows.T, block, preferred_element_type=jnp.float32),
+            )
+        )
+        grad_ssm.append(jnp.dot(normed_rows.T, columns[1][k], preferred_element_type=jnp.float32))
+    grad_attn = halves_summed(grad_attn[0], grad_attn[1], side, half)
+    grad_ssm = halves_summed(grad_ssm[0], grad_ssm[1], side, half)
+    grad_ssm_down = halves_summed(
+        jnp.dot(columns[2][0].T, ssm_grad_rows, preferred_element_type=jnp.float32),
+        jnp.dot(columns[2][1].T, ssm_grad_rows, preferred_element_type=jnp.float32),
+        side,
+        half,
+    )
     grad_select = jnp.dot(normed.T, grad_select_in, preferred_element_type=jnp.float32)
     mixer_norm_pull = jax.vjp(scaled_norm, layer_in, mixer_gain)[1]
     grad_from_mixer, grad_mixer_gain = mixer_norm_pull(grad_normed)
@@ -459,13 +794,7 @@
         ),
         "seq",
     )
-    shares = (
-        lax.psum_scatter(grad_attn, "seq", scatter_dimension=1, tiled=True),
-        lax.psum_scatter(grad_ssm, "seq", scatter_dimension=1, tiled=True),
-        lax.psum_scatter(grad_ssm_down, "seq", scatter_dimension=0, tiled=True),
-        lax.psum_scatter(grad_gate_up, "seq", scatter_dimension=1, tiled=True),
-        lax.psum_scatter(grad_ffn_down, "seq", scatter_dimension=0, tiled=True),
-    )
+    shares = (grad_attn, grad_ssm, grad_ssm_down, grad_gate_up, grad_ffn_down)
     return (
         layer_out,
         grad_tokens,

time: 3180 us -> 1120 us (0.35)
  blocking collectives: 930 us -> 76.1 us
  waiting for transfers between devices: 1120 us -> 312 us
  starting transfers between devices: 386 us -> 37.6 us
  Pallas kernels: 0 us -> 226 us
  matrix products: 349 us -> 207 us
  other arithmetic: 213 us -> 150 us
  local copies, waits for them, and re-layouts: 128 us -> 81.5 us
    unnamed x13 -> x9, waiting for transfers between devices: 1120 us -> 1.17 us
    unnamed x2 -> x0, blocking collectives: 889 us -> none
    ppermute x93 -> x3, starting transfers between devices: 296 us -> 8.15 us  [from_behind(): return lax.ppermute(x, axis, pairs)]
    pallas_call x0 -> x6, Pallas kernels: none -> 226 us  [the longest x2 119 us: sum_half(): pl.pallas_call(partial(sum_kernel, arrays, half), out_shape=[jax.ShapeDty...]
    psum x2, waiting for transfers between devices: 0.01 us -> 199 us  [per_device(): lax.psum((grad_meta, grad_mixer_gain, grad_select, grad_conv, grad_step_b...]
    dot_general x123 -> x20, matrix products: 262 us -> 110 us  [the longest x1 10.4 us: per_device(): jnp.dot(grad_gate, gate_w.T, preferred_element_type=jnp.float32)]
    ppermute x32 -> x8, waiting for transfers between devices: 1.12 us -> 92.7 us  [the longest x5 92.7 us: halves_summed(): lax.ppermute(send, 'seq', [(d, (d + half) % (2 * half)) for d in range(2...]
    while x195 -> x0, local copies, waits for them, and re-layouts: 55.5 us -> none
  transfers between devices with their start and end apart: 136 -> 21, of which waited for: 18 -> 9; matrix products, arithmetic and copies ran while one was open for 40% -> 33% of each run, Pallas kernels for 0% -> 20%
where the time goes in v1:
time: 1120 us; the launch traced here: 1110 us
  waiting for transfers between devices  312 us (28%)
  Pallas kernels  226 us (20%)
  matrix products  207 us (18%)
  other arithmetic  150 us (13%)
  local copies, waits for them, and re-layouts  81.5 us (7%)
  blocking collectives  76.1 us (7%)
  starting transfers between devices  37.6 us (3%)
  between operations  17.5 us (2%)
    psum x2, waiting for transfers between devices, per_device(): lax.psum((grad_meta, grad_mixer_gain, grad_select, grad_conv, grad_step_b...  199 us
    pallas_call x2, Pallas kernels, sum_half(): pl.pallas_call(partial(sum_kernel, arrays, half), out_shape=[jax.ShapeDty...  119 us
    pallas_call x2, Pallas kernels, gather_half(): pl.pallas_call(partial(gather_kernel, count, half), out_shape=jax.ShapeDt...  94.3 us
    ppermute x5, waiting for transfers between devices, halves_summed(): lax.ppermute(send, 'seq', [(d, (d + half) % (2 * half)) for d in range(2...  92.7 us
    select_n x64, other arithmetic, hop(): return jax.tree.map(lambda a, b: jnp.where(reached, a, b), new, before)  70.4 us
    all_gather x1, blocking collectives, per_device(): seg_all = lax.all_gather(seg_ids, 'seq', tiled=True)  39.4 us
    all_gather x1, blocking collectives, carried_in_2(): lax.all_gather(part.astype(kind), axis)  36.8 us
    dot_general x3, matrix products, ssm_output(): jnp.einsum('htr,rhp->thp', weights, scaled_x, precision=highest)  23 us
  transfers between devices with their start and end apart: 21, of which 9 were waited for; matrix products, arithmetic and copies ran while one was open for 33% of the time, Pallas kernels for 20%

profile of v1, /device:TPU:0, one launch (start us, length us, event | category | flops | bytes accessed | tf_op | source)
XLA Modules:
  0.0 1110.3 jit_solution(212449848836396762)
XLA Ops:
  13.6 8.7 fusion.189
  47.0 39.4 %all-gather.2 = s32[32,1,128]{2,1,0:T(1,128)S(1)} all-gather(s32[1,1,128]{2,1,0:T(1,128)S(1)} %bitcast.242), channel_id=1, replica_groups=mesh['seq'=32] {'seq'}, dimensions={0}, use_global_device_ids=true | all-gather | bytes 16896 | tf_op jit(solution)/shard_map/all_gather | solution.py:619
  96.1 36.8 %all-gather.3 = bf16[32,1,50]{2,1,0:T(2,128)(2,1)S(1)} all-gather(bf16[1,1,50]{2,1,0:T(2,128)(2,1)S(1)} %bitcast.251), channel_id=1, replica_groups=mesh['seq'=32] {'seq'}, dimensions={0}, use_global_device_ids=true | all-gather | bytes 3300 | tf_op jit(solution)/shard_map/all_gather | solution.py:419
  132.9 44.8 %gather_half.2.kv_ref = bf16[32,128,640]{2,1,0:T(8,128)(2,1)} custom-call(bf16[128,640]{1,0:T(8,128)(2,1)} %collective-permute-done.refs_0_, bf16[128,640]{1,0:T(8,128)(2,1)} %copy-done.44), custom_call_target="tpu_custom_call" | custom-call | tf_op jit(solution)/shard_map/gather_half/pallas_call | solution.py:129
  192.1 36.5 %while.30 = (s32[]{:T(128)}, f32[50,64,16]{1,2,0:T(8,128)S(1)}, s32[]{:T(128)}, bf16[32,50]{1,0:T(8,128)(2,1)S(1)}, bf16[32,50,64,16]{2,3,1,0:T(8,128)(2,1)}, /*index=5*/s32[]{:T(128)}, s32[]{:T(128)}) while((s32[]{:T(128)}, f32[50,64,16]{1,2,0:T(8,128)S(1)}, s32[]{:T(128)}, bf16[32,50]{1,0:T(8,128)(2,1)S(1)}, ...), condition=%wide.region_4.6_spmd.clone, body=%wide.region_3.5_spmd.clone.sunk | while | flops 256054 | bytes 512605 | solution.py:435
  257.7 49.4 %gather_half.3 = bf16[16,128,1600]{2,1,0:T(8,128)(2,1)} custom-call(bf16[128,1600]{1,0:T(8,128)(2,1)} %multiply_convert_fusion.3.refs_0_), custom_call_target="tpu_custom_call" | custom-call | tf_op jit(solution)/shard_map/gather_half/pallas_call | solution.py:129
  337.4 9.6 copy.172
  348.2 10.4 fusion.82
  358.6 9.5 add_convert_fusion
  368.1 9.6 copy.174
  377.7 56.8 %sum_half.2 = bf16[128,1600]{1,0:T(8,128)(2,1)} custom-call(bf16[16,128,1600]{2,1,0:T(8,128)(2,1)} %bitcast.211), custom_call_target="tpu_custom_call" | custom-call | tf_op jit(solution)/shard_map/sum_half/pallas_call | solution.py:238
  436.7 8.4 reduce-scatter.2.cloned.1.call-done
  450.0 9.6 multiply_reduce_fusion.1
  487.1 44.3 %collective-permute-done.9 = bf16[172,1600]{1,0:T(8,128)(2,1)S(1)} collective-permute-done((bf16[172,1600]{1,0:T(8,128)(2,1)S(1)}, bf16[172,1600]{1,0:T(8,128)(2,1)S(1)}, u32[]{:S(2)}, u32[]{:S(2)}) %collective-permute-start.9) | collective-permute-done | bytes 550432 | tf_op jit(solution)/shard_map/ppermute | solution.py:453
  546.4 9.6 collective-permute-done.8
  575.2 62.5 %sum_half.3 = (bf16[128,640]{1,0:T(8,128)(2,1)}, bf16[128,640]{1,0:T(8,128)(2,1)}) custom-call(bf16[32,128,640]{2,1,0:T(8,128)(2,1)} %get-tuple-element.256.refs_0_), custom_call_target="tpu_custom_call" | custom-call | tf_op jit(solution)/shard_map/sum_half/pallas_call | solution.py:238
  645.1 9.3 fusion.33
  660.7 58.4 %while.31 = (s32[]{:T(128)}, f32[50,64,16]{1,2,0:T(8,128)S(1)}, s32[]{:T(128)}, bf16[32,50,64,16]{2,3,1,0:T(8,128)(2,1)}, bf16[32,50]{1,0:T(8,128)(2,1)}, /*index=5*/s32[]{:T(128)}, s32[]{:T(128)}, s32[]{:T(128)}, s32[]{:T(128)}) while((s32[]{:T(128)}, f32[50,64,16]{1,2,0:T(8,128)S(1)}, s32[]{:T(128)}, ...), condition=%wide.region_12.14_spmd.clone, body=%wide.region_11.13_spmd.clone.sunk | while | flops 256058 | bytes 512667 | solution.py:435
  777.4 10.5 fusion.42
  800.9 10.9 all-to-all-done
  853.0 18.2 %collective-permute-done.7 = bf16[100,1600]{1,0:T(8,128)(2,1)} collective-permute-done((bf16[100,1600]{1,0:T(8,128)(2,1)}, bf16[100,1600]{1,0:T(8,128)(2,1)}, u32[]{:S(2)}, u32[]{:S(2)}) %collective-permute-start.7) | collective-permute-done | bytes 320032 | tf_op jit(solution)/shard_map/ppermute | solution.py:453
  873.1 20.6 %collective-permute-done.5 = bf16[1600,120]{0,1:T(8,128)(2,1)S(1)} collective-permute-done((bf16[1600,120]{0,1:T(8,128)(2,1)S(1)}, bf16[1600,120]{0,1:T(8,128)(2,1)S(1)}, u32[]{:S(2)}, u32[]{:S(2)}) %collective-permute-start.5) | collective-permute-done | bytes 384032 | tf_op jit(solution)/shard_map/ppermute | solution.py:453
  897.1 58.9 %all-reduce.26.cloned.1.call-done = (f32[1600]{0:T(1024)}, f32[4,3200]{1,0:T(4,128)}, f32[50]{0:T(128)}, f32[50]{0:T(128)}, f32[50]{0:T(128)}, /*index=5*/f32[1600]{0:T(1024)}, f32[1600]{0:T(1024)}, f32[1600]{0:T(1024)}) async-done(((f32[1600]{0:T(1024)}, f32[4,3200]{1,0:T(4,128)}, f32[50]{0:T(128)}, f32[50]{0:T(128)}, f32[50]{0:T(128)}, /*index=5*/f32[1600]{0:T(1024)}, f32[1600]{0:T(1024)}, ...) | async-done | bytes 77416 | tf_op jit(solution)/shard_map/psum | solution.py:782
  956.1 140.0 %all-reduce.28.cloned.1.call-done = (f32[128,1600]{0,1:T(8,128)}, f32[1600,82]{0,1:T(8,128)}) async-done(((f32[128,1600]{0,1:T(8,128)}, f32[1600,82]{0,1:T(8,128)}), (f32[128,1600]{0,1:T(8,128)}, f32[1600,82]{0,1:T(8,128)})) %all-reduce.28.cloned.1.call-update) | async-done | bytes 1344016 | tf_op jit(solution)/shard_map/psum | solution.py:782
  (577 shorter events, 413.2 us)
Async XLA Ops:
  7.2 184.8 %all-gather.19.cloned.1.call-start = ((), (), s32[]{:S(2)}) async-start(), calls=%async_computation.7 | async-start | bytes 6758400 | tf_op jit(solution)/shard_map/all_gather | solution.py:419
  8.0 22.1 %collective-permute-start.1 = (s32[3]{0:T(128)S(1)}, s32[3]{0:T(128)S(1)}, u32[]{:S(2)}, u32[]{:S(2)}) collective-permute-start(s32[3]{0:T(128)S(1)} %slice.129), channel_id=1, source_target_pairs={{0,1},{1,2},{2,3},{3,4},{4,5},{5,6},{6,7},{7,8},{8,9},{9,10},{10,1... | collective-permute-start | bytes 44 | tf_op jit(solution)/shard_map/ppermute | solution.py:413
  22.3 10.0 collective-permute-start.2
  28.7 432.9 %copy-start.51 = (f32[128,16]{0,1:T(8,128)}, f32[128,16]{0,1:T(8,128)S(1)}, u32[]{:S(2)}) copy-start(f32[128,16]{0,1:T(8,128)S(1)} %get-tuple-element.481) | copy-start | bytes 24580
  41.1 273.8 %all-gather.11.cloned.1.call-start = ((), (), s32[]{:S(2)}) async-start(), calls=%async_computation.3 | async-start | bytes 6963200 | tf_op jit(solution)/shard_map/all_gather | solution.py:443
  43.8 89.1 %collective-permute-start = (bf16[128,640]{1,0:T(8,128)(2,1)S(1)}, bf16[128,640]{1,0:T(8,128)(2,1)}, u32[]{:S(2)}, u32[]{:S(2)}) collective-permute-start(bf16[128,640]{1,0:T(8,128)(2,1)S(1)} %fusion.74.refs_1_), channel_id=1, source_target_pairs={{0,16},{1,17},{2,18},{3,19},{4,20},{5,21},{6,22},{7,23},{8,24},{9,... | collective-permute-start | bytes 491528 | tf_op jit(solution)/shard_map/ppermute | solution.py:612
  46.5 398.5 %reduce-scatter.2.cloned.1.call-start = ((), (), s32[]{:S(2)}) async-start(), calls=%async_computation.2 | async-start | bytes 7241728 | tf_op jit(solution)/shard_map/reduce_scatter | solution.py:447
  46.9 598.2 %copy-start.41 = (f32[128,128]{1,0:T(8,128)}, f32[128,128]{1,0:T(8,128)S(1)}, u32[]{:S(2)}) copy-start(f32[128,128]{1,0:T(8,128)S(1)} %fusion.173) | copy-start | bytes 196612
  47.0 598.1 %copy-start.61 = (pred[128,128]{1,0:T(8,128)(4,1)}, pred[128,128]{1,0:T(8,128)(4,1)S(1)}, u32[]{:S(2)}) copy-start(pred[128,128]{1,0:T(8,128)(4,1)S(1)} %fusion.133) | copy-start | bytes 49156
  347.0 313.7 %all-gather.21.cloned.1.call-start = ((), (), s32[]{:S(2)}) async-start(), calls=%async_computation.8 | async-start | bytes 6758400 | tf_op jit(solution)/shard_map/all_gather | solution.py:419
  465.0 355.5 %all-gather.17.cloned.1.call-start = ((), (), s32[]{:S(2)}) async-start(), calls=%async_computation.6 | async-start | bytes 7241728 | tf_op jit(solution)/shard_map/all_gather | solution.py:443
  465.6 362.9 %all-gather.13.cloned.1.call-start = ((), (), s32[]{:S(2)}) async-start(), calls=%async_computation.4 | async-start | bytes 7241728 | tf_op jit(solution)/shard_map/all_gather | solution.py:443
  466.1 379.5 %all-gather.15.cloned.1.call-start = ((), (), s32[]{:S(2)}) async-start(), calls=%async_computation.5 | async-start | bytes 7241728 | tf_op jit(solution)/shard_map/all_gather | solution.py:443
  472.8 58.6 %collective-permute-start.9 = (bf16[172,1600]{1,0:T(8,128)(2,1)S(1)}, bf16[172,1600]{1,0:T(8,128)(2,1)S(1)}, u32[]{:S(2)}, u32[]{:S(2)}) collective-permute-start(bf16[172,1600]{1,0:T(8,128)(2,1)S(1)} %select_convert_fusion.2), channel_id=1, source_target_pairs={{0,16},{1,17},{2,18},{3,19},{4,20},{5,21},{6,22},{7,23},{8,24},{9,... | collective-permute-start | bytes 1651208 | tf_op jit(solution)/shard_map/ppermute | solution.py:453
  486.9 69.2 %collective-permute-start.8 = (bf16[1600,344]{0,1:T(8,128)(2,1)}, bf16[1600,344]{0,1:T(8,128)(2,1)}, u32[]{:S(2)}, u32[]{:S(2)}) collective-permute-start(bf16[1600,344]{0,1:T(8,128)(2,1)} %get-tuple-element.507), channel_id=1, source_target_pairs={{0,16},{1,17},{2,18},{3,19},{4,20},{5,21},{6,22},{7,23},{8,24},{9,... | collective-permute-start | bytes 3302408 | tf_op jit(solution)/shard_map/ppermute | solution.py:453
  532.4 11.8 %collective-permute-start.10 = (bf16[172,1600]{1,0:T(8,128)(2,1)}, bf16[172,1600]{1,0:T(8,128)(2,1)}, u32[]{:S(2)}, u32[]{:S(2)}) collective-permute-start(bf16[172,1600]{1,0:T(8,128)(2,1)} %add_convert_fusion.1), channel_id=1, source_target_pairs={{0,0},{1,2},{2,4},{3,6},{4,8},{5,10},{6,12},{7,14},{8,16},{9,18},{... | collective-permute-start | bytes 1651208 | tf_op jit(solution)/shard_map/ppermute | solution.py:687
  637.7 18.9 %collective-permute-start.3 = (bf16[128,640]{1,0:T(8,128)(2,1)}, bf16[128,640]{1,0:T(8,128)(2,1)}, u32[]{:S(2)}, u32[]{:S(2)}) collective-permute-start(bf16[128,640]{1,0:T(8,128)(2,1)} %get-tuple-element.258), channel_id=1, source_target_pairs={{0,16},{1,17},{2,18},{3,19},{4,20},{5,21},{6,22},{7,23},{8,24},{9,... | collective-permute-start | bytes 491528 | tf_op jit(solution)/shard_map/ppermute | solution.py:713
  741.2 3.1 collective-permute-start.4
  755.0 56.8 %all-to-all-start = ((bf16[16,128,2,420]{1,2,3,0:T(2,128)(2,1)}), bf16[16,128,2,420]{1,2,3,0:T(2,128)(2,1)}, u32[]{:S(2)}, u32[]{:S(2)}) async-start(bf16[16,128,2,420]{1,2,3,0:T(2,128)(2,1)} %copy.195), calls=%async_computation.1 | async-start | bytes 6881280 | tf_op jit(solution)/shard_map/all_to_all | solution.py:463
  761.2 194.8 %all-reduce.26.cloned.1.call-start = ((), (), s32[]{:S(2)}) async-start(), calls=%async_computation.9 | async-start | bytes 171008 | tf_op jit(solution)/shard_map/psum | solution.py:782
  795.8 300.3 %all-reduce.28.cloned.1.call-start = ((), (), s32[]{:S(2)}) async-start(), calls=%async_computation.10 | async-start | bytes 2809856 | tf_op jit(solution)/shard_map/psum | solution.py:782
  828.5 42.6 %collective-permute-start.7 = (bf16[100,1600]{1,0:T(8,128)(2,1)}, bf16[100,1600]{1,0:T(8,128)(2,1)}, u32[]{:S(2)}, u32[]{:S(2)}) collective-permute-start(bf16[100,1600]{1,0:T(8,128)(2,1)} %get-tuple-element.505), channel_id=1, source_target_pairs={{0,16},{1,17},{2,18},{3,19},{4,20},{5,21},{6,22},{7,23},{8,24},{9,... | collective-permute-start | bytes 960008 | tf_op jit(solution)/shard_map/ppermute | solution.py:453
  838.3 56.3 %collective-permute-start.6 = (bf16[1600,200]{0,1:T(8,128)(2,1)}, bf16[1600,200]{0,1:T(8,128)(2,1)}, u32[]{:S(2)}, u32[]{:S(2)}) collective-permute-start(bf16[1600,200]{0,1:T(8,128)(2,1)} %get-tuple-element.503), channel_id=1, source_target_pairs={{0,16},{1,17},{2,18},{3,19},{4,20},{5,21},{6,22},{7,23},{8,24},{9,... | collective-permute-start | bytes 1920008 | tf_op jit(solution)/shard_map/ppermute | solution.py:453
  852.9 40.8 %collective-permute-start.5 = (bf16[1600,120]{0,1:T(8,128)(2,1)S(1)}, bf16[1600,120]{0,1:T(8,128)(2,1)S(1)}, u32[]{:S(2)}, u32[]{:S(2)}) collective-permute-start(bf16[1600,120]{0,1:T(8,128)(2,1)S(1)} %get-tuple-element.501), channel_id=1, source_target_pairs={{0,16},{1,17},{2,18},{3,19},{4,20},{5,21},{6,22},{7,23},{8,24},{9,... | collective-permute-start | bytes 1152008 | tf_op jit(solution)/shard_map/ppermute | solution.py:453
  (123 other events, 2757.1 us)
Sparse Core Ops, SparseCore 0:
  41.2 72.0 all-gather.18
  114.9 63.5 all-gather.10
  347.1 97.8 reduce-scatter.1
  465.1 161.0 all-gather.20
  627.6 52.8 all-gather.16
  682.5 40.8 all-gather.12
  725.0 48.5 all-gather.14
  795.9 160.0 all-reduce.25
  962.9 133.1 all-reduce.27

commit v2 on v1

--- a/solution.py
+++ b/solution.py
@@ -27,6 +27,12 @@
 MIB = 2**20
 
 
+def cost(microseconds):
+    return pl.CostEstimate(
+        flops=0, transcendentals=0, bytes_accessed=int(microseconds * 3_000_000)
+    )
+
+
 def flipped(v, k):
     bit = 1 << k
     return jnp.where(lax.rem(v // bit, 2) == 0, v + bit, v - bit)
@@ -42,6 +48,10 @@
 def thirds(rows):
     most = (rows // 3 + 15) // 16 * 16
     return [(0, most), (most, most), (2 * most, rows - 2 * most)]
+
+
+def parts_of(rows):
+    return [part for part in thirds(rows) if part[1] > 0] if rows >= 48 else [(0, rows)]
 
 
 def greet(partners):
@@ -133,8 +143,193 @@
         out_specs=pl.BlockSpec(memory_space=pl.ANY),
         scratch_shapes=[semaphores] * 4 + [pltpu.SemaphoreType.DMA((count,))],
         compiler_params=pltpu.CompilerParams(collective_id=collective_id, has_side_effects=True),
+        cost_estimate=cost(40),
         name="gather_half",
     )(*arrays)
+
+
+def gather_both_kernel(arrays, half, *refs):
+    ins, outs = refs[:arrays], refs[arrays : 2 * arrays]
+    send, recv, core_send, core_recv, flip_send, flip_recv, local_sem = refs[2 * arrays :]
+    me = lax.axis_index("seq")
+    place = lax.rem(me, half)
+    twin = jnp.where(me < half, me + half, me - half)
+    bits = half.bit_length() - 1
+    greet([flipped(me, k) for k in range(bits)] + [twin])
+    links = bits - 1
+    orders = [[1 + (c + s) % links for s in range(links)] for c in range(3)]
+    parts = [parts_of(ref.shape[0]) for ref in ins]
+    local, sent, handed, twins = [], [], [], []
+    for a in range(arrays):
+        copy = remote(ins[a], outs[a].at[place], flip_send.at[a], flip_recv.at[a], twin)
+        copy.start()
+        twins.append(copy)
+        copy = pltpu.make_async_copy(ins[a], outs[a].at[half + place], local_sem.at[a])
+        copy.start()
+        local.append(copy)
+    for time in range(links + 2):
+        arriving = []
+        for own in (1, 0):
+            step = time - (1 - own)
+            if step < 0 or step > links:
+                continue
+            for a in range(arrays):
+                for c, (first, count) in enumerate(parts[a]):
+                    rows = pl.ds(first, count)
+                    slot = own * arrays + a
+                    held = flips_of(place, orders[c][:step])
+                    if step < links:
+                        for i, b in enumerate(held):
+                            place_at = outs[a].at[own * half + b, rows]
+                            at = (1 << step) - 1 + i
+                            copy = remote(
+                                ins[a].at[rows] if i == 0 and own else place_at,
+                                place_at,
+                                send.at[slot, c, at],
+                                recv.at[slot, c, at],
+                                flipped(me, orders[c][step]),
+                            )
+                            copy.start()
+                            arriving.append(copy)
+                    new = held if step == 0 else held[len(held) // 2 :]
+                    for i, b in enumerate(new):
+                        place_at = outs[a].at[own * half + b, rows]
+                        at = 0 if step == 0 else (1 << (step - 1)) + i
+                        copy = remote(
+                            ins[a].at[rows] if step == 0 and own else place_at,
+                            place_at,
+                            core_send.at[slot, c, at],
+                            core_recv.at[slot, c, at],
+                            flipped(me, 0),
+                        )
+                        copy.start()
+                        handed.append(copy)
+        if time == 0:
+            for copy in twins:
+                copy.wait_recv()
+        for copy in arriving:
+            copy.wait_recv()
+        sent += arriving
+    for copy in sent + twins:
+        copy.wait_send()
+    for copy in handed:
+        copy.wait()
+    for copy in local:
+        copy.wait()
+
+
+def gather_both(arrays, half, collective_id):
+    count = len(arrays)
+    semaphores = pltpu.SemaphoreType.DMA((2 * count, 3, half // 2))
+    single = pltpu.SemaphoreType.DMA((count,))
+    return pl.pallas_call(
+        partial(gather_both_kernel, count, half),
+        out_shape=[jax.ShapeDtypeStruct((2 * half,) + a.shape, a.dtype) for a in arrays],
+        in_specs=[pl.BlockSpec(memory_space=pl.ANY)] * count,
+        out_specs=[pl.BlockSpec(memory_space=pl.ANY)] * count,
+        scratch_shapes=[semaphores] * 4 + [single] * 3,
+        compiler_params=pltpu.CompilerParams(collective_id=collective_id, has_side_effects=True),
+        cost_estimate=cost(50),
+        name="gather_both",
+    )(*arrays)
+
+
+def total_kernel(devices, terms, out, mine, core_in, link_in, send, recv, send_back, recv_back):
+    me = lax.axis_index("seq")
+    bits = devices.bit_length() - 1
+    greet([flipped(me, k) for k in range(bits)])
+    pairs = devices // 2
+    columns = terms.shape[2]
+    third = columns // 3 // 128 * 128
+    parts = [(0, third), (third, third), (2 * third, columns - 2 * third)]
+    turned = min(3, bits - 1)
+    orders = [
+        [1 + (c + s) % turned for s in range(turned)] + list(range(1 + turned, bits))
+        for c in range(3)
+    ]
+    everything = pl.ds(0, columns)
+    copies = []
+    first = []
+    for i in range(pairs):
+        block = 2 * i + 1 - lax.rem(me, 2)
+        copy = remote(
+            terms.at[block], core_in.at[i], send.at[0, i], recv.at[0, i], flipped(me, 0)
+        )
+        copy.start()
+        first.append(copy)
+    copies += first
+    for i in range(pairs):
+        first[i].wait_recv()
+        mine[i] = terms[2 * i + lax.rem(me, 2)] + core_in[i]
+    for step in range(bits - 1):
+        arriving = []
+        for c, (start, count) in enumerate(parts):
+            lanes = pl.ds(start, count)
+            for i, b in enumerate(flips_of(me, orders[c][step + 1 :])):
+                away = flipped(b, orders[c][step])
+                at = pairs - (pairs >> step) + i
+                copy = remote(
+                    mine.at[away // 2, :, lanes],
+                    link_in.at[at, :, lanes],
+                    send.at[1 + c, at],
+                    recv.at[1 + c, at],
+                    flipped(me, orders[c][step]),
+                )
+                copy.start()
+                arriving.append((copy, b, at, lanes))
+        for copy, b, at, lanes in arriving:
+            copy.wait_recv()
+            mine[b // 2, :, lanes] = mine[b // 2, :, lanes] + link_in[at, :, lanes]
+            copies.append(copy)
+    out[me] = mine[me // 2]
+    for step in range(bits - 1):
+        arriving = []
+        for c, (start, count) in enumerate(parts):
+            lanes = pl.ds(start, count)
+            order = orders[c][::-1]
+            for i, b in enumerate(flips_of(me, order[:step])):
+                at = (1 << step) - 1 + i
+                copy = remote(
+                    out.at[b, :, lanes],
+                    out.at[b, :, lanes],
+                    send_back.at[1 + c, at],
+                    recv_back.at[1 + c, at],
+                    flipped(me, order[step]),
+                )
+                copy.start()
+                arriving.append(copy)
+        for copy in arriving:
+            copy.wait_recv()
+        copies += arriving
+    last = []
+    for i, b in enumerate(flips_of(me, range(1, bits))):
+        copy = remote(
+            out.at[b], out.at[b], send_back.at[0, i], recv_back.at[0, i], flipped(me, 0)
+        )
+        copy.start()
+        last.append(copy)
+    for copy in last:
+        copy.wait()
+    for copy in copies:
+        copy.wait_send()
+
+
+def total_of(terms, devices, collective_id):
+    pairs = devices // 2
+    half_shape = (pairs,) + terms.shape[1:]
+    semaphores = pltpu.SemaphoreType.DMA((4, pairs))
+    return pl.pallas_call(
+        partial(total_kernel, devices),
+        out_shape=jax.ShapeDtypeStruct(terms.shape, terms.dtype),
+        in_specs=[pl.BlockSpec(memory_space=pltpu.VMEM)],
+        out_specs=pl.BlockSpec(memory_space=pltpu.VMEM),
+        scratch_shapes=[pltpu.VMEM(half_shape, terms.dtype)] * 3 + [semaphores] * 4,
+        compiler_params=pltpu.CompilerParams(
+            collective_id=collective_id, has_side_effects=True, vmem_limit_bytes=48 * MIB
+        ),
+        cost_estimate=cost(40),
+        name="total_of",
+    )(terms)
 
 
 def sum_kernel(arrays, half, *refs):
@@ -250,8 +445,60 @@
         compiler_params=pltpu.CompilerParams(
             collective_id=collective_id, has_side_effects=True, vmem_limit_bytes=60 * MIB
         ),
+        cost_estimate=cost(50),
         name="sum_half",
     )(terms)
+
+
+def ffn_kernel(x_ref, cot_ref, in_ref, down_ref, out_ref, grad_in_ref, grad_w_ref, grad_d_ref):
+    wide = down_ref.shape[0]
+    x, cot = x_ref[...], cot_ref[...]
+    low = jnp.bfloat16
+
+    def dot(a, b, contract):
+        return lax.dot_general(a, b, (contract, ((), ())), preferred_element_type=jnp.float32)
+
+    vals = dot(x, in_ref[...], ((1,), (0,)))
+    gate, up = vals[:, :wide], vals[:, wide:]
+    sigma = jax.nn.sigmoid(gate)
+    act = gate * sigma
+    hidden = (act * up).astype(low)
+    out_ref[...] = dot(hidden, down_ref[...], ((1,), (0,))).astype(low)
+    grad_hidden = dot(cot, down_ref[...], ((1,), (1,))).astype(low).astype(jnp.float32)
+    slope = sigma * (1.0 + gate * (1.0 - sigma))
+    grads = jnp.concatenate([grad_hidden * up * slope, grad_hidden * act], 1).astype(low)
+    grad_in_ref[...] = dot(grads, in_ref[...], ((1,), (1,))).astype(low)
+
+    @pl.when(pl.program_id(0) == 0)
+    def _():
+        grad_w_ref[...] = jnp.zeros_like(grad_w_ref)
+        grad_d_ref[...] = jnp.zeros_like(grad_d_ref)
+
+    grad_w_ref[...] += dot(grads, x, ((0,), (0,)))
+    grad_d_ref[...] += dot(hidden, cot, ((0,), (0,)))
+
+
+def ffn(x, cot, in_weight, down_weight):
+    rows, model = x.shape
+    block = min(256, rows)
+    wide = down_weight.shape[0]
+    moving = pl.BlockSpec((block, model), lambda i: (i, 0))
+    fixed = lambda shape: pl.BlockSpec(shape, lambda i: (0, 0))
+    return pl.pallas_call(
+        ffn_kernel,
+        grid=(rows // block,),
+        out_shape=[
+            jax.ShapeDtypeStruct(x.shape, jnp.bfloat16),
+            jax.ShapeDtypeStruct(x.shape, jnp.bfloat16),
+            jax.ShapeDtypeStruct((2 * wide, model), jnp.float32),
+            jax.ShapeDtypeStruct((wide, model), jnp.float32),
+        ],
+        in_specs=[moving, moving, fixed(in_weight.shape), fixed(down_weight.shape)],
+        out_specs=[moving, moving, fixed((2 * wide, model)), fixed((wide, model))],
+        compiler_params=pltpu.CompilerParams(vmem_limit_bytes=56 * MIB),
+        cost_estimate=cost(35),
+        name="ffn",
+    )(x, cot, in_weight, down_weight)
 
 
 def masked_block(at, first_ref, device_index, rows):
@@ -327,6 +574,7 @@
             pltpu.VMEM((GROUPS, HEAD, wide), jnp.float32),
         ],
         compiler_params=pltpu.CompilerParams(vmem_limit_bytes=56 * MIB),
+        cost_estimate=cost(15),
         name="attend",
     )(steps, queries, kv, first)
 
@@ -403,6 +651,7 @@
             pltpu.VMEM((GROUPS, HEAD, wide), jnp.float32),
         ],
         compiler_params=pltpu.CompilerParams(vmem_limit_bytes=60 * MIB),
+        cost_estimate=cost(20),
         name="attend_back",
     )(steps, queries, kv, first, out, log_sum, grads)
 
@@ -413,28 +662,6 @@
     return lax.ppermute(x, axis, pairs)
 
 
-def carried_in_2(x, axis, combine, identity, reverse):
-    count, place = (lax.axis_size(axis), lax.axis_index(axis))
-    everything = jax.tree.map(
-        lambda part, kind: lax.all_gather(part.astype(kind), axis),
-        x,
-        jax.tree.map(lambda a: jnp.bfloat16 if a.dtype == jnp.float32 else a.dtype, x),
-    )
-    start = jax.tree.map(
-        lambda part, zero: jnp.broadcast_to(jnp.asarray(zero, part.dtype), part.shape), x, identity
-    )
-
-    def hop(k, before):
-        at = count - 1 - k if reverse else k
-        reached = at > place if reverse else at < place
-        new = combine(
-            before, jax.tree.map(lambda part, own: part[at].astype(own.dtype), everything, x)
-        )
-        return jax.tree.map(lambda a, b: jnp.where(reached, a, b), new, before)
-
-    return lax.fori_loop(0, count, hop, start)
-
-
 def as_sent(x):
     return jax.tree.map(lambda a: a.astype(jnp.bfloat16) if a.dtype == jnp.float32 else a, x)
 
@@ -447,12 +674,15 @@
     return lax.psum_scatter(x, "seq", scatter_dimension=0, axis_index_groups=groups, tiled=True)
 
 
-def halves_summed(first, second, side, half):
+def exchanged(first, second, side, half):
     send = jnp.where(side == 0, second, first).astype(jnp.bfloat16)
     keep = jnp.where(side == 0, first, second)
-    return keep + lax.ppermute(
-        send, "seq", [(d, (d + half) % (2 * half)) for d in range(2 * half)]
-    ).astype(jnp.float32)
+    pairs = [(d, (d + half) % (2 * half)) for d in range(2 * half)]
+    return keep, lax.ppermute(send, "seq", pairs), send
+
+
+def after(x, late):
+    return lax.optimization_barrier((x, late))[0]
 
 
 def swapped(arrays, half, groups):
@@ -486,23 +716,22 @@
     return sigma * (1.0 + entries * (1.0 - sigma))
 
 
-def conv_local(conv_in, tail_x, conv_weight, seg_ids, tail_seg):
+def conv_local(conv_in, tail_x, conv_weight, place_in_item):
     row_count = conv_in.shape[0]
     tap_count = conv_weight.shape[0]
     extended = jnp.concatenate([tail_x, conv_in], 0)
-    ext_seg = jnp.concatenate([tail_seg, seg_ids], 0)
     summed = conv_weight[0] * conv_in
     for tap_lag in range(1, tap_count):
         first_row = tap_count - 1 - tap_lag
         lagged = extended[first_row : first_row + row_count]
-        same_item = (ext_seg[first_row : first_row + row_count] == seg_ids)[:, None]
+        same_item = (place_in_item >= tap_lag)[:, None]
         summed = summed + conv_weight[tap_lag] * jnp.where(same_item, lagged, 0.0)
     return jax.nn.silu(summed)
 
 
-def ssm_parts(conv_in, select, tail_x, conv_weight, step_bias, decay_log, seg_ids, tail_seg):
+def ssm_parts(conv_in, select, tail_x, conv_weight, step_bias, decay_log, place_in_item):
     row_count = conv_in.shape[0]
-    conv_out = conv_local(conv_in, tail_x, conv_weight, seg_ids, tail_seg)
+    conv_out = conv_local(conv_in, tail_x, conv_weight, place_in_item)
     heads_x = conv_out.reshape(row_count, -1, SHEAD)
     b_proj = select[:, :STATE]
     c_proj = select[:, STATE : 2 * STATE]
@@ -525,42 +754,32 @@
     decay_log,
     skip_gain,
     held_in,
-    seg_ids,
-    tail_seg,
+    place_in_item,
+    items,
 ):
     heads_x, b_proj, c_proj, cum_decay, scaled_x, lower_tri = ssm_parts(
-        conv_in, select, tail_x, conv_weight, step_bias, decay_log, seg_ids, tail_seg
-    )
-    seg_prev = tail_seg[-1]
-    same_item = (seg_ids[:, None] == seg_ids[None, :]) & (lower_tri > 0)
+        conv_in, select, tail_x, conv_weight, step_bias, decay_log, place_in_item
+    )
+    same_item = (items[:, None] == items[None, :]) & (lower_tri > 0)
     exponent = jnp.where(same_item[None], cum_decay.T[:, :, None] - cum_decay.T[:, None, :], -1e30)
     weights = jnp.exp(exponent) * jnp.dot(c_proj, b_proj.T, precision=highest)[None]
     local_part = jnp.einsum("htr,rhp->thp", weights, scaled_x, precision=highest)
-    follow = (seg_ids == seg_prev).astype(jnp.float32)
+    follow = (items == 0).astype(jnp.float32)
     carry_weight = jnp.exp(cum_decay) * follow[:, None]
     carried = jnp.einsum("th,hpn,tn->thp", carry_weight, held_in, c_proj, precision=highest)
     outputs = local_part + carried + skip_gain[None, :, None] * heads_x
     return outputs.reshape(conv_in.shape[0], -1)
 
 
-def ssm_state(conv_in, select, tail_x, conv_weight, step_bias, decay_log, seg_ids, tail_seg):
+def ssm_state(conv_in, select, tail_x, conv_weight, step_bias, decay_log, place_in_item, items):
     heads_x, b_proj, c_proj, cum_decay, scaled_x, lower_tri = ssm_parts(
-        conv_in, select, tail_x, conv_weight, step_bias, decay_log, seg_ids, tail_seg
-    )
-    seg_prev = tail_seg[-1]
-    last_same = (seg_ids == seg_ids[-1]).astype(jnp.float32)
+        conv_in, select, tail_x, conv_weight, step_bias, decay_log, place_in_item
+    )
+    last_same = (items == items[-1]).astype(jnp.float32)
     last_weight = jnp.exp(cum_decay[-1][None, :] - cum_decay) * last_same[:, None]
     fresh_state = jnp.einsum("rh,rhp,rn->hpn", last_weight, scaled_x, b_proj, precision=highest)
-    through = (seg_ids[-1] == seg_prev).astype(jnp.float32)
+    through = (items[-1] == 0).astype(jnp.float32)
     return (fresh_state, jnp.exp(cum_decay[-1]) * through)
-
-
-def chain_forward(earlier, later):
-    return (earlier[0] * later[0], later[0][:, None, None] * earlier[1] + later[1])
-
-
-def chain_backward(earlier, later):
-    return (later[0] * earlier[0], later[1] + later[0][:, None, None] * earlier[1])
 
 
 def per_device(
@@ -609,32 +828,25 @@
     kv_weight = attn_weight[:, model_width:qkv_cols]
     flip = [(d, (d + half) % devices) for d in range(devices)]
     kv = jnp.dot(normed, kv_weight, preferred_element_type=jnp.float32).astype(jnp.bfloat16)
-    kv_all = gather_half([lax.ppermute(kv, "seq", flip), kv], half, 0)
     queries = lax.dot_general(
         query_weight, normed, (((0,), (1,)), ((), ())), preferred_element_type=jnp.float32
     )
     queries = (queries.astype(jnp.bfloat16) * score_scale).reshape(
         GROUPS, per_group, HEAD, row_count
     )
-    seg_all = lax.all_gather(seg_ids, "seq", tiled=True)
-    first = jnp.sum((seg_all[:, None] < seg_ids[None, :]).astype(jnp.int32), axis=0)
-    steps = jnp.stack([device_index, device_index - first[0] // row_count])
-    attn_full, log_sum = attend(steps, queries, kv_all, first[None, :], half)
-    attended = attn_full.reshape(model_width, row_count).astype(jnp.bfloat16).T
-    out_weight = attn_weight[:, qkv_cols:]
-    attn_proj = jnp.dot(attended, out_weight.T, preferred_element_type=jnp.float32)
     ssm_proj = jnp.dot(normed, ssm_weight, preferred_element_type=jnp.float32)
     conv_in = ssm_proj[:, :INNER]
     z_gate = ssm_proj[:, INNER:]
     select = jnp.dot(normed, select_weight, preferred_element_type=jnp.float32)
-    tail_x, tail_seg = (
-        from_behind(conv_in[row_count - CONV + 1 :].astype(jnp.bfloat16), "seq", 1).astype(
-            jnp.float32
-        ),
-        from_behind(seg_ids[row_count - CONV + 1 :], "seq", 1),
-    )
+    tail_x = from_behind(conv_in[row_count - CONV + 1 :].astype(jnp.bfloat16), "seq", 1).astype(
+        jnp.float32
+    )
+    row = jnp.arange(row_count, dtype=jnp.int32)
+    starts = jnp.where((meta_index == 0)[None, :] & (row[None, :] <= row[:, None]), 1, 0)
+    items = jnp.sum(starts, axis=1)
+    own_start = jnp.max(starts * (row[None, :] + 1), axis=1) - 1 + device_index * row_count
     (fresh_state, decay_all), state_pull = jax.vjp(
-        partial(ssm_state, seg_ids=seg_ids, tail_seg=tail_seg),
+        partial(ssm_state, place_in_item=meta_index, items=items),
         conv_in,
         select,
         tail_x,
@@ -642,10 +854,50 @@
         step_bias,
         decay_log,
     )
-    carry_identity = (jnp.ones_like(decay_all), jnp.zeros_like(fresh_state))
-    held_in = carried_in_2((decay_all, fresh_state), "seq", chain_forward, carry_identity, False)[1]
+    sheads = INNER // SHEAD
+    padded = (sheads + 15) // 16 * 16
+    state_sent = jnp.pad(
+        fresh_state.reshape(sheads, SHEAD * STATE).astype(jnp.bfloat16),
+        ((0, padded - sheads), (0, 0)),
+    )
+    last_start = jnp.where(items[-1] > 0, own_start[-1], -1).astype(jnp.float32)
+    facts = jnp.concatenate(
+        [decay_all, jnp.full((128 - sheads,), 1.0) * last_start]
+    )
+    facts = jnp.broadcast_to(facts[None, :], (8, 128))
+    kv_all, states, facts = gather_both([kv, state_sent, facts], half, 0)
+    ordered = facts[:, 0].reshape(2, half, 128)
+    ordered = jnp.where(side == 0, ordered[::-1], ordered).reshape(devices, 128)
+    shard = jnp.arange(devices, dtype=jnp.int32)
+    earlier_start = jnp.max(jnp.where(shard < device_index, ordered[:, sheads], -1.0)).astype(
+        jnp.int32
+    )
+    first = jnp.where(items > 0, own_start, earlier_start)
+    steps = jnp.stack([device_index, device_index - first[0] // row_count])
+    attn_full, log_sum = attend(steps, queries, kv_all, first[None, :], half)
+    attended = attn_full.reshape(model_width, row_count).astype(jnp.bfloat16).T
+    out_weight = attn_weight[:, qkv_cols:]
+    attn_proj = jnp.dot(attended, out_weight.T, preferred_element_type=jnp.float32)
+    decays = ordered[:, :sheads]
+    between_before = (shard[None, :] > shard[:, None]) & (shard[None, :] < device_index)
+    weight_before = jnp.where(
+        (shard < device_index)[:, None],
+        jnp.prod(jnp.where(between_before[:, :, None], decays[None], 1.0), axis=1),
+        0.0,
+    )
+    between_after = (shard[None, :] < shard[:, None]) & (shard[None, :] > device_index)
+    weight_after = jnp.where(
+        (shard > device_index)[:, None],
+        jnp.prod(jnp.where(between_after[:, :, None], decays[None], 1.0), axis=1),
+        0.0,
+    )
+    by_slot = weight_before.reshape(2, half, sheads)
+    by_slot = jnp.where(side == 0, by_slot[::-1], by_slot).reshape(devices, sheads)
+    by_slot = jnp.pad(by_slot, ((0, 0), (0, padded - sheads)))
+    held_in = jnp.sum(by_slot[:, :, None] * states.astype(jnp.float32), axis=0)[:sheads]
+    held_in = held_in.reshape(sheads, SHEAD, STATE)
     scanned, output_pull = jax.vjp(
-        partial(ssm_output, seg_ids=seg_ids, tail_seg=tail_seg),
+        partial(ssm_output, place_in_item=meta_index, items=items),
         conv_in,
         select,
         tail_x,
@@ -664,36 +916,32 @@
     ffn_rows = gather_half([ffn_in], half, 2).reshape(half * row_count, model_width)
     cot_rows = gathered(cotangent, groups)
     units = FF // half
-    gate_w = lax.dynamic_slice_in_dim(gate_up, place * units, units, 1)
-    up_w = lax.dynamic_slice_in_dim(gate_up, FF + place * units, units, 1)
-    down_w = lax.dynamic_slice_in_dim(ffn_down, place * units, units, 0)
-    gate_part = jnp.dot(ffn_rows, gate_w, preferred_element_type=jnp.float32)
-    up_part = jnp.dot(ffn_rows, up_w, preferred_element_type=jnp.float32)
-    hidden = (jax.nn.silu(gate_part) * up_part).astype(jnp.bfloat16)
-    out_terms = jnp.dot(hidden, down_w, preferred_element_type=jnp.float32).astype(jnp.bfloat16)
-    layer_out = (hidden1 + summed_rows(out_terms, groups).astype(jnp.float32)).astype(jnp.bfloat16)
-    grad_hidden = (
-        jnp.dot(cot_rows, down_w.T, preferred_element_type=jnp.float32)
-        .astype(jnp.bfloat16)
-        .astype(jnp.float32)
-    )
-    down_terms = jnp.dot(hidden.T, cot_rows, preferred_element_type=jnp.float32)
-    grad_gate = (grad_hidden * up_part * silu_slope(gate_part)).astype(jnp.bfloat16)
-    grad_up = (grad_hidden * jax.nn.silu(gate_part)).astype(jnp.bfloat16)
-    gate_terms = jnp.dot(ffn_rows.T, grad_gate, preferred_element_type=jnp.float32)
-    up_terms = jnp.dot(ffn_rows.T, grad_up, preferred_element_type=jnp.float32)
-    grad_gate_up = halves_summed(gate_terms, up_terms, side, half)
-    own_down = halves_summed(down_terms[: units // 2], down_terms[units // 2 :], side, half)
-    grad_ffn_down = lax.ppermute(
-        own_down.astype(jnp.bfloat16),
-        "seq",
-        [(h * half + q, 2 * q + h) for h in range(2) for q in range(half)],
-    ).astype(jnp.float32)
-    in_terms = jnp.dot(grad_gate, gate_w.T, preferred_element_type=jnp.float32) + jnp.dot(
-        grad_up, up_w.T, preferred_element_type=jnp.float32
-    )
-    in_terms = in_terms.astype(jnp.bfloat16).reshape(half, row_count, model_width)
+    wide = (units + 127) // 128 * 128
+    in_weight = jnp.concatenate(
+        [
+            jnp.pad(
+                lax.dynamic_slice_in_dim(gate_up, first_unit + place * units, units, 1),
+                ((0, 0), (0, wide - units)),
+            )
+            for first_unit in (0, FF)
+        ],
+        1,
+    )
+    down_weight = jnp.pad(
+        lax.dynamic_slice_in_dim(ffn_down, place * units, units, 0), ((0, wide - units), (0, 0))
+    )
+    out_terms, in_terms, in_weight_terms, down_terms = ffn(
+        ffn_rows, cot_rows, in_weight, down_weight
+    )
+    in_terms = in_terms.reshape(half, row_count, model_width)
     grad_ffn_in = sum_half(in_terms, 1, half, 3)[0].astype(jnp.float32)
+    out_sum = summed_rows(out_terms, groups)
+    gate_keep, gate_sent, _ = exchanged(
+        in_weight_terms[:units], in_weight_terms[wide : wide + units], side, half
+    )
+    down_keep, down_sent, _ = exchanged(
+        down_terms[: units // 2], down_terms[units // 2 : units], side, half
+    )
     grad_from_ffn, grad_ffn_gain = ffn_norm_pull(grad_ffn_in)
     grad_hidden1 = cotangent.astype(jnp.float32) + grad_from_ffn
     grad_attn_proj, grad_ssm_proj_out, grad_attn_beta, grad_ssm_beta = mix_pull(grad_hidden1)
@@ -709,9 +957,42 @@
     grad_queries, kv_terms = attend_back(
         steps, queries, kv_all, first[None, :], attn_full, log_sum, out_grad, half
     )
+    down_own = down_keep + after(down_sent, grad_queries).astype(jnp.float32)
+    down_moved = lax.ppermute(
+        down_own.astype(jnp.bfloat16),
+        "seq",
+        [(h * half + q, 2 * q + h) for h in range(2) for q in range(half)],
+    )
     grad_kv_other, grad_kv = sum_half(kv_terms, 2, half, 1)
     grad_kv = grad_kv.astype(jnp.float32) + lax.ppermute(grad_kv_other, "seq", flip).astype(
         jnp.float32
+    )
+    qkv_grad = jnp.concatenate(
+        [grad_queries.reshape(model_width, row_count).T, grad_kv.astype(jnp.bfloat16)], 1
+    )
+    gated_columns = swapped([gated], half, groups)[0]
+    attn_columns = swapped([jnp.concatenate([qkv_grad, attended], 1)], half, groups)[0]
+    normed_rows = gathered(normed, groups)
+    attn_grad_rows = gathered(attn_grad_low, groups)
+    ssm_grad_rows = gathered(ssm_grad_low, groups)
+    attn_terms = []
+    for k in range(2):
+        block = attn_columns[k]
+        width = block.shape[1]
+        column = (k * half + place) * width + jnp.arange(width, dtype=jnp.int32)
+        attn_terms.append(
+            jnp.where(
+                (column < qkv_cols)[:, None],
+                jnp.dot(block.T, normed_rows, preferred_element_type=jnp.float32),
+                jnp.dot(block.T, attn_grad_rows, preferred_element_type=jnp.float32),
+            )
+        )
+    attn_keep, attn_sent, attn_send = exchanged(attn_terms[0], attn_terms[1], side, half)
+    ssm_down_keep, ssm_down_sent, ssm_down_send = exchanged(
+        jnp.dot(gated_columns[0].T, ssm_grad_rows, preferred_element_type=jnp.float32),
+        jnp.dot(gated_columns[1].T, ssm_grad_rows, preferred_element_type=jnp.float32),
+        side,
+        half,
     )
     grad_gated = (
         jnp.dot(ssm_grad_low, ssm_down.T, preferred_element_type=jnp.float32)
@@ -721,9 +1002,11 @@
     grad_scanned = grad_gated * jax.nn.silu(z_gate)
     grad_z_gate = grad_gated * scanned * silu_slope(z_gate)
     output_grads = output_pull(grad_scanned)
-    later_grad = carried_in_2(
-        (decay_all, output_grads[7]), "seq", chain_backward, carry_identity, True
-    )[1]
+    held_grads = lax.all_gather(
+        output_grads[7].reshape(sheads, SHEAD * STATE).astype(jnp.bfloat16), "seq"
+    )
+    later_grad = jnp.sum(weight_after[:, :, None] * held_grads.astype(jnp.float32), axis=0)
+    later_grad = later_grad.reshape(sheads, SHEAD, STATE)
     grad_decay_all = jnp.sum(later_grad * held_in, axis=(1, 2))
     state_grads = state_pull((later_grad, grad_decay_all))
     grad_tail = output_grads[2] + state_grads[2]
@@ -738,63 +1021,70 @@
     grad_decay = output_grads[5] + state_grads[5]
     grad_skip = output_grads[6]
     proj_grad = jnp.concatenate([grad_conv_in, grad_z_gate], 1).astype(jnp.bfloat16)
-    qkv_grad = jnp.concatenate(
-        [grad_queries.reshape(model_width, row_count).T, grad_kv.astype(jnp.bfloat16)], 1
-    )
+    ssm_columns = swapped([proj_grad], half, groups)[0]
     grad_normed = jnp.dot(qkv_grad, attn_weight[:, :qkv_cols].T, preferred_element_type=jnp.float32)
     grad_normed = grad_normed + jnp.dot(proj_grad, ssm_weight.T, preferred_element_type=jnp.float32)
     grad_normed = grad_normed + jnp.dot(
         grad_select_in, select_weight.T, preferred_element_type=jnp.float32
     )
-    columns = swapped(
-        [jnp.concatenate([qkv_grad, attended], 1), proj_grad, gated], half, groups
-    )
-    normed_rows = gathered(normed, groups)
-    attn_grad_rows = gathered(attn_grad_low, groups)
-    ssm_grad_rows = gathered(ssm_grad_low, groups)
-    grad_attn, grad_ssm = [], []
-    for k in range(2):
-        block = columns[0][k]
-        width = block.shape[1]
-        column = (k * half + place) * width + jnp.arange(width, dtype=jnp.int32)
-        grad_attn.append(
-            jnp.where(
-                (column < qkv_cols)[None, :],
-                jnp.dot(normed_rows.T, block, preferred_element_type=jnp.float32),
-                jnp.dot(attn_grad_rows.T, block, preferred_element_type=jnp.float32),
-            )
-        )
-        grad_ssm.append(jnp.dot(normed_rows.T, columns[1][k], preferred_element_type=jnp.float32))
-    grad_attn = halves_summed(grad_attn[0], grad_attn[1], side, half)
-    grad_ssm = halves_summed(grad_ssm[0], grad_ssm[1], side, half)
-    grad_ssm_down = halves_summed(
-        jnp.dot(columns[2][0].T, ssm_grad_rows, preferred_element_type=jnp.float32),
-        jnp.dot(columns[2][1].T, ssm_grad_rows, preferred_element_type=jnp.float32),
+    ssm_keep, ssm_sent, ssm_send = exchanged(
+        jnp.dot(ssm_columns[0].T, normed_rows, preferred_element_type=jnp.float32),
+        jnp.dot(ssm_columns[1].T, normed_rows, preferred_element_type=jnp.float32),
         side,
         half,
     )
-    grad_select = jnp.dot(normed.T, grad_select_in, preferred_element_type=jnp.float32)
+    grad_select = jnp.dot(grad_select_in.T, normed, preferred_element_type=jnp.float32)
     mixer_norm_pull = jax.vjp(scaled_norm, layer_in, mixer_gain)[1]
     grad_from_mixer, grad_mixer_gain = mixer_norm_pull(grad_normed)
     grad_layer_in = grad_hidden1 + grad_from_mixer
     grad_tokens = jnp.where(is_meta, 0.0, grad_layer_in).astype(jnp.bfloat16)
     grad_meta = jnp.dot(one_hot.T, jnp.where(is_meta, grad_layer_in, 0.0), precision=highest)
-    small = lax.psum(
-        (
-            grad_meta,
-            grad_mixer_gain,
-            grad_select,
-            grad_conv,
-            grad_step_bias,
-            grad_decay,
-            grad_skip,
-            grad_attn_beta,
-            grad_ssm_beta,
-            grad_ffn_gain,
+    pieces = [
+        grad_meta,
+        grad_select,
+        grad_conv.reshape(-1, model_width),
+        jnp.stack([grad_mixer_gain, grad_attn_beta, grad_ssm_beta, grad_ffn_gain]),
+        jnp.pad(
+            jnp.concatenate([grad_step_bias, grad_decay, grad_skip])[None, :],
+            ((0, 0), (0, model_width - 3 * sheads)),
         ),
-        "seq",
-    )
-    shares = (grad_attn, grad_ssm, grad_ssm_down, grad_gate_up, grad_ffn_down)
+    ]
+    counts = [piece.shape[0] for piece in pieces]
+    share = -(-sum(counts) // (8 * devices)) * 8
+    packed = jnp.concatenate(
+        pieces + [jnp.zeros((share * devices - sum(counts), model_width), jnp.float32)], 0
+    )
+    packed = after(packed, (attn_send, ssm_down_send, ssm_send))
+    packed = total_of(packed.reshape(devices, share, model_width), devices, 4)
+    packed = packed.reshape(devices * share, model_width)
+    at = [sum(counts[:i]) for i in range(len(counts))]
+    gains = packed[at[3] : at[4]]
+    little = packed[at[4]]
+    small = (
+        packed[: counts[0]],
+        gains[0],
+        packed[at[1] : at[2]].T,
+        packed[at[2] : at[3]].reshape(grad_conv.shape),
+        little[:sheads],
+        little[sheads : 2 * sheads],
+        little[2 * sheads : 3 * sheads],
+        gains[1],
+        gains[2],
+        gains[3],
+    )
+    late = little
+
+    def complete(keep, sent):
+        return keep + after(sent, late).astype(jnp.float32)
+
+    layer_out = (hidden1 + after(out_sum, late).astype(jnp.float32)).astype(jnp.bfloat16)
+    shares = (
+        complete(attn_keep, attn_sent).T,
+        complete(ssm_keep, ssm_sent).T,
+        complete(ssm_down_keep, ssm_down_sent),
+        complete(gate_keep, gate_sent).T,
+        after(down_moved, late).astype(jnp.float32),
+    )
     return (
         layer_out,
         grad_tokens,

time: 1120 us -> 778 us (0.69)
  waiting for transfers between devices: 312 us -> 34 us
  Pallas kernels: 226 us -> 341 us
  blocking collectives: 76.1 us -> 0 us
  other arithmetic: 150 us -> 78.5 us
  matrix products: 207 us -> 145 us
  starting transfers between devices: 37.6 us -> 54.5 us
  local copies, waits for them, and re-layouts: 81.5 us -> 96.8 us
    psum x2 -> x0, waiting for transfers between devices: 199 us -> none  [per_device(): lax.psum((grad_meta, grad_mixer_gain, grad_select, grad_conv, grad_step_b...]
    pallas_call x0 -> x3, Pallas kernels: none -> 195 us  [the longest x1 79.7 us: gather_both(): pl.pallas_call(partial(gather_both_kernel, count, half), out_shape=[jax.S...]
    ppermute x7 -> x6, waiting for transfers between devices: 92.7 us -> 0.02 us  [the longest x5 0.01 us: exchanged(): return (keep, lax.ppermute(send, 'seq', pairs), send)]
    all_gather x2 -> x0, blocking collectives: 76.1 us -> none  [the longest x1 39.4 us: per_device(): seg_all = lax.all_gather(seg_ids, 'seq', tiled=True)]
    select_n x64 -> x5, other arithmetic: 70.4 us -> 0.76 us  [the longest x1 0.67 us: per_device(): jnp.where((shard > device_index)[:, None], jnp.prod(jnp.where(between_aft...]
    dot_general x18 -> x9, matrix products: 95.1 us -> 31.9 us  [the longest x2 7.99 us: per_device(): jnp.dot(block.T, attn_grad_rows, preferred_element_type=jnp.float32)]
    pallas_call x2 -> x1, Pallas kernels: 94.3 us -> 50.3 us  [gather_half(): pl.pallas_call(partial(gather_kernel, count, half), out_shape=jax.ShapeDt...]
    pallas_call x2, Pallas kernels: 119 us -> 82.3 us  [sum_half(): pl.pallas_call(partial(sum_kernel, arrays, half), out_shape=[jax.ShapeDty...]
  transfers between devices with their start and end apart: 21 -> 18, of which waited for: 9 -> 3; matrix products, arithmetic and copies ran while one was open for 33% -> 40% of each run, Pallas kernels for 20% -> 44%
where the time goes in v2:
time: 778 us; the launch traced here: 768 us
  Pallas kernels  341 us (44%)
  matrix products  145 us (19%)
  local copies, waits for them, and re-layouts  96.8 us (12%)
  other arithmetic  78.5 us (10%)
  starting transfers between devices  54.5 us (7%)
  waiting for transfers between devices  34 us (4%)
  between operations  19.2 us (2%)
    pallas_call x2, Pallas kernels, sum_half(): pl.pallas_call(partial(sum_kernel, arrays, half), out_shape=[jax.ShapeDty...  82.3 us
    pallas_call x1, Pallas kernels, gather_both(): pl.pallas_call(partial(gather_both_kernel, count, half), out_shape=[jax.S...  79.7 us
    pallas_call x1, Pallas kernels, total_of(): pl.pallas_call(partial(total_kernel, devices), out_shape=jax.ShapeDtypeSt...  71.9 us
    pallas_call x1, Pallas kernels, gather_half(): pl.pallas_call(partial(gather_kernel, count, half), out_shape=jax.ShapeDt...  50.3 us
    pallas_call x1, Pallas kernels, ffn(): pl.pallas_call(ffn_kernel, grid=(rows // block,), out_shape=[jax.ShapeDty...  43.2 us
    all_to_all x3, waiting for transfers between devices, swapped(): lax.all_to_all(packed, 'seq', 0, 0, axis_index_groups=groups, tiled=True)  32.8 us
    ppermute x5, starting transfers between devices, exchanged(): return (keep, lax.ppermute(send, 'seq', pairs), send)  23.8 us
    dot_general x3, matrix products, ssm_output(): jnp.einsum('htr,rhp->thp', weights, scaled_x, precision=highest)  21.7 us
  transfers between devices with their start and end apart: 18, of which 3 were waited for; matrix products, arithmetic and copies ran while one was open for 40% of the time, Pallas kernels for 44%

profile of v2, /device:TPU:0, one launch (start us, length us, event | category | flops | bytes accessed | tf_op | source)
XLA Modules:
  0.0 768.1 jit_solution(4074062352953291582)
XLA Ops:
  13.7 9.0 %fusion.170 = f32[128,6400]{1,0:T(8,128)S(1)} fusion(bf16[128,1600]{1,0:T(8,128)(2,1)} %multiply_convert_fusion.3, bf16[1600,6400]{1,0:T(8,128)(2,1)} %param.25), kind=kOutput, calls=%fused_computation.329 | convolution fusion | flops 2621440000 | bytes 24166400 | tf_op jit(solution)/shard_map/dot_general | solution.py:837
  69.7 79.7 %gather_both.1 = (bf16[32,128,640]{2,1,0:T(8,128)(2,1)}, bf16[32,64,1024]{2,1,0:T(8,128)(2,1)}, f32[32,8,128]{2,1,0:T(8,128)}) custom-call(bf16[128,640]{1,0:T(8,128)(2,1)} %fusion.71.refs_0_, bf16[64,1024]{1,0:T(8,128)(2,1)} %pad.87.refs_1_, f32[8,128]{1,0:T(8,128)} %broadcast_in_dim.264.refs_2_), custom_call_target="tpu_custom_call" | custom-call | bytes 150000000 | tf_op jit(solution)/shard_map/gather_both/pallas_call | solution.py:225
  173.5 7.7 fusion.46
  186.0 8.0 %multiply_reduce_fusion.20 = (f32[128]{0:T(128)S(1)}, f32[128,1600]{0,1:T(8,128)}) fusion(bf16[128,3200]{1,0:T(8,128)(2,1)S(1)} %multiply_convert_fusion.1, bf16[3200,1600]{0,1:T(8,128)(2,1)} %param.31), kind=kOutput, calls=%fused_computation.154 | convolution fusion | flops 1311129472 | bytes 11878912 | tf_op jit(solution)/shard_map/dot_general | solution.py:911
  199.5 50.3 %gather_half.1 = bf16[16,128,1600]{2,1,0:T(8,128)(2,1)} custom-call(bf16[128,1600]{1,0:T(8,128)(2,1)} %multiply_convert_fusion.2.refs_0_), custom_call_target="tpu_custom_call" | custom-call | bytes 120000000 | tf_op jit(solution)/shard_map/gather_half/pallas_call | solution.py:139
  249.8 43.2 %ffn.1 = (bf16[2048,1600]{1,0:T(8,128)(2,1)}, bf16[2048,1600]{1,0:T(8,128)(2,1)}, f32[768,1600]{1,0:T(8,128)}, f32[384,1600]{1,0:T(8,128)}) custom-call(bf16[2048,1600]{1,0:T(8,128)(2,1)} %bitcast.212, bf16[2048,1600]{1,0:T(8,128)(2,1)} %all-gather.6.cloned.1.call-done.cot_ref, bf16[1600,768]{1,0:T(8,128)(2,1)} %fusion.19.in_ref, bf16[384,1600]{1,0:T(8,128)(2,1)} %pad.91.down_ref), custom_call_target="tpu_custom_call" | custom-call | bytes 105000000 | tf_op jit(solution)/shard_map/ffn/pallas_call | solution.py:487
  293.0 35.3 %sum_half.2 = bf16[128,1600]{1,0:T(8,128)(2,1)} custom-call(bf16[16,128,1600]{2,1,0:T(8,128)(2,1)} %bitcast.218), custom_call_target="tpu_custom_call" | custom-call | bytes 150000000 | tf_op jit(solution)/shard_map/sum_half/pallas_call | solution.py:433
  335.2 9.1 %multiply_reduce_fusion.3 = (f32[3200]{0:T(1024)}, f32[128,3200]{1,0:T(8,128)}, bf16[128,3200]{1,0:T(8,128)(2,1)}) fusion(f32[128,3200]{1,0:T(8,128)S(1)} %copy-done.25, f32[128,6400]{1,0:T(8,128)} %copy-done.9, f32[128,3200]{1,0:T(8,128)} %copy-done.26, bf16[128,1600]{1,0:T(8,128)(2,1)} %get-tuple-element.237, bf16[3200,1600]{0,1:T(8,128)(2,1)} %param.31), kind=kOutput, calls=%fused_computation.69 | convolution fusion | flops 1318908800 | bytes 18035200 | tf_op jit(solution)/shard_map/dot_general | solution.py:998
  366.3 14.1 %all-to-all-done.1 = bf16[16,128,2,100]{1,2,3,0:T(2,128)(2,1)} async-done(((bf16[16,128,2,100]{1,2,3,0:T(2,128)(2,1)}), bf16[16,128,2,100]{1,2,3,0:T(2,128)(2,1)}, u32[]{:S(2)}, u32[]{:S(2)}) %all-to-all-start.1) | async-done | bytes 819232 | tf_op jit(solution)/shard_map/all_to_all | solution.py:693
  387.7 6.6 collective-permute-start.7
  394.4 7.8 %fusion.20 = bf16[128,1600]{0,1:T(8,128)(2,1)} fusion(bf16[128,1600]{1,0:T(8,128)(2,1)S(1)} %copy-done.42, bf16[1600,3840]{1,0:T(8,128)(2,1)} %param.24), kind=kOutput, calls=%fused_computation.31 | convolution fusion | flops 655564800 | bytes 6144000 | tf_op jit(solution)/shard_map/dot_general | solution.py:951
  402.1 7.9 %attend_back.1 = (bf16[5,5,64,128]{3,2,1,0:T(8,128)(2,1)}, bf16[32,128,640]{2,1,0:T(8,128)(2,1)}) custom-call(s32[2]{0:T(128)} %pad_add_fusion.2.steps_ref, bf16[5,5,64,128]{3,2,1,0:T(8,128)(2,1)} %bitcast.231, bf16[32,128,640]{2,1,0:T(8,128)(2,1)} %get-tuple-element.42.kv_ref, s32[1,128]{1,0:T(1,128)} %bitcast.250, ...), custom_call_target="tpu_custom_call" | custom-call | bytes 60000000 | tf_op jit(solution)/shard_map/attend_back/pallas_call | solution.py:640
  410.0 47.0 %sum_half.3 = (bf16[128,640]{1,0:T(8,128)(2,1)}, bf16[128,640]{1,0:T(8,128)(2,1)}) custom-call(bf16[32,128,640]{2,1,0:T(8,128)(2,1)} %get-tuple-element.49.refs_0_), custom_call_target="tpu_custom_call" | custom-call | bytes 150000000 | tf_op jit(solution)/shard_map/sum_half/pallas_call | solution.py:433
  485.1 7.9 %fusion.30 = (f32[50,128]{1,0:T(8,128)}, f32[50,128]{1,0:T(8,128)}, f32[128,128]{1,0:T(8,128)S(1)}) fusion(f32[128,128]{1,0:T(8,128)S(1)} %copy-done.66, f32[50,128]{1,0:T(8,128)S(1)} %bitcast.235, pred[128,128]{1,0:T(8,128)(4,1)S(1)} %copy-done.85, f32[50,64,128]{2,1,0:T(8,128)S(1)} %bitcast.209, f32[128,50,64]{0,2,1:T(8,128)S(1)} %bitcast.215, ...), kind=kOutput, calls=%fused_computation.37 | convolution fusion | flops 636898816 | bytes 3526656 | tf_op jit(solution)/shard_map/transpose(jvp(htr,rhp->thp))/dot_general | solution.py:766
  498.2 6.1 collective-permute-start.8
  504.3 17.3 %all-to-all-done = bf16[16,128,2,120]{1,3,2,0:T(8,128)(2,1)} async-done(((bf16[16,128,2,120]{1,3,2,0:T(8,128)(2,1)}), bf16[16,128,2,120]{1,3,2,0:T(8,128)(2,1)}, u32[]{:S(2)}, u32[]{:S(2)}) %all-to-all-start) | async-done | bytes 983072 | tf_op jit(solution)/shard_map/all_to_all | solution.py:693
  541.1 6.0 fusion.45
  552.9 5.9 multiply_reduce_fusion.11
  590.7 5.9 all-to-all-start.2
  596.6 10.7 %fusion.39 = f32[128,1600]{1,0:T(8,128)S(1)} fusion(bf16[1600,6400]{1,0:T(8,128)(2,1)} %param.25, bf16[128,3200]{1,0:T(8,128)(2,1)S(1)} %copy-done.37, bf16[128,3200]{1,0:T(8,128)(2,1)S(1)} %maximum_convert_fusion), kind=kOutput, calls=%fused_computation.55 | convolution fusion | flops 2624716800 | bytes 22937600 | tf_op jit(solution)/shard_map/dot_general | solution.py:1026
  607.4 5.8 fusion.16
  620.1 6.4 concatenate.45
  635.9 14.2 %collective-permute-start.4 = (bf16[200,1600]{1,0:T(8,128)(2,1)}, bf16[200,1600]{1,0:T(8,128)(2,1)}, u32[]{:S(2)}, u32[]{:S(2)}) collective-permute-start(bf16[200,1600]{1,0:T(8,128)(2,1)} %get-tuple-element.271), channel_id=1, source_target_pairs={{0,16},{1,17},{2,18},{3,19},{4,20},{5,21},{6,22},{7,23},{8,24},{9,... | collective-permute-start | bytes 1920008 | tf_op jit(solution)/shard_map/ppermute | solution.py:681
  669.7 71.9 %total_of.1 = f32[32,8,1600]{2,1,0:T(8,128)S(1)} custom-call(f32[32,8,1600]{2,1,0:T(8,128)S(1)} %bitcast.200), custom_call_target="tpu_custom_call" | custom-call | bytes 120000000 | tf_op jit(solution)/shard_map/total_of/pallas_call | solution.py:321
  (485 shorter events, 265.1 us)
Async XLA Ops:
  7.2 242.6 %all-gather.6.cloned.1.call-start = ((), (), s32[]{:S(2)}) async-start(), calls=%async_computation.4 | async-start | bytes 7241728 | tf_op jit(solution)/shard_map/all_gather | solution.py:670
  9.3 514.6 %all-gather.10.cloned.1.call-start = ((), (), s32[]{:S(2)}) async-start(), calls=%async_computation.7 | async-start | bytes 7241728 | tf_op jit(solution)/shard_map/all_gather | solution.py:670
  23.4 37.2 %collective-permute-start = (bf16[3,3200]{1,0:T(4,128)(2,1)}, bf16[3,3200]{1,0:T(4,128)(2,1)}, u32[]{:S(2)}, u32[]{:S(2)}) collective-permute-start(bf16[3,3200]{1,0:T(4,128)(2,1)} %slice.367), channel_id=1, source_target_pairs={{0,1},{1,2},{2,3},{3,4},{4,5},{5,6},{6,7},{7,8},{8,9},{9,10},{10,1... | collective-permute-start | bytes 57608 | tf_op jit(solution)/shard_map/ppermute | solution.py:662
  26.4 504.9 %all-gather.8.cloned.1.call-start = ((), (), s32[]{:S(2)}) async-start(), calls=%async_computation.6 | async-start | bytes 3784704 | tf_op jit(solution)/shard_map/all_gather | solution.py:1005
  30.8 142.6 %copy-start.65 = (f32[128,128]{1,0:T(8,128)}, f32[128,128]{1,0:T(8,128)S(1)}, u32[]{:S(2)}) copy-start(f32[128,128]{1,0:T(8,128)S(1)} %fusion.158) | copy-start | bytes 196612
  31.6 141.8 %copy-start.48 = (f32[128,50]{0,1:T(8,128)}, f32[128,50]{0,1:T(8,128)S(1)}, u32[]{:S(2)}) copy-start(f32[128,50]{0,1:T(8,128)S(1)} %compare_select_fusion.2) | copy-start | bytes 76804
  31.9 141.5 %copy-start.50 = (f32[128,50]{0,1:T(8,128)}, f32[128,50]{0,1:T(8,128)S(1)}, u32[]{:S(2)}) copy-start(f32[128,50]{0,1:T(8,128)S(1)} %get-tuple-element.257) | copy-start | bytes 76804
  31.9 314.3 %copy-start.60 = (f32[128,50]{0,1:T(8,128)}, f32[128,50]{0,1:T(8,128)S(1)}, u32[]{:S(2)}) copy-start(f32[128,50]{0,1:T(8,128)S(1)} %get-tuple-element.256) | copy-start | bytes 76804
  65.2 86.5 %copy-start.95 = (s32[128]{0:T(128)S(1)}, s32[128]{0:T(128)}, u32[]{:S(2)}) copy-start(s32[128]{0:T(128)} %copy-done.94) | copy-start | bytes 1540
  198.5 131.9 %copy-start.5 = (f32[128,1600]{1,0:T(8,128)}, f32[128,1600]{1,0:T(8,128)S(1)}, u32[]{:S(2)}) copy-start(f32[128,1600]{1,0:T(8,128)S(1)} %get-tuple-element.217) | copy-start | bytes 2457604
  351.7 298.4 %all-gather.14.cloned.1.call-start = ((), (), s32[]{:S(2)}) async-start(), calls=%async_computation.9 | async-start | bytes 7241728 | tf_op jit(solution)/shard_map/all_gather | solution.py:670
  352.3 305.1 %all-gather.12.cloned.1.call-start = ((), (), s32[]{:S(2)}) async-start(), calls=%async_computation.8 | async-start | bytes 7241728 | tf_op jit(solution)/shard_map/all_gather | solution.py:670
  360.0 20.5 %all-to-all-start.1 = ((bf16[16,128,2,100]{1,2,3,0:T(2,128)(2,1)}), bf16[16,128,2,100]{1,2,3,0:T(2,128)(2,1)}, u32[]{:S(2)}, u32[]{:S(2)}) async-start(bf16[16,128,2,100]{1,2,3,0:T(2,128)(2,1)} %copy.329), calls=%async_computation.2 | async-start | bytes 1638400 | tf_op jit(solution)/shard_map/all_to_all | solution.py:693
  364.3 394.4 %reduce-scatter.2.cloned.1.call-start = ((), (), s32[]{:S(2)}) async-start(), calls=%async_computation.5 | async-start | bytes 7241728 | tf_op jit(solution)/shard_map/reduce_scatter | solution.py:674
  387.7 108.3 %collective-permute-start.7 = (bf16[172,1600]{1,0:T(8,128)(2,1)}, bf16[172,1600]{1,0:T(8,128)(2,1)}, u32[]{:S(2)}, u32[]{:S(2)}) collective-permute-start(bf16[172,1600]{1,0:T(8,128)(2,1)} %select_convert_fusion.2), channel_id=1, source_target_pairs={{0,16},{1,17},{2,18},{3,19},{4,20},{5,21},{6,22},{7,23},{8,24},{9,... | collective-permute-start | bytes 1651208 | tf_op jit(solution)/shard_map/ppermute | solution.py:681
  457.1 15.5 %collective-permute-start.1 = (bf16[128,640]{1,0:T(8,128)(2,1)}, bf16[128,640]{1,0:T(8,128)(2,1)S(1)}, u32[]{:S(2)}, u32[]{:S(2)}) collective-permute-start(bf16[128,640]{1,0:T(8,128)(2,1)} %get-tuple-element.51), channel_id=1, source_target_pairs={{0,16},{1,17},{2,18},{3,19},{4,20},{5,21},{6,22},{7,23},{8,24},{9,... | collective-permute-start | bytes 491528 | tf_op jit(solution)/shard_map/ppermute | solution.py:967
  472.5 269.8 %collective-permute-start.6 = (bf16[344,1600]{1,0:T(8,128)(2,1)}, bf16[344,1600]{1,0:T(8,128)(2,1)}, u32[]{:S(2)}, u32[]{:S(2)}) collective-permute-start(bf16[344,1600]{1,0:T(8,128)(2,1)} %select_convert_fusion), channel_id=1, source_target_pairs={{0,16},{1,17},{2,18},{3,19},{4,20},{5,21},{6,22},{7,23},{8,24},{9,... | collective-permute-start | bytes 3302408 | tf_op jit(solution)/shard_map/ppermute | solution.py:681
  477.4 44.2 %all-to-all-start = ((bf16[16,128,2,120]{1,3,2,0:T(8,128)(2,1)}), bf16[16,128,2,120]{1,3,2,0:T(8,128)(2,1)}, u32[]{:S(2)}, u32[]{:S(2)}) async-start(bf16[16,128,2,120]{1,3,2,0:T(8,128)(2,1)} %copy.326), calls=%async_computation.1 | async-start | bytes 1966080 | tf_op jit(solution)/shard_map/all_to_all | solution.py:693
  498.2 251.8 %collective-permute-start.8 = (bf16[172,1600]{1,0:T(8,128)(2,1)}, bf16[172,1600]{1,0:T(8,128)(2,1)}, u32[]{:S(2)}, u32[]{:S(2)}) collective-permute-start(bf16[172,1600]{1,0:T(8,128)(2,1)} %add_convert_fusion), channel_id=1, source_target_pairs={{0,0},{1,2},{2,4},{3,6},{4,8},{5,10},{6,12},{7,14},{8,16},{9,18},{... | collective-permute-start | bytes 1651208 | tf_op jit(solution)/shard_map/ppermute | solution.py:961
  566.3 20.0 %collective-permute-start.2 = (bf16[3,3200]{1,0:T(4,128)(2,1)}, bf16[3,3200]{1,0:T(4,128)(2,1)}, u32[]{:S(2)}, u32[]{:S(2)}) collective-permute-start(bf16[3,3200]{1,0:T(4,128)(2,1)} %fusion.130), channel_id=1, source_target_pairs={{1,0},{2,1},{3,2},{4,3},{5,4},{6,5},{7,6},{8,7},{9,8},{10,9},{11,1... | collective-permute-start | bytes 57608 | tf_op jit(solution)/shard_map/ppermute | solution.py:662
  590.7 37.1 %all-to-all-start.2 = ((bf16[16,128,2,200]{1,3,2,0:T(8,128)(2,1)}), bf16[16,128,2,200]{1,3,2,0:T(8,128)(2,1)S(1)}, u32[]{:S(2)}, u32[]{:S(2)}) async-start(bf16[16,128,2,200]{1,3,2,0:T(8,128)(2,1)} %copy.333), calls=%async_computation.3 | async-start | bytes 3276800 | tf_op jit(solution)/shard_map/all_to_all | solution.py:693
  635.9 106.4 %collective-permute-start.4 = (bf16[200,1600]{1,0:T(8,128)(2,1)}, bf16[200,1600]{1,0:T(8,128)(2,1)}, u32[]{:S(2)}, u32[]{:S(2)}) collective-permute-start(bf16[200,1600]{1,0:T(8,128)(2,1)} %get-tuple-element.271), channel_id=1, source_target_pairs={{0,16},{1,17},{2,18},{3,19},{4,20},{5,21},{6,22},{7,23},{8,24},{9,... | collective-permute-start | bytes 1920008 | tf_op jit(solution)/shard_map/ppermute | solution.py:681
  657.3 97.4 %collective-permute-start.5 = (bf16[100,1600]{1,0:T(8,128)(2,1)}, bf16[100,1600]{1,0:T(8,128)(2,1)}, u32[]{:S(2)}, u32[]{:S(2)}) collective-permute-start(bf16[100,1600]{1,0:T(8,128)(2,1)} %get-tuple-element.269), channel_id=1, source_target_pairs={{0,16},{1,17},{2,18},{3,19},{4,20},{5,21},{6,22},{7,23},{8,24},{9,... | collective-permute-start | bytes 960008 | tf_op jit(solution)/shard_map/ppermute | solution.py:681
  666.1 90.5 %collective-permute-start.3 = (bf16[120,1600]{1,0:T(8,128)(2,1)}, bf16[120,1600]{1,0:T(8,128)(2,1)}, u32[]{:S(2)}, u32[]{:S(2)}) collective-permute-start(bf16[120,1600]{1,0:T(8,128)(2,1)} %get-tuple-element.267), channel_id=1, source_target_pairs={{0,16},{1,17},{2,18},{3,19},{4,20},{5,21},{6,22},{7,23},{8,24},{9,... | collective-permute-start | bytes 1152008 | tf_op jit(solution)/shard_map/ppermute | solution.py:681
  (126 other events, 935.5 us)
Sparse Core Ops, SparseCore 0:
  10.2 45.0 all-gather.5
  57.5 62.4 all-gather.9
  351.8 85.7 all-gather.7
  439.0 73.6 all-gather.13
  514.2 66.5 all-gather.11
  583.0 106.5 reduce-scatter.1

commit v3 on v2

--- a/solution.py
+++ b/solution.py
@@ -333,12 +333,13 @@
 
 
 def sum_kernel(arrays, half, *refs):
-    terms, outs = refs[0], refs[1 : 1 + arrays]
-    mine, core_in, link_in, load_sem, send, recv, core_send, core_recv = refs[1 + arrays :]
+    terms, out = refs[:2]
+    mine, core_in, link_in, load_sem, send, recv, core_send, core_recv, flip_in, flip_sem = refs[2:]
     me = lax.axis_index("seq")
     place = lax.rem(me, half)
     bits = half.bit_length() - 1
-    greet([flipped(me, k) for k in range(bits)])
+    twin = jnp.where(me < half, me + half, me - half)
+    greet([flipped(me, k) for k in range(bits)] + ([twin] if arrays == 2 else []))
     parts = thirds(terms.shape[1])
     links = bits - 1
     orders = [[1 + (c + s) % links for s in range(links)] for c in range(3)]
@@ -417,8 +418,14 @@
                     at = pairs - (pairs >> step) + i
                     arriving[a, c, at].wait_recv()
                     add(mine.at[a], b // 2, rows, link_in.at[a, at, rows])
-    for a in range(arrays):
-        outs[a][...] = mine[a, place // 2]
+    if arrays == 2:
+        flip = remote(mine.at[0, place // 2], flip_in, flip_sem.at[0], flip_sem.at[1], twin)
+        flip.start()
+        flip.wait_recv()
+        out[...] = mine[1, place // 2].astype(jnp.float32) + flip_in[...].astype(jnp.float32)
+        sent.append(flip)
+    else:
+        out[...] = mine[0, place // 2].astype(jnp.float32)
     for copy in sent:
         copy.wait_send()
     for copy in handed.values():
@@ -432,16 +439,20 @@
     semaphores = pltpu.SemaphoreType.DMA((arrays, 3, pairs))
     return pl.pallas_call(
         partial(sum_kernel, arrays, half),
-        out_shape=[jax.ShapeDtypeStruct(block, terms.dtype)] * arrays,
+        out_shape=jax.ShapeDtypeStruct(block, jnp.float32),
         in_specs=[pl.BlockSpec(memory_space=pl.ANY)],
-        out_specs=[pl.BlockSpec(memory_space=pltpu.VMEM)] * arrays,
+        out_specs=pl.BlockSpec(memory_space=pltpu.VMEM),
         scratch_shapes=[
             pltpu.VMEM((arrays, pairs) + block, terms.dtype),
             pltpu.VMEM((arrays, pairs) + block, terms.dtype),
             pltpu.VMEM((arrays, pairs) + block, terms.dtype),
             pltpu.SemaphoreType.DMA((arrays, pairs)),
         ]
-        + [semaphores] * 4,
+        + [semaphores] * 4
+        + [
+            pltpu.VMEM(block if arrays == 2 else (16, 128), terms.dtype),
+            pltpu.SemaphoreType.DMA((2,)),
+        ],
         compiler_params=pltpu.CompilerParams(
             collective_id=collective_id, has_side_effects=True, vmem_limit_bytes=60 * MIB
         ),
@@ -656,6 +667,383 @@
     )(steps, queries, kv, first, out, log_sum, grads)
 
 
+def spread_heads(ref, tile, rows):
+    first_half = lax.broadcasted_iota(jnp.int32, (rows, 128), 1) < SHEAD
+    return jnp.where(
+        first_half, ref[:, 2 * tile : 2 * tile + 1], ref[:, 2 * tile + 1 : 2 * tile + 2]
+    )
+
+
+def conv_tile(proj_ref, tail_ref, taps_ref, place, extended, at, rows):
+    extended[8 : 8 + rows] = proj_ref[:, at]
+    extended[0:8] = tail_ref[:, at]
+    lagged = []
+    summed = jnp.zeros((rows, 128), jnp.float32)
+    for lag in range(taps_ref.shape[0]):
+        moved = extended[8 - lag : 8 - lag + rows]
+        moved = moved if lag == 0 else jnp.where(place >= lag, moved, 0.0)
+        lagged.append(moved)
+        summed = summed + taps_ref[lag : lag + 1, at] * moved
+    return summed, lagged
+
+
+def ssm_state_kernel(
+    proj_ref,
+    tail_ref,
+    taps_ref,
+    place_ref,
+    items_ref,
+    select_ref,
+    bias_ref,
+    rate_ref,
+    state_ref,
+    b_ref,
+    c_ref,
+    raw_ref,
+    step_ref,
+    cum_ref,
+    cum_t_ref,
+    last_ref,
+    carry_ref,
+    all_ref,
+    extended,
+):
+    rows, inner = proj_ref.shape[0], taps_ref.shape[1]
+    heads = step_ref.shape[1]
+    low = jnp.bfloat16
+    b_ref[...] = select_ref[:, :STATE].astype(low)
+    c_ref[...] = select_ref[:, STATE : 2 * STATE].astype(low)
+    raw = select_ref[:, 2 * STATE :] + bias_ref[...]
+    raw_ref[...] = raw
+    step = jnp.maximum(raw, 0.0) + jnp.log1p(jnp.exp(-jnp.abs(raw)))
+    step_ref[...] = step
+    lower = (
+        lax.broadcasted_iota(jnp.int32, (rows, rows), 0)
+        >= lax.broadcasted_iota(jnp.int32, (rows, rows), 1)
+    ).astype(jnp.float32)
+    cum = jnp.dot(
+        lower, -step * rate_ref[...], precision=highest, preferred_element_type=jnp.float32
+    )
+    cum_ref[...] = cum
+    wide = jnp.concatenate([cum, jnp.zeros((rows, 128 - heads), jnp.float32)], 1)
+    cum_t_ref[...] = wide.T[:heads]
+    items = items_ref[...]
+    final = items_ref[rows - 1 : rows, :]
+    total = cum[rows - 1 : rows, :]
+    last_ref[...] = jnp.where(items == final, jnp.exp(total - cum), 0.0)
+    carry_ref[...] = jnp.where(items == 0, jnp.exp(cum), 0.0)
+    all_ref[...] = jnp.where(final == 0, jnp.exp(total), 0.0)
+    place = place_ref[...]
+    b = b_ref[...]
+    for tile in range(inner // 128):
+        at = slice(tile * 128, (tile + 1) * 128)
+        summed, _ = conv_tile(proj_ref, tail_ref, taps_ref, place, extended, at, rows)
+        x = summed * jax.nn.sigmoid(summed)
+        taken = x * spread_heads(step_ref, tile, rows) * spread_heads(last_ref, tile, rows)
+        state_ref[:, at] = lax.dot_general(
+            b, taken.astype(low), (((0,), (0,)), ((), ())), preferred_element_type=jnp.float32
+        ).astype(low)
+
+
+def whole_call(kernel, operands, outs, scratch, microseconds, name):
+    return pl.pallas_call(
+        kernel,
+        out_shape=[jax.ShapeDtypeStruct(dims, kind) for dims, kind in outs],
+        in_specs=[pl.BlockSpec(memory_space=pltpu.VMEM)] * len(operands),
+        out_specs=[pl.BlockSpec(memory_space=pltpu.VMEM)] * len(outs),
+        scratch_shapes=scratch,
+        compiler_params=pltpu.CompilerParams(vmem_limit_bytes=48 * MIB),
+        cost_estimate=cost(microseconds),
+        name=name,
+    )(*operands)
+
+
+def ssm_state(proj, tail, taps, place, items, select, bias, rate):
+    rows, inner, heads = proj.shape[0], taps.shape[1], bias.shape[1]
+    low, full = jnp.bfloat16, jnp.float32
+    by_head = ((rows, heads), full)
+    outs = [((STATE, inner), low), ((rows, STATE), low), ((rows, STATE), low)]
+    outs += [by_head, by_head, by_head, ((heads, rows), full), by_head, by_head]
+    outs += [((1, heads), full)]
+    operands = (proj, tail, taps, place, items, select, bias, rate)
+    scratch = [pltpu.VMEM((rows + 8, 128), full)]
+    return whole_call(ssm_state_kernel, operands, outs, scratch, 8, "ssm_state")
+
+
+def ssm_output_kernel(
+    proj_ref,
+    tail_ref,
+    taps_ref,
+    place_ref,
+    b_ref,
+    c_ref,
+    cum_ref,
+    cum_t_ref,
+    step_ref,
+    skip_ref,
+    carry_ref,
+    same_ref,
+    held_ref,
+    scanned_ref,
+    gated_ref,
+    extended,
+):
+    rows, inner = proj_ref.shape[0], taps_ref.shape[1]
+    low = jnp.bfloat16
+    place, c = place_ref[...], c_ref[...]
+    both = lax.dot_general(
+        c, b_ref[...], (((1,), (1,)), ((), ())), preferred_element_type=jnp.float32
+    )
+    same = same_ref[...] > 0.0
+    first_half = lax.broadcasted_iota(jnp.int32, (rows, 128), 1) < SHEAD
+    for tile in range(inner // 128):
+        at = slice(tile * 128, (tile + 1) * 128)
+        summed, _ = conv_tile(proj_ref, tail_ref, taps_ref, place, extended, at, rows)
+        x = summed * jax.nn.sigmoid(summed)
+        scaled = (x * spread_heads(step_ref, tile, rows)).astype(low)
+        halves = []
+        for k in range(2):
+            head = 2 * tile + k
+            exponent = jnp.where(
+                same, cum_ref[:, head : head + 1] - cum_t_ref[head : head + 1, :], -1e30
+            )
+            weights = (jnp.exp(exponent) * both).astype(low)
+            halves.append(jnp.dot(weights, scaled, preferred_element_type=jnp.float32))
+        carried = jnp.dot(c, held_ref[:, at].astype(low), preferred_element_type=jnp.float32)
+        out = (
+            jnp.where(first_half, halves[0], halves[1])
+            + carried * spread_heads(carry_ref, tile, rows)
+            + spread_heads(skip_ref, tile, rows) * x
+        )
+        scanned_ref[:, at] = out
+        z = proj_ref[:, inner + tile * 128 : inner + (tile + 1) * 128]
+        gated_ref[:, at] = (out * z * jax.nn.sigmoid(z)).astype(low)
+
+
+def ssm_output(*operands):
+    rows, inner = operands[0].shape[0], operands[2].shape[1]
+    outs = [((rows, inner), jnp.float32), ((rows, inner), jnp.bfloat16)]
+    scratch = [pltpu.VMEM((rows + 8, 128), jnp.float32)]
+    return whole_call(ssm_output_kernel, operands, outs, scratch, 8, "ssm_output")
+
+
+def held_grad_kernel(proj_ref, grad_ref, carry_ref, c_ref, out_ref):
+    rows, inner = grad_ref.shape
+    for tile in range(inner // 128):
+        at = slice(tile * 128, (tile + 1) * 128)
+        z = proj_ref[:, inner + tile * 128 : inner + (tile + 1) * 128]
+        grad = grad_ref[:, at].astype(jnp.float32) * z * jax.nn.sigmoid(z)
+        grad = (grad * spread_heads(carry_ref, tile, rows)).astype(jnp.bfloat16)
+        out_ref[:, at] = lax.dot_general(
+            c_ref[...], grad, (((0,), (0,)), ((), ())), preferred_element_type=jnp.float32
+        ).astype(jnp.bfloat16)
+
+
+def held_grad(proj, grad, carry, c):
+    outs = [((STATE, grad.shape[1]), jnp.bfloat16)]
+    return whole_call(held_grad_kernel, (proj, grad, carry, c), outs, [], 4, "held_grad")[0]
+
+
+def ssm_back_kernel(
+    proj_ref,
+    tail_ref,
+    taps_ref,
+    place_ref,
+    grad_ref,
+    scanned_ref,
+    b_ref,
+    c_ref,
+    cum_ref,
+    cum_t_ref,
+    step_ref,
+    raw_ref,
+    rate_ref,
+    skip_ref,
+    last_ref,
+    carry_ref,
+    same_ref,
+    held_ref,
+    later_ref,
+    grad_all_ref,
+    grad_conv_ref,
+    grad_z_ref,
+    end_ref,
+    grad_tail_ref,
+    grad_b_ref,
+    grad_c_ref,
+    grad_raw_ref,
+    grad_taps_ref,
+    grad_heads_ref,
+    extended,
+    sums,
+    columns,
+):
+    rows = b_ref.shape[0]
+    inner = taps_ref.shape[1]
+    tap_count = taps_ref.shape[0]
+    heads = step_ref.shape[1]
+    low = jnp.bfloat16
+
+    def dot(a, b, left=1, right=0):
+        return lax.dot_general(
+            a, b, (((left,), (right,)), ((), ())), preferred_element_type=jnp.float32
+        )
+
+    lane = lax.broadcasted_iota(jnp.int32, (rows, 128), 1)
+    first_half = lane < SHEAD
+    place = place_ref[...]
+    b, c = b_ref[...], c_ref[...]
+    both = dot(c, b, 1, 1)
+    same = same_ref[...] > 0.0
+    sums[...] = jnp.zeros_like(sums)
+    columns[...] = jnp.zeros_like(columns)
+    grad_b = jnp.zeros((rows, STATE), jnp.float32)
+    grad_c = jnp.zeros((rows, STATE), jnp.float32)
+    grad_both = jnp.zeros((rows, rows), jnp.float32)
+    grad_skip = jnp.zeros((1, 128), jnp.float32)
+    picker_row = lax.broadcasted_iota(jnp.int32, (128, 128), 0)
+    picker_lane = lax.broadcasted_iota(jnp.int32, (128, 128), 1)
+
+    def head_sums(values, tile):
+        pick = (picker_lane == 2 * tile + picker_row // SHEAD).astype(low)
+        high = values.astype(low)
+        rest = (values - high.astype(jnp.float32)).astype(low)
+        return dot(high, pick) + dot(rest, pick)
+
+    def spread(ref, tile):
+        return jnp.where(
+            first_half,
+            ref[:, 2 * tile : 2 * tile + 1],
+            ref[:, 2 * tile + 1 : 2 * tile + 2],
+        )
+
+    for tile in range(inner // 128):
+        at = slice(tile * 128, (tile + 1) * 128)
+        z_at = slice(inner + tile * 128, inner + (tile + 1) * 128)
+        extended[8 : 8 + rows] = proj_ref[:, at]
+        extended[0:8] = tail_ref[:, at]
+        lagged = []
+        summed = jnp.zeros((rows, 128), jnp.float32)
+        for lag in range(tap_count):
+            moved = extended[8 - lag : 8 - lag + rows]
+            moved = moved if lag == 0 else jnp.where(place >= lag, moved, 0.0)
+            lagged.append(moved)
+            summed = summed + taps_ref[lag : lag + 1, at] * moved
+        sigma = jax.nn.sigmoid(summed)
+        x = summed * sigma
+        step = spread(step_ref, tile)
+        scaled = x * step
+        z = proj_ref[:, z_at]
+        z_sigma = jax.nn.sigmoid(z)
+        grad_gated = grad_ref[:, at].astype(jnp.float32)
+        grad_y = grad_gated * z * z_sigma
+        grad_z_ref[:, at] = (
+            grad_gated * scanned_ref[:, at] * (z_sigma * (1.0 + z * (1.0 - z_sigma)))
+        ).astype(low)
+        held, later = held_ref[:, at].astype(low), later_ref[:, at].astype(low)
+        last, carry = spread(last_ref, tile), spread(carry_ref, tile)
+        from_later = dot(b, later)
+        from_held = dot(c, held)
+        grad_b = grad_b + dot((scaled * last).astype(low), later, 1, 1)
+        carried_grad = grad_y * carry
+        grad_c = grad_c + dot(carried_grad.astype(low), held, 1, 1)
+        cum_grad = head_sums(carried_grad * from_held - scaled * last * from_later, tile)
+        last_total = head_sums(
+            jnp.sum(scaled * last * from_later, axis=0, keepdims=True), tile
+        )
+        grad_scaled = last * from_later
+        grad_skip = grad_skip + head_sums(jnp.sum(grad_y * x, axis=0, keepdims=True), tile)
+        grad_low, scaled_low = grad_y.astype(low), scaled.astype(low)
+        halves = []
+        for k in range(2):
+            head = 2 * tile + k
+            mine = first_half if k == 0 else ~first_half
+            exponent = jnp.where(
+                same, cum_ref[:, head : head + 1] - cum_t_ref[head : head + 1, :], -1e30
+            )
+            fade = jnp.exp(exponent)
+            weights = fade * both
+            halves.append(dot(weights.astype(low), grad_low, 0, 0))
+            grad_weights = dot(jnp.where(mine, grad_y, 0.0).astype(low), scaled_low, 1, 1)
+            grad_both = grad_both + grad_weights * fade
+            grad_exponent = grad_weights * weights
+            columns[head : head + 1, :] = jnp.sum(grad_exponent, axis=0, keepdims=True)
+            pick = (picker_lane == head).astype(low)
+            high = grad_exponent.astype(low)
+            rest = (grad_exponent - high.astype(jnp.float32)).astype(low)
+            cum_grad = cum_grad + dot(high, pick) + dot(rest, pick)
+        grad_scaled = grad_scaled + jnp.where(first_half, halves[0], halves[1])
+        sums[0] += cum_grad
+        sums[1] += head_sums(grad_scaled * x, tile)
+        sums[2] += last_total
+        grad_x = grad_scaled * step + spread(skip_ref, tile) * grad_y
+        grad_summed = grad_x * (sigma * (1.0 + summed * (1.0 - sigma)))
+        for lag in range(tap_count):
+            grad_taps_ref[lag : lag + 1, at] = jnp.sum(
+                grad_summed * lagged[lag], axis=0, keepdims=True
+            )
+        extended[...] = jnp.zeros_like(extended)
+        for lag in range(tap_count):
+            moved = taps_ref[lag : lag + 1, at] * grad_summed
+            moved = moved if lag == 0 else jnp.where(place >= lag, moved, 0.0)
+            extended[8 - lag : 8 - lag + rows] += moved
+        grad_conv_ref[:, at] = extended[8 : 8 + rows].astype(low)
+        end_ref[:, at] = extended[rows : 8 + rows]
+        grad_tail_ref[:, at] = extended[0:8]
+
+    grad_c_ref[...] = grad_c + dot(grad_both.astype(low), b)
+    grad_b_ref[...] = grad_b + dot(grad_both.astype(low), c, 0, 0)
+    row_at = lax.broadcasted_iota(jnp.int32, (rows, 128), 0)
+    cum_grad = sums[0] - columns[...].T
+    cum_grad = cum_grad + jnp.where(row_at == rows - 1, sums[2] + grad_all_ref[...], 0.0)
+    upper = (
+        lax.broadcasted_iota(jnp.int32, (rows, rows), 0)
+        <= lax.broadcasted_iota(jnp.int32, (rows, rows), 1)
+    ).astype(jnp.float32)
+    log_grad = jnp.dot(upper, cum_grad, precision=highest, preferred_element_type=jnp.float32)
+    log_grad = log_grad[:, :heads]
+    rate = rate_ref[...]
+    step = step_ref[...]
+    raw_grad = (sums[1][:, :heads] - rate * log_grad) * jax.nn.sigmoid(raw_ref[...])
+    grad_raw_ref[...] = raw_grad
+    grad_heads_ref[0:1, :] = jnp.sum(raw_grad, axis=0, keepdims=True)
+    grad_heads_ref[1:2, :] = jnp.sum(-rate * step * log_grad, axis=0, keepdims=True)
+    grad_heads_ref[2:3, :] = grad_skip[:, :heads]
+    grad_heads_ref[3:8, :] = jnp.zeros((5, heads), jnp.float32)
+
+
+def ssm_back(*operands):
+    proj, taps, b, step = operands[0], operands[2], operands[6], operands[10]
+    rows, inner = proj.shape[0], taps.shape[1]
+    heads = step.shape[1]
+    shape = lambda dims, kind: jax.ShapeDtypeStruct(dims, kind)
+    outs = [
+        shape((rows, inner), jnp.bfloat16),
+        shape((rows, inner), jnp.bfloat16),
+        shape((8, inner), jnp.float32),
+        shape((8, inner), jnp.float32),
+        shape((rows, STATE), jnp.float32),
+        shape((rows, STATE), jnp.float32),
+        shape((rows, heads), jnp.float32),
+        shape(taps.shape, jnp.float32),
+        shape((8, heads), jnp.float32),
+    ]
+    return pl.pallas_call(
+        ssm_back_kernel,
+        out_shape=outs,
+        in_specs=[pl.BlockSpec(memory_space=pltpu.VMEM)] * len(operands),
+        out_specs=[pl.BlockSpec(memory_space=pltpu.VMEM)] * len(outs),
+        scratch_shapes=[
+            pltpu.VMEM((rows + 8, 128), jnp.float32),
+            pltpu.VMEM((3, rows, 128), jnp.float32),
+            pltpu.VMEM((128, rows), jnp.float32),
+        ],
+        compiler_params=pltpu.CompilerParams(vmem_limit_bytes=48 * MIB),
+        cost_estimate=cost(20),
+        name="ssm_back",
+    )(*operands)
+
+
 def from_behind(x, axis, by):
     count = lax.axis_size(axis)
     pairs = [(i, i + by) for i in range(count) if 0 <= i + by < count]
@@ -674,23 +1062,27 @@
     return lax.psum_scatter(x, "seq", scatter_dimension=0, axis_index_groups=groups, tiled=True)
 
 
-def exchanged(first, second, side, half):
+def after(x, late):
+    return lax.optimization_barrier((x, late))[0]
+
+
+def exchanged(first, second, side, half, late=None):
     send = jnp.where(side == 0, second, first).astype(jnp.bfloat16)
     keep = jnp.where(side == 0, first, second)
+    if late is not None:
+        send = after(send, late)
     pairs = [(d, (d + half) % (2 * half)) for d in range(2 * half)]
     return keep, lax.ppermute(send, "seq", pairs), send
 
 
-def after(x, late):
-    return lax.optimization_barrier((x, late))[0]
-
-
-def swapped(arrays, half, groups):
+def swapped(arrays, half, groups, late=None):
     widths = [a.shape[1] // (2 * half) for a in arrays]
     rows = arrays[0].shape[0]
     packed = jnp.concatenate([a.reshape(rows, 2, half, -1) for a in arrays], 3)
     packed = jnp.transpose(packed, (2, 0, 1, 3))
     packed = lax.all_to_all(packed, "seq", 0, 0, axis_index_groups=groups, tiled=True)
+    if late is not None:
+        packed = after(packed, late)
     packed = packed.reshape(half * rows, 2, -1)
     out, at = [], 0
     for width in widths:
@@ -709,77 +1101,6 @@
 
 def branch_mix(attn_proj, ssm_proj_out, attn_beta, ssm_beta):
     return attn_beta * rms_scale(attn_proj) + ssm_beta * rms_scale(ssm_proj_out)
-
-
-def silu_slope(entries):
-    sigma = jax.nn.sigmoid(entries)
-    return sigma * (1.0 + entries * (1.0 - sigma))
-
-
-def conv_local(conv_in, tail_x, conv_weight, place_in_item):
-    row_count = conv_in.shape[0]
-    tap_count = conv_weight.shape[0]
-    extended = jnp.concatenate([tail_x, conv_in], 0)
-    summed = conv_weight[0] * conv_in
-    for tap_lag in range(1, tap_count):
-        first_row = tap_count - 1 - tap_lag
-        lagged = extended[first_row : first_row + row_count]
-        same_item = (place_in_item >= tap_lag)[:, None]
-        summed = summed + conv_weight[tap_lag] * jnp.where(same_item, lagged, 0.0)
-    return jax.nn.silu(summed)
-
-
-def ssm_parts(conv_in, select, tail_x, conv_weight, step_bias, decay_log, place_in_item):
-    row_count = conv_in.shape[0]
-    conv_out = conv_local(conv_in, tail_x, conv_weight, place_in_item)
-    heads_x = conv_out.reshape(row_count, -1, SHEAD)
-    b_proj = select[:, :STATE]
-    c_proj = select[:, STATE : 2 * STATE]
-    step_size = jax.nn.softplus(select[:, 2 * STATE :] + step_bias)
-    log_decay = -step_size * jnp.exp(decay_log)
-    lower_tri = (jnp.arange(row_count)[:, None] >= jnp.arange(row_count)[None, :]).astype(
-        jnp.float32
-    )
-    cum_decay = jnp.dot(lower_tri, log_decay, precision=highest)
-    scaled_x = heads_x * step_size[:, :, None]
-    return (heads_x, b_proj, c_proj, cum_decay, scaled_x, lower_tri)
-
-
-def ssm_output(
-    conv_in,
-    select,
-    tail_x,
-    conv_weight,
-    step_bias,
-    decay_log,
-    skip_gain,
-    held_in,
-    place_in_item,
-    items,
-):
-    heads_x, b_proj, c_proj, cum_decay, scaled_x, lower_tri = ssm_parts(
-        conv_in, select, tail_x, conv_weight, step_bias, decay_log, place_in_item
-    )
-    same_item = (items[:, None] == items[None, :]) & (lower_tri > 0)
-    exponent = jnp.where(same_item[None], cum_decay.T[:, :, None] - cum_decay.T[:, None, :], -1e30)
-    weights = jnp.exp(exponent) * jnp.dot(c_proj, b_proj.T, precision=highest)[None]
-    local_part = jnp.einsum("htr,rhp->thp", weights, scaled_x, precision=highest)
-    follow = (items == 0).astype(jnp.float32)
-    carry_weight = jnp.exp(cum_decay) * follow[:, None]
-    carried = jnp.einsum("th,hpn,tn->thp", carry_weight, held_in, c_proj, precision=highest)
-    outputs = local_part + carried + skip_gain[None, :, None] * heads_x
-    return outputs.reshape(conv_in.shape[0], -1)
-
-
-def ssm_state(conv_in, select, tail_x, conv_weight, step_bias, decay_log, place_in_item, items):
-    heads_x, b_proj, c_proj, cum_decay, scaled_x, lower_tri = ssm_parts(
-        conv_in, select, tail_x, conv_weight, step_bias, decay_log, place_in_item
-    )
-    last_same = (items == items[-1]).astype(jnp.float32)
-    last_weight = jnp.exp(cum_decay[-1][None, :] - cum_decay) * last_same[:, None]
-    fresh_state = jnp.einsum("rh,rhp,rn->hpn", last_weight, scaled_x, b_proj, precision=highest)
-    through = (items[-1] == 0).astype(jnp.float32)
-    return (fresh_state, jnp.exp(cum_decay[-1]) * through)
 
 
 def per_device(
@@ -826,7 +1147,6 @@
     normed = scaled_norm(layer_in, mixer_gain).astype(jnp.bfloat16)
     query_weight = attn_weight[:, :model_width]
     kv_weight = attn_weight[:, model_width:qkv_cols]
-    flip = [(d, (d + half) % devices) for d in range(devices)]
     kv = jnp.dot(normed, kv_weight, preferred_element_type=jnp.float32).astype(jnp.bfloat16)
     queries = lax.dot_general(
         query_weight, normed, (((0,), (1,)), ((), ())), preferred_element_type=jnp.float32
@@ -835,37 +1155,40 @@
         GROUPS, per_group, HEAD, row_count
     )
     ssm_proj = jnp.dot(normed, ssm_weight, preferred_element_type=jnp.float32)
-    conv_in = ssm_proj[:, :INNER]
-    z_gate = ssm_proj[:, INNER:]
     select = jnp.dot(normed, select_weight, preferred_element_type=jnp.float32)
-    tail_x = from_behind(conv_in[row_count - CONV + 1 :].astype(jnp.bfloat16), "seq", 1).astype(
-        jnp.float32
+    last_rows = ssm_proj[row_count - CONV + 1 :, :INNER].astype(jnp.bfloat16)
+    tail_x = jnp.pad(
+        from_behind(last_rows, "seq", 1).astype(jnp.float32), ((8 - CONV + 1, 0), (0, 0))
     )
     row = jnp.arange(row_count, dtype=jnp.int32)
     starts = jnp.where((meta_index == 0)[None, :] & (row[None, :] <= row[:, None]), 1, 0)
     items = jnp.sum(starts, axis=1)
     own_start = jnp.max(starts * (row[None, :] + 1), axis=1) - 1 + device_index * row_count
-    (fresh_state, decay_all), state_pull = jax.vjp(
-        partial(ssm_state, place_in_item=meta_index, items=items),
-        conv_in,
-        select,
-        tail_x,
-        conv_weight,
-        step_bias,
-        decay_log,
+    same_item = ((items[:, None] == items[None, :]) & (row[None, :] <= row[:, None])).astype(
+        jnp.float32
     )
     sheads = INNER // SHEAD
-    padded = (sheads + 15) // 16 * 16
-    state_sent = jnp.pad(
-        fresh_state.reshape(sheads, SHEAD * STATE).astype(jnp.bfloat16),
-        ((0, padded - sheads), (0, 0)),
-    )
+    place_in_item = meta_index[:, None]
+    rate = jnp.exp(decay_log)[None, :]
+    state, b_proj, c_proj, raw, step_size, cum, cum_t, last_weight, carry_weight, decay_all = (
+        ssm_state(
+            ssm_proj,
+            tail_x,
+            conv_weight,
+            place_in_item,
+            items[:, None],
+            select,
+            step_bias[None, :],
+            rate,
+        )
+    )
+    states = lax.all_gather(state, "seq")
     last_start = jnp.where(items[-1] > 0, own_start[-1], -1).astype(jnp.float32)
     facts = jnp.concatenate(
-        [decay_all, jnp.full((128 - sheads,), 1.0) * last_start]
+        [decay_all[0], jnp.full((128 - sheads,), 1.0) * last_start]
     )
     facts = jnp.broadcast_to(facts[None, :], (8, 128))
-    kv_all, states, facts = gather_both([kv, state_sent, facts], half, 0)
+    kv_all, facts = gather_both([kv, facts], half, 0)
     ordered = facts[:, 0].reshape(2, half, 128)
     ordered = jnp.where(side == 0, ordered[::-1], ordered).reshape(devices, 128)
     shard = jnp.arange(devices, dtype=jnp.int32)
@@ -891,23 +1214,23 @@
         jnp.prod(jnp.where(between_after[:, :, None], decays[None], 1.0), axis=1),
         0.0,
     )
-    by_slot = weight_before.reshape(2, half, sheads)
-    by_slot = jnp.where(side == 0, by_slot[::-1], by_slot).reshape(devices, sheads)
-    by_slot = jnp.pad(by_slot, ((0, 0), (0, padded - sheads)))
-    held_in = jnp.sum(by_slot[:, :, None] * states.astype(jnp.float32), axis=0)[:sheads]
-    held_in = held_in.reshape(sheads, SHEAD, STATE)
-    scanned, output_pull = jax.vjp(
-        partial(ssm_output, place_in_item=meta_index, items=items),
-        conv_in,
-        select,
+    per_channel = lambda weight: jnp.repeat(weight, SHEAD, axis=1)[:, None, :]
+    held_in = jnp.sum(per_channel(weight_before) * states.astype(jnp.float32), axis=0)
+    scanned, gated = ssm_output(
+        ssm_proj,
         tail_x,
         conv_weight,
-        step_bias,
-        decay_log,
-        skip_gain,
+        place_in_item,
+        b_proj,
+        c_proj,
+        cum,
+        cum_t,
+        step_size,
+        skip_gain[None, :],
+        carry_weight,
+        same_item,
         held_in,
     )
-    gated = (scanned * jax.nn.silu(z_gate)).astype(jnp.bfloat16)
     ssm_proj_out = jnp.dot(gated, ssm_down, preferred_element_type=jnp.float32)
     mixed_terms, mix_pull = jax.vjp(branch_mix, attn_proj, ssm_proj_out, attn_beta, ssm_beta)
     hidden1 = layer_in + mixed_terms
@@ -934,19 +1257,28 @@
         ffn_rows, cot_rows, in_weight, down_weight
     )
     in_terms = in_terms.reshape(half, row_count, model_width)
-    grad_ffn_in = sum_half(in_terms, 1, half, 3)[0].astype(jnp.float32)
-    out_sum = summed_rows(out_terms, groups)
+    grad_ffn_in = sum_half(in_terms, 1, half, 3)
     gate_keep, gate_sent, _ = exchanged(
         in_weight_terms[:units], in_weight_terms[wide : wide + units], side, half
     )
-    down_keep, down_sent, _ = exchanged(
-        down_terms[: units // 2], down_terms[units // 2 : units], side, half
-    )
+    down_low = down_terms[:units].astype(jnp.bfloat16).reshape(2, units // 2, model_width)
+    down_low = jnp.where(side == 0, down_low, down_low[::-1])
+    down_sent = [
+        lax.ppermute(
+            down_low[k],
+            "seq",
+            [(h * half + q, 2 * q + (h + k) % 2) for h in range(2) for q in range(half)],
+        )
+        for k in range(2)
+    ]
     grad_from_ffn, grad_ffn_gain = ffn_norm_pull(grad_ffn_in)
     grad_hidden1 = cotangent.astype(jnp.float32) + grad_from_ffn
     grad_attn_proj, grad_ssm_proj_out, grad_attn_beta, grad_ssm_beta = mix_pull(grad_hidden1)
     attn_grad_low = grad_attn_proj.astype(jnp.bfloat16)
     ssm_grad_low = grad_ssm_proj_out.astype(jnp.bfloat16)
+    grad_gated = jnp.dot(ssm_grad_low, ssm_down.T, preferred_element_type=jnp.float32).astype(
+        jnp.bfloat16
+    )
     out_grad = (
         lax.dot_general(
             out_weight, attn_grad_low, (((0,), (1,)), ((), ())), preferred_element_type=jnp.float32
@@ -957,20 +1289,17 @@
     grad_queries, kv_terms = attend_back(
         steps, queries, kv_all, first[None, :], attn_full, log_sum, out_grad, half
     )
-    down_own = down_keep + after(down_sent, grad_queries).astype(jnp.float32)
-    down_moved = lax.ppermute(
-        down_own.astype(jnp.bfloat16),
-        "seq",
-        [(h * half + q, 2 * q + h) for h in range(2) for q in range(half)],
-    )
-    grad_kv_other, grad_kv = sum_half(kv_terms, 2, half, 1)
-    grad_kv = grad_kv.astype(jnp.float32) + lax.ppermute(grad_kv_other, "seq", flip).astype(
-        jnp.float32
-    )
+    def complete(keep, sent, late):
+        return keep + after(sent, late).astype(jnp.float32)
+
+    grad_kv = sum_half(kv_terms, 2, half, 1)
+    grad_gate_up = complete(gate_keep, gate_sent, grad_queries)
+    grad_ffn_down = sum(after(sent, grad_queries).astype(jnp.float32) for sent in down_sent)
+    grad_kv = after(grad_kv, (grad_gate_up, grad_ffn_down))
     qkv_grad = jnp.concatenate(
         [grad_queries.reshape(model_width, row_count).T, grad_kv.astype(jnp.bfloat16)], 1
     )
-    gated_columns = swapped([gated], half, groups)[0]
+    gated_columns = swapped([gated], half, groups, grad_kv)[0]
     attn_columns = swapped([jnp.concatenate([qkv_grad, attended], 1)], half, groups)[0]
     normed_rows = gathered(normed, groups)
     attn_grad_rows = gathered(attn_grad_low, groups)
@@ -987,40 +1316,54 @@
                 jnp.dot(block.T, attn_grad_rows, preferred_element_type=jnp.float32),
             )
         )
-    attn_keep, attn_sent, attn_send = exchanged(attn_terms[0], attn_terms[1], side, half)
+    held_grads = lax.all_gather(held_grad(ssm_proj, grad_gated, carry_weight, c_proj), "seq")
+    later_grad = jnp.sum(per_channel(weight_after) * held_grads.astype(jnp.float32), axis=0)
+    grad_decay_all = jnp.sum((later_grad * held_in).reshape(STATE, sheads, SHEAD), axis=(0, 2))
+    grad_all = jnp.pad((grad_decay_all * decay_all[0])[None, :], ((0, 0), (0, 128 - sheads)))
+    conv_grad, z_grad, end_rows, grad_tail, grad_b, grad_c, grad_raw, grad_conv, grad_heads = (
+        ssm_back(
+            ssm_proj,
+            tail_x,
+            conv_weight,
+            place_in_item,
+            grad_gated,
+            scanned,
+            b_proj,
+            c_proj,
+            cum,
+            cum_t,
+            step_size,
+            raw,
+            rate,
+            skip_gain[None, :],
+            last_weight,
+            carry_weight,
+            same_item,
+            held_in,
+            later_grad,
+            grad_all,
+        )
+    )
+    grad_step_bias, grad_decay, grad_skip = grad_heads[0], grad_heads[1], grad_heads[2]
+    out_sum = summed_rows(after(out_terms, grad_raw), groups)
+    tail_back = from_behind(grad_tail[8 - CONV + 1 :].astype(jnp.bfloat16), "seq", -1)
+    end_rows = end_rows[8 - CONV + 1 :] + tail_back.astype(jnp.float32)
+    grad_select_in = jnp.concatenate([grad_b, grad_c, grad_raw], 1).astype(jnp.bfloat16)
+    attn_keep, attn_sent, attn_send = exchanged(
+        attn_terms[0], attn_terms[1], side, half, tail_back
+    )
     ssm_down_keep, ssm_down_sent, ssm_down_send = exchanged(
         jnp.dot(gated_columns[0].T, ssm_grad_rows, preferred_element_type=jnp.float32),
         jnp.dot(gated_columns[1].T, ssm_grad_rows, preferred_element_type=jnp.float32),
         side,
         half,
-    )
-    grad_gated = (
-        jnp.dot(ssm_grad_low, ssm_down.T, preferred_element_type=jnp.float32)
-        .astype(jnp.bfloat16)
-        .astype(jnp.float32)
-    )
-    grad_scanned = grad_gated * jax.nn.silu(z_gate)
-    grad_z_gate = grad_gated * scanned * silu_slope(z_gate)
-    output_grads = output_pull(grad_scanned)
-    held_grads = lax.all_gather(
-        output_grads[7].reshape(sheads, SHEAD * STATE).astype(jnp.bfloat16), "seq"
-    )
-    later_grad = jnp.sum(weight_after[:, :, None] * held_grads.astype(jnp.float32), axis=0)
-    later_grad = later_grad.reshape(sheads, SHEAD, STATE)
-    grad_decay_all = jnp.sum(later_grad * held_in, axis=(1, 2))
-    state_grads = state_pull((later_grad, grad_decay_all))
-    grad_tail = output_grads[2] + state_grads[2]
-    tail_back = from_behind(as_sent(grad_tail), "seq", -1).astype(grad_tail.dtype)
-    grad_conv_in = output_grads[0] + state_grads[0]
-    grad_conv_in = jnp.concatenate(
-        [grad_conv_in[: row_count - CONV + 1], grad_conv_in[row_count - CONV + 1 :] + tail_back], 0
-    )
-    grad_select_in = (output_grads[1] + state_grads[1]).astype(jnp.bfloat16)
-    grad_conv = output_grads[3] + state_grads[3]
-    grad_step_bias = output_grads[4] + state_grads[4]
-    grad_decay = output_grads[5] + state_grads[5]
-    grad_skip = output_grads[6]
-    proj_grad = jnp.concatenate([grad_conv_in, grad_z_gate], 1).astype(jnp.bfloat16)
+        tail_back,
+    )
+    conv_grad = jnp.concatenate(
+        [conv_grad[: row_count - CONV + 1], end_rows.astype(jnp.bfloat16)], 0
+    )
+    proj_grad = jnp.concatenate([conv_grad, z_grad], 1)
+    proj_grad = after(proj_grad, attn_send)
     ssm_columns = swapped([proj_grad], half, groups)[0]
     grad_normed = jnp.dot(qkv_grad, attn_weight[:, :qkv_cols].T, preferred_element_type=jnp.float32)
     grad_normed = grad_normed + jnp.dot(proj_grad, ssm_weight.T, preferred_element_type=jnp.float32)
@@ -1054,7 +1397,9 @@
     packed = jnp.concatenate(
         pieces + [jnp.zeros((share * devices - sum(counts), model_width), jnp.float32)], 0
     )
-    packed = after(packed, (attn_send, ssm_down_send, ssm_send))
+    packed = after(
+        packed, (attn_send, ssm_down_send, ssm_send)
+    )
     packed = total_of(packed.reshape(devices, share, model_width), devices, 4)
     packed = packed.reshape(devices * share, model_width)
     at = [sum(counts[:i]) for i in range(len(counts))]
@@ -1072,18 +1417,15 @@
         gains[2],
         gains[3],
     )
-    late = little
-
-    def complete(keep, sent):
-        return keep + after(sent, late).astype(jnp.float32)
-
+    grad_ssm = complete(ssm_keep, ssm_sent, little)
+    late = grad_ssm[0]
     layer_out = (hidden1 + after(out_sum, late).astype(jnp.float32)).astype(jnp.bfloat16)
     shares = (
-        complete(attn_keep, attn_sent).T,
-        complete(ssm_keep, ssm_sent).T,
-        complete(ssm_down_keep, ssm_down_sent),
-        complete(gate_keep, gate_sent).T,
-        after(down_moved, late).astype(jnp.float32),
+        complete(attn_keep, attn_sent, late).T,
+        grad_ssm.T,
+        complete(ssm_down_keep, ssm_down_sent, late),
+        grad_gate_up.T,
+        grad_ffn_down,
     )
     return (
         layer_out,

time: 778 us -> 733 us (0.942)
  waiting for transfers between devices: 34 us -> 88.2 us
  matrix products: 145 us -> 95.6 us
  other arithmetic: 78.5 us -> 43.6 us
  Pallas kernels: 341 us -> 366 us
  local copies, waits for them, and re-layouts: 96.8 us -> 76 us
  starting transfers between devices: 54.5 us -> 39 us
    all_gather x4, waiting for transfers between devices: 0.05 us -> 65.3 us  [gathered(): return lax.all_gather(x, 'seq', axis_index_groups=groups, tiled=True)]
    pallas_call x2 -> x6, Pallas kernels: 82.3 us -> 145 us  [the longest x2 119 us: sum_half(): pl.pallas_call(partial(sum_kernel, arrays, half), out_shape=jax.ShapeDtyp...]
    dot_general x15 -> x0, matrix products: 44.6 us -> none  [the longest x3 21.7 us: ssm_output(): jnp.einsum('htr,rhp->thp', weights, scaled_x, precision=highest)]
    pallas_call x1, Pallas kernels: 79.7 us -> 52.7 us  [gather_both(): pl.pallas_call(partial(gather_both_kernel, count, half), out_shape=[jax.S...]
    reshape x13 -> x1, local copies, waits for them, and re-layouts: 15.6 us -> 0.27 us  [per_device(): down_terms[:units].astype(jnp.bfloat16).reshape(2, units // 2, model_width)]
    unnamed x270 -> x254, local copies, waits for them, and re-layouts: 15.7 us -> 27.7 us
    all_to_all x3, waiting for transfers between devices: 32.8 us -> 21.2 us  [swapped(): lax.all_to_all(packed, 'seq', 0, 0, axis_index_groups=groups, tiled=True)]
    ppermute x5 -> x4, starting transfers between devices: 23.8 us -> 13.9 us  [exchanged(): return (keep, lax.ppermute(send, 'seq', pairs), send)]
  transfers between devices with their start and end apart: 18 -> 18, of which waited for: 3 -> 4; matrix products, arithmetic and copies ran while one was open for 40% -> 23% of each run, Pallas kernels for 44% -> 39%
where the time goes in v3:
time: 733 us; the launch traced here: 727 us
  Pallas kernels  366 us (50%)
  matrix products  95.6 us (13%)
  waiting for transfers between devices  88.2 us (12%)
  local copies, waits for them, and re-layouts  76 us (10%)
  other arithmetic  43.6 us (6%)
  starting transfers between devices  39 us (5%)
  between operations  18.3 us (2%)
    pallas_call x2, Pallas kernels, sum_half(): pl.pallas_call(partial(sum_kernel, arrays, half), out_shape=jax.ShapeDtyp...  119 us
    all_gather x4, waiting for transfers between devices, gathered(): return lax.all_gather(x, 'seq', axis_index_groups=groups, tiled=True)  65.3 us
    pallas_call x1, Pallas kernels, total_of(): pl.pallas_call(partial(total_kernel, devices), out_shape=jax.ShapeDtypeSt...  62.4 us
    pallas_call x1, Pallas kernels, gather_both(): pl.pallas_call(partial(gather_both_kernel, count, half), out_shape=[jax.S...  52.7 us
    pallas_call x1, Pallas kernels, gather_half(): pl.pallas_call(partial(gather_kernel, count, half), out_shape=jax.ShapeDt...  50 us
    pallas_call x1, Pallas kernels, ffn(): pl.pallas_call(ffn_kernel, grid=(rows // block,), out_shape=[jax.ShapeDty...  43.2 us
    unnamed x254, local copies, waits for them, and re-layouts  27.7 us
    all_to_all x3, waiting for transfers between devices, swapped(): lax.all_to_all(packed, 'seq', 0, 0, axis_index_groups=groups, tiled=True)  21.2 us
  transfers between devices with their start and end apart: 18, of which 4 were waited for; matrix products, arithmetic and copies ran while one was open for 23% of the time, Pallas kernels for 39%

profile of v3, /device:TPU:0, one launch (start us, length us, event | category | flops | bytes accessed | tf_op | source)
XLA Modules:
  0.0 727.1 jit_solution(10197260565999877603)
XLA Ops:
  13.0 10.2 %fusion.64.proj_ref = f32[128,6400]{1,0:T(8,128)S(1)} fusion(bf16[128,1600]{1,0:T(8,128)(2,1)} %multiply_convert_fusion.1, bf16[1600,6400]{1,0:T(8,128)(2,1)} %param.24), kind=kOutput, calls=%fused_computation.162 | convolution fusion | flops 2621440000 | bytes 24166400 | tf_op jit(solution)/shard_map/dot_general | solution.py:1157
  59.2 5.4 fusion.22
  65.3 52.7 %gather_both.1 = (bf16[32,128,640]{2,1,0:T(8,128)(2,1)}, f32[32,8,128]{2,1,0:T(8,128)}) custom-call(bf16[128,640]{1,0:T(8,128)(2,1)} %fusion.27.refs_0_, f32[8,128]{1,0:T(8,128)} %broadcast_in_dim.193.refs_1_), custom_call_target="tpu_custom_call" | custom-call | bytes 150000000 | tf_op jit(solution)/shard_map/gather_both/pallas_call | solution.py:225
  121.1 5.6 attend.1
  137.7 5.9 ssm_output.1
  143.7 6.9 multiply_reduce_fusion.10
  154.4 50.0 %gather_half.1 = bf16[16,128,1600]{2,1,0:T(8,128)(2,1)} custom-call(bf16[128,1600]{1,0:T(8,128)(2,1)} %multiply_convert_fusion.refs_0_), custom_call_target="tpu_custom_call" | custom-call | bytes 120000000 | tf_op jit(solution)/shard_map/gather_half/pallas_call | solution.py:139
  204.5 43.2 %ffn.1 = (bf16[2048,1600]{1,0:T(8,128)(2,1)}, bf16[2048,1600]{1,0:T(8,128)(2,1)}, f32[768,1600]{1,0:T(8,128)}, f32[384,1600]{1,0:T(8,128)}) custom-call(bf16[2048,1600]{1,0:T(8,128)(2,1)} %bitcast.150, bf16[2048,1600]{1,0:T(8,128)(2,1)} %all-gather.9.cloned.1.call-done.cot_ref, bf16[1600,768]{1,0:T(8,128)(2,1)} %fusion.15.in_ref, bf16[384,1600]{1,0:T(8,128)(2,1)} %pad.30.down_ref), custom_call_target="tpu_custom_call" | custom-call | bytes 105000000 | tf_op jit(solution)/shard_map/ffn/pallas_call | solution.py:498
  247.7 35.5 %sum_half.2 = f32[128,1600]{1,0:T(8,128)} custom-call(bf16[16,128,1600]{2,1,0:T(8,128)(2,1)} %bitcast.151), custom_call_target="tpu_custom_call" | custom-call | bytes 150000000 | tf_op jit(solution)/shard_map/sum_half/pallas_call | solution.py:440
  289.1 5.9 convolution_convert_fusion.grad_ref
  305.4 9.1 %collective-permute-start.2 = (bf16[344,1600]{1,0:T(8,128)(2,1)}, bf16[344,1600]{1,0:T(8,128)(2,1)}, u32[]{:S(2)}, u32[]{:S(2)}) collective-permute-start(bf16[344,1600]{1,0:T(8,128)(2,1)} %select_convert_fusion), channel_id=1, source_target_pairs={{0,16},{1,17},{2,18},{3,19},{4,20},{5,21},{6,22},{7,23},{8,24},{9,... | collective-permute-start | bytes 3302408 | tf_op jit(solution)/shard_map/ppermute | solution.py:1075
  315.6 5.9 collective-permute-start.3
  328.3 7.8 %fusion.16 = bf16[128,1600]{0,1:T(8,128)(2,1)} fusion(bf16[128,1600]{1,0:T(8,128)(2,1)S(1)} %copy-done.87, bf16[1600,3840]{1,0:T(8,128)(2,1)} %param.23), kind=kOutput, calls=%fused_computation.23 | convolution fusion | flops 655564800 | bytes 6144000 | tf_op jit(solution)/shard_map/dot_general | solution.py:1283
  336.1 7.5 %attend_back.1 = (bf16[5,5,64,128]{3,2,1,0:T(8,128)(2,1)}, bf16[32,128,640]{2,1,0:T(8,128)(2,1)}) custom-call(s32[2]{0:T(128)} %pad_add_fusion.steps_ref, bf16[5,5,64,128]{3,2,1,0:T(8,128)(2,1)} %bitcast.161, bf16[32,128,640]{2,1,0:T(8,128)(2,1)} %get-tuple-element.63.kv_ref, s32[1,128]{1,0:T(1,128)} %bitcast.175, ...), custom_call_target="tpu_custom_call" | custom-call | bytes 60000000 | tf_op jit(solution)/shard_map/attend_back/pallas_call | solution.py:651
  343.6 83.8 %sum_half.3 = f32[128,640]{1,0:T(8,128)} custom-call(bf16[32,128,640]{2,1,0:T(8,128)(2,1)} %get-tuple-element.86.refs_0_), custom_call_target="tpu_custom_call" | custom-call | bytes 150000000 | tf_op jit(solution)/shard_map/sum_half/pallas_call | solution.py:440
  435.8 6.2 all-to-all-start
  449.7 13.2 %all-to-all-done = bf16[16,128,2,120]{1,3,2,0:T(8,128)(2,1)} async-done(((bf16[16,128,2,120]{1,3,2,0:T(8,128)(2,1)}), bf16[16,128,2,120]{1,3,2,0:T(8,128)(2,1)}, u32[]{:S(2)}, u32[]{:S(2)}) %all-to-all-start) | async-done | bytes 983072 | tf_op jit(solution)/shard_map/all_to_all | solution.py:1083
  470.3 15.4 %ssm_back.1 = (bf16[128,3200]{1,0:T(8,128)(2,1)S(1)}, bf16[128,3200]{1,0:T(8,128)(2,1)S(1)}, f32[8,3200]{1,0:T(8,128)S(1)}, f32[8,3200]{1,0:T(8,128)S(1)}, f32[1...) custom-call(f32[128,6400]{1,0:T(8,128)} %copy-done.2, ...), custom_call_target="tpu_custom_call" | custom-call | bytes 60000000 | tf_op jit(solution)/shard_map/ssm_back/pallas_call | solution.py:1031
  506.4 24.0 %all-gather.15.cloned.1.call-done = bf16[2048,1600]{1,0:T(8,128)(2,1)} async-done(((bf16[128,1600]{1,0:T(8,128)(2,1)}), bf16[2048,1600]{1,0:T(8,128)(2,1)}) %all-gather.15.cloned.1.call-update) | async-done | bytes 6553616 | tf_op jit(solution)/shard_map/all_gather | solution.py:1058
  540.2 41.3 %all-gather.13.cloned.1.call-done = bf16[2048,1600]{1,0:T(8,128)(2,1)} async-done(((bf16[128,1600]{1,0:T(8,128)(2,1)}), bf16[2048,1600]{1,0:T(8,128)(2,1)}) %all-gather.13.cloned.1.call-update) | async-done | bytes 6553616 | tf_op jit(solution)/shard_map/all_gather | solution.py:1058
  599.4 10.6 %fusion.66 = f32[128,1600]{1,0:T(8,128)S(1)} fusion(bf16[128,6400]{1,0:T(8,128)(2,1)S(1)} %pad_maximum_fusion, bf16[1600,6400]{1,0:T(8,128)(2,1)} %param.24), kind=kOutput, calls=%fused_computation.164 | convolution fusion | flops 2621440000 | bytes 22937600 | tf_op jit(solution)/shard_map/dot_general | solution.py:1369
  610.1 5.7 fusion.12
  627.2 8.0 %all-to-all-done.1 = bf16[16,128,2,200]{1,3,2,0:T(8,128)(2,1)S(1)} async-done(((bf16[16,128,2,200]{1,3,2,0:T(8,128)(2,1)}), bf16[16,128,2,200]{1,3,2,0:T(8,128)(2,1)S(1)}, u32[]{:S(2)}, u32[]{:S(2)}) %all-to-all-start.1) | async-done | bytes 1638432 | tf_op jit(solution)/shard_map/all_to_all | solution.py:1083
  644.3 62.4 %total_of.1 = f32[32,8,1600]{2,1,0:T(8,128)S(1)} custom-call(f32[32,8,1600]{2,1,0:T(8,128)S(1)} %bitcast.138), custom_call_target="tpu_custom_call" | custom-call | bytes 120000000 | tf_op jit(solution)/shard_map/total_of/pallas_call | solution.py:321
  (418 shorter events, 186.6 us)
Async XLA Ops:
  7.2 127.7 %all-gather.17.cloned.1.call-start = ((), (), s32[]{:S(2)}) async-start(), calls=%async_computation.9 | async-start | bytes 3379200 | tf_op jit(solution)/shard_map/all_gather | solution.py:1185
  23.9 3.6 collective-permute-start
  37.4 167.1 %all-gather.9.cloned.1.call-start = ((), (), s32[]{:S(2)}) async-start(), calls=%async_computation.4 | async-start | bytes 7241728 | tf_op jit(solution)/shard_map/all_gather | solution.py:1058
  39.4 425.6 %all-gather.19.cloned.1.call-start = ((), (), s32[]{:S(2)}) async-start(), calls=%async_computation.10 | async-start | bytes 3379200 | tf_op jit(solution)/shard_map/all_gather | solution.py:1319
  50.8 86.8 %copy-start.21 = (f32[128,128]{1,0:T(8,128)}, f32[128,128]{1,0:T(8,128)S(1)}, u32[]{:S(2)}) copy-start(f32[128,128]{1,0:T(8,128)S(1)} %fusion.50.same_ref) | copy-start | bytes 196612
  153.4 131.9 %copy-start.66 = (f32[128,1600]{1,0:T(8,128)}, f32[128,1600]{1,0:T(8,128)S(1)}, u32[]{:S(2)}) copy-start(f32[128,1600]{1,0:T(8,128)S(1)} %get-tuple-element.212) | copy-start | bytes 2457604
  247.7 37.5 %copy-start.73 = (f32[128,1600]{1,0:T(8,128)S(1)}, f32[128,1600]{1,0:T(8,128)}, u32[]{:S(2)}) copy-start(f32[128,1600]{1,0:T(8,128)} %copy.184) | copy-start | bytes 2457604
  298.0 193.4 %all-gather.11.cloned.1.call-start = ((), (), s32[]{:S(2)}) async-start(), calls=%async_computation.6 | async-start | bytes 7241728 | tf_op jit(solution)/shard_map/all_gather | solution.py:1058
  298.6 231.8 %all-gather.15.cloned.1.call-start = ((), (), s32[]{:S(2)}) async-start(), calls=%async_computation.8 | async-start | bytes 7241728 | tf_op jit(solution)/shard_map/all_gather | solution.py:1058
  299.2 282.3 %all-gather.13.cloned.1.call-start = ((), (), s32[]{:S(2)}) async-start(), calls=%async_computation.7 | async-start | bytes 7241728 | tf_op jit(solution)/shard_map/all_gather | solution.py:1058
  305.4 124.5 %collective-permute-start.2 = (bf16[344,1600]{1,0:T(8,128)(2,1)}, bf16[344,1600]{1,0:T(8,128)(2,1)}, u32[]{:S(2)}, u32[]{:S(2)}) collective-permute-start(bf16[344,1600]{1,0:T(8,128)(2,1)} %select_convert_fusion), channel_id=1, source_target_pairs={{0,16},{1,17},{2,18},{3,19},{4,20},{5,21},{6,22},{7,23},{8,24},{9,... | collective-permute-start | bytes 3302408 | tf_op jit(solution)/shard_map/ppermute | solution.py:1075
  315.6 111.9 %collective-permute-start.3 = (bf16[172,1600]{1,0:T(8,128)(2,1)}, bf16[172,1600]{1,0:T(8,128)(2,1)}, u32[]{:S(2)}, u32[]{:S(2)}) collective-permute-start(bf16[172,1600]{1,0:T(8,128)(2,1)} %get-tuple-element.218), channel_id=1, source_target_pairs={{0,0},{1,2},{2,4},{3,6},{4,8},{5,10},{6,12},{7,14},{8,16},{9,18},{... | collective-permute-start | bytes 1651208 | tf_op jit(solution)/shard_map/ppermute | solution.py:1267
  321.6 105.9 %collective-permute-start.4 = (bf16[172,1600]{1,0:T(8,128)(2,1)S(1)}, bf16[172,1600]{1,0:T(8,128)(2,1)}, u32[]{:S(2)}, u32[]{:S(2)}) collective-permute-start(bf16[172,1600]{1,0:T(8,128)(2,1)S(1)} %get-tuple-element.219), channel_id=1, source_target_pairs={{0,1},{1,3},{2,5},{3,7},{4,9},{5,11},{6,13},{7,15},{8,17},{9,19},{... | collective-permute-start | bytes 1651208 | tf_op jit(solution)/shard_map/ppermute | solution.py:1267
  324.3 111.5 %all-to-all-start.2 = ((bf16[16,128,2,100]{1,2,3,0:T(2,128)(2,1)}), bf16[16,128,2,100]{1,2,3,0:T(2,128)(2,1)S(1)}, u32[]{:S(2)}, u32[]{:S(2)}) async-start(bf16[16,128,2,100]{1,2,3,0:T(2,128)(2,1)} %copy.211), calls=%async_computation.3 | async-start | bytes 1638400 | tf_op jit(solution)/shard_map/all_to_all | solution.py:1083
  435.8 27.0 %all-to-all-start = ((bf16[16,128,2,120]{1,3,2,0:T(8,128)(2,1)}), bf16[16,128,2,120]{1,3,2,0:T(8,128)(2,1)}, u32[]{:S(2)}, u32[]{:S(2)}) async-start(bf16[16,128,2,120]{1,3,2,0:T(8,128)(2,1)} %copy.194), calls=%async_computation.1 | async-start | bytes 1966080 | tf_op jit(solution)/shard_map/all_to_all | solution.py:1083
  442.0 275.7 %reduce-scatter.2.cloned.1.call-start = ((), (), s32[]{:S(2)}) async-start(), calls=%async_computation.5 | async-start | bytes 7241728 | tf_op jit(solution)/shard_map/reduce_scatter | solution.py:1062
  501.1 5.1 collective-permute-start.1
  535.6 45.9 %copy-start.72 = (bf16[2048,2,120]{0,2,1:T(8,128)(2,1)S(1)}, bf16[2048,2,120]{0,2,1:T(8,128)(2,1)}, u32[]{:S(2)}) copy-start(bf16[2048,2,120]{0,2,1:T(8,128)(2,1)} %copy_bitcast_fusion.1) | copy-start | bytes 2949124
  535.6 45.9 %copy-start.118 = (pred[120]{0:T(512)(128)(4,1)S(1)}, pred[120]{0:T(512)(128)(4,1)}, u32[]{:S(2)}) copy-start(pred[120]{0:T(512)(128)(4,1)} %add_compare_fusion) | copy-start | bytes 364
  537.8 48.0 %copy-start.115 = (pred[120]{0:T(512)(128)(4,1)S(1)}, pred[120]{0:T(512)(128)(4,1)}, u32[]{:S(2)}) copy-start(pred[120]{0:T(512)(128)(4,1)} %add_compare_fusion.1) | copy-start | bytes 364
  537.8 175.8 %collective-permute-start.7 = (bf16[100,1600]{1,0:T(8,128)(2,1)}, bf16[100,1600]{1,0:T(8,128)(2,1)}, u32[]{:S(2)}, u32[]{:S(2)}) collective-permute-start(bf16[100,1600]{1,0:T(8,128)(2,1)} %get-tuple-element.101), channel_id=1, source_target_pairs={{0,16},{1,17},{2,18},{3,19},{4,20},{5,21},{6,22},{7,23},{8,24},{9,... | collective-permute-start | bytes 960008 | tf_op jit(solution)/shard_map/ppermute | solution.py:1075
  590.3 123.4 %collective-permute-start.6 = (bf16[120,1600]{1,0:T(8,128)(2,1)}, bf16[120,1600]{1,0:T(8,128)(2,1)}, u32[]{:S(2)}, u32[]{:S(2)}) collective-permute-start(bf16[120,1600]{1,0:T(8,128)(2,1)} %get-tuple-element.93), channel_id=1, source_target_pairs={{0,16},{1,17},{2,18},{3,19},{4,20},{5,21},{6,22},{7,23},{8,24},{9,... | collective-permute-start | bytes 1152008 | tf_op jit(solution)/shard_map/ppermute | solution.py:1075
  595.4 39.7 %all-to-all-start.1 = ((bf16[16,128,2,200]{1,3,2,0:T(8,128)(2,1)}), bf16[16,128,2,200]{1,3,2,0:T(8,128)(2,1)S(1)}, u32[]{:S(2)}, u32[]{:S(2)}) async-start(bf16[16,128,2,200]{1,3,2,0:T(8,128)(2,1)} %copy.197), calls=%async_computation.2 | async-start | bytes 3276800 | tf_op jit(solution)/shard_map/all_to_all | solution.py:1083
  643.3 67.5 %collective-permute-start.5 = (bf16[200,1600]{1,0:T(8,128)(2,1)}, bf16[200,1600]{1,0:T(8,128)(2,1)}, u32[]{:S(2)}, u32[]{:S(2)}) collective-permute-start(bf16[200,1600]{1,0:T(8,128)(2,1)} %get-tuple-element.235), channel_id=1, source_target_pairs={{0,16},{1,17},{2,18},{3,19},{4,20},{5,21},{6,22},{7,23},{8,24},{9,... | collective-permute-start | bytes 1920008 | tf_op jit(solution)/shard_map/ppermute | solution.py:1075
  (118 other events, 830.7 us)
Sparse Core Ops, SparseCore 0:
  37.5 71.5 all-gather.16
  111.2 43.7 all-gather.8
  298.1 135.3 all-gather.18
  435.6 51.6 all-gather.10
  488.7 41.6 all-gather.14
  531.9 49.5 all-gather.12
  583.8 107.0 reduce-scatter.1

commit v4 on v3

--- a/solution.py
+++ b/solution.py
@@ -1147,7 +1147,9 @@
     normed = scaled_norm(layer_in, mixer_gain).astype(jnp.bfloat16)
     query_weight = attn_weight[:, :model_width]
     kv_weight = attn_weight[:, model_width:qkv_cols]
+    cot_rows = gathered(cotangent, groups)
     kv = jnp.dot(normed, kv_weight, preferred_element_type=jnp.float32).astype(jnp.bfloat16)
+    kv = after(kv, cot_rows)
     queries = lax.dot_general(
         query_weight, normed, (((0,), (1,)), ((), ())), preferred_element_type=jnp.float32
     )
@@ -1235,9 +1237,9 @@
     mixed_terms, mix_pull = jax.vjp(branch_mix, attn_proj, ssm_proj_out, attn_beta, ssm_beta)
     hidden1 = layer_in + mixed_terms
     ffn_in_f, ffn_norm_pull = jax.vjp(scaled_norm, hidden1, ffn_gain)
-    ffn_in = ffn_in_f.astype(jnp.bfloat16)
+    normed_rows = gathered(after(normed, state), groups)
+    ffn_in = after(ffn_in_f.astype(jnp.bfloat16), normed_rows)
     ffn_rows = gather_half([ffn_in], half, 2).reshape(half * row_count, model_width)
-    cot_rows = gathered(cotangent, groups)
     units = FF // half
     wide = (units + 127) // 128 * 128
     in_weight = jnp.concatenate(
@@ -1263,14 +1265,6 @@
     )
     down_low = down_terms[:units].astype(jnp.bfloat16).reshape(2, units // 2, model_width)
     down_low = jnp.where(side == 0, down_low, down_low[::-1])
-    down_sent = [
-        lax.ppermute(
-            down_low[k],
-            "seq",
-            [(h * half + q, 2 * q + (h + k) % 2) for h in range(2) for q in range(half)],
-        )
-        for k in range(2)
-    ]
     grad_from_ffn, grad_ffn_gain = ffn_norm_pull(grad_ffn_in)
     grad_hidden1 = cotangent.astype(jnp.float32) + grad_from_ffn
     grad_attn_proj, grad_ssm_proj_out, grad_attn_beta, grad_ssm_beta = mix_pull(grad_hidden1)
@@ -1294,14 +1288,20 @@
 
     grad_kv = sum_half(kv_terms, 2, half, 1)
     grad_gate_up = complete(gate_keep, gate_sent, grad_queries)
-    grad_ffn_down = sum(after(sent, grad_queries).astype(jnp.float32) for sent in down_sent)
-    grad_kv = after(grad_kv, (grad_gate_up, grad_ffn_down))
+    down_sent = [
+        lax.ppermute(
+            after(down_low[k], grad_kv),
+            "seq",
+            [(h * half + q, 2 * q + (h + k) % 2) for h in range(2) for q in range(half)],
+        )
+        for k in range(2)
+    ]
+    grad_kv = after(grad_kv, grad_gate_up)
     qkv_grad = jnp.concatenate(
         [grad_queries.reshape(model_width, row_count).T, grad_kv.astype(jnp.bfloat16)], 1
     )
     gated_columns = swapped([gated], half, groups, grad_kv)[0]
     attn_columns = swapped([jnp.concatenate([qkv_grad, attended], 1)], half, groups)[0]
-    normed_rows = gathered(normed, groups)
     attn_grad_rows = gathered(attn_grad_low, groups)
     ssm_grad_rows = gathered(ssm_grad_low, groups)
     attn_terms = []
@@ -1346,6 +1346,7 @@
     )
     grad_step_bias, grad_decay, grad_skip = grad_heads[0], grad_heads[1], grad_heads[2]
     out_sum = summed_rows(after(out_terms, grad_raw), groups)
+    grad_ffn_down = sum(after(sent, grad_raw).astype(jnp.float32) for sent in down_sent)
     tail_back = from_behind(grad_tail[8 - CONV + 1 :].astype(jnp.bfloat16), "seq", -1)
     end_rows = end_rows[8 - CONV + 1 :] + tail_back.astype(jnp.float32)
     grad_select_in = jnp.concatenate([grad_b, grad_c, grad_raw], 1).astype(jnp.bfloat16)
@@ -1398,7 +1399,7 @@
         pieces + [jnp.zeros((share * devices - sum(counts), model_width), jnp.float32)], 0
     )
     packed = after(
-        packed, (attn_send, ssm_down_send, ssm_send)
+        packed, (attn_send, ssm_down_send, ssm_send, grad_ffn_down)
     )
     packed = total_of(packed.reshape(devices, share, model_width), devices, 4)
     packed = packed.reshape(devices * share, model_width)

time: 733 us -> 676 us (0.922)
  waiting for transfers between devices: 88.2 us -> 53.6 us
  Pallas kernels: 366 us -> 332 us
    all_gather x4, waiting for transfers between devices: 65.3 us -> 14.3 us  [gathered(): return lax.all_gather(x, 'seq', axis_index_groups=groups, tiled=True)]
    all_to_all x3, waiting for transfers between devices: 21.2 us -> 37.4 us  [swapped(): lax.all_to_all(packed, 'seq', 0, 0, axis_index_groups=groups, tiled=True)]
    pallas_call x1, Pallas kernels: 50 us -> 37.6 us  [gather_half(): pl.pallas_call(partial(gather_kernel, count, half), out_shape=jax.ShapeDt...]
    pallas_call x2, Pallas kernels: 119 us -> 107 us  [sum_half(): pl.pallas_call(partial(sum_kernel, arrays, half), out_shape=jax.ShapeDtyp...]
    unnamed x254 -> x256, local copies, waits for them, and re-layouts: 27.7 us -> 28.8 us
  transfers between devices with their start and end apart: 18 -> 18, of which waited for: 4 -> 3; matrix products, arithmetic and copies ran while one was open for 23% -> 28% of each run, Pallas kernels for 39% -> 32%
where the time goes in v4:
time: 676 us; the launch traced here: 669 us
  Pallas kernels  332 us (49%)
  matrix products  98.9 us (15%)
  local copies, waits for them, and re-layouts  80 us (12%)
  waiting for transfers between devices  53.6 us (8%)
  starting transfers between devices  42.9 us (6%)
  other arithmetic  42.8 us (6%)
  between operations  18.4 us (3%)
    pallas_call x2, Pallas kernels, sum_half(): pl.pallas_call(partial(sum_kernel, arrays, half), out_shape=jax.ShapeDtyp...  107 us
    pallas_call x1, Pallas kernels, total_of(): pl.pallas_call(partial(total_kernel, devices), out_shape=jax.ShapeDtypeSt...  56.6 us
    pallas_call x1, Pallas kernels, gather_both(): pl.pallas_call(partial(gather_both_kernel, count, half), out_shape=[jax.S...  48.6 us
    pallas_call x1, Pallas kernels, ffn(): pl.pallas_call(ffn_kernel, grid=(rows // block,), out_shape=[jax.ShapeDty...  43.3 us
    pallas_call x1, Pallas kernels, gather_half(): pl.pallas_call(partial(gather_kernel, count, half), out_shape=jax.ShapeDt...  37.6 us
    all_to_all x3, waiting for transfers between devices, swapped(): lax.all_to_all(packed, 'seq', 0, 0, axis_index_groups=groups, tiled=True)  37.4 us
    unnamed x256, local copies, waits for them, and re-layouts  28.8 us
    all_to_all x3, starting transfers between devices, swapped(): lax.all_to_all(packed, 'seq', 0, 0, axis_index_groups=groups, tiled=True)  18.5 us
  transfers between devices with their start and end apart: 18, of which 3 were waited for; matrix products, arithmetic and copies ran while one was open for 28% of the time, Pallas kernels for 32%

profile of v4, /device:TPU:0, one launch (start us, length us, event | category | flops | bytes accessed | tf_op | source)
XLA Modules:
  0.0 668.6 jit_solution(3626516281836747575)
XLA Ops:
  14.4 10.2 %fusion.64.proj_ref = f32[128,6400]{1,0:T(8,128)S(1)} fusion(bf16[128,1600]{1,0:T(8,128)(2,1)} %multiply_convert_fusion.1, bf16[1600,6400]{1,0:T(8,128)(2,1)} %param.24), kind=kOutput, calls=%fused_computation.162 | convolution fusion | flops 2621440000 | bytes 24166400 | tf_op jit(solution)/shard_map/dot_general | solution.py:1159
  65.4 48.6 %gather_both.1 = (bf16[32,128,640]{2,1,0:T(8,128)(2,1)}, f32[32,8,128]{2,1,0:T(8,128)}) custom-call(bf16[128,640]{1,0:T(8,128)(2,1)} %fusion.27.refs_0_, f32[8,128]{1,0:T(8,128)} %broadcast_in_dim.193.refs_1_), custom_call_target="tpu_custom_call" | custom-call | bytes 150000000 | tf_op jit(solution)/shard_map/gather_both/pallas_call | solution.py:225
  117.1 5.6 attend.1
  134.0 5.9 ssm_output.1
  140.0 6.8 %multiply_reduce_fusion.10 = (f32[128]{0:T(128)S(1)}, f32[128,1600]{0,1:T(8,128)S(1)}) fusion(bf16[128,3200]{1,0:T(8,128)(2,1)S(1)} %get-tuple-element.78, bf16[3200,1600]{0,1:T(8,128)(2,1)} %param.30), kind=kOutput, calls=%fused_computation.70 | convolution fusion | flops 1311129472 | bytes 11878912 | tf_op jit(solution)/shard_map/dot_general | solution.py:1236
  150.8 14.3 %all-gather.11.cloned.1.call-done = bf16[2048,1600]{1,0:T(8,128)(2,1)} async-done(((bf16[128,1600]{1,0:T(8,128)(2,1)}), bf16[2048,1600]{1,0:T(8,128)(2,1)}) %all-gather.11.cloned.1.call-update) | async-done | bytes 6553616 | tf_op jit(solution)/shard_map/all_gather | solution.py:1058
  165.0 37.6 %gather_half.1 = bf16[16,128,1600]{2,1,0:T(8,128)(2,1)} custom-call(bf16[128,1600]{1,0:T(8,128)(2,1)} %multiply_convert_fusion.refs_0_), custom_call_target="tpu_custom_call" | custom-call | bytes 120000000 | tf_op jit(solution)/shard_map/gather_half/pallas_call | solution.py:139
  202.6 43.3 %ffn.1 = (bf16[2048,1600]{1,0:T(8,128)(2,1)}, bf16[2048,1600]{1,0:T(8,128)(2,1)}, f32[768,1600]{1,0:T(8,128)}, f32[384,1600]{1,0:T(8,128)}) custom-call(bf16[2048,1600]{1,0:T(8,128)(2,1)} %bitcast.150, bf16[2048,1600]{1,0:T(8,128)(2,1)} %all-gather.9.cloned.1.call-done.cot_ref, bf16[1600,768]{1,0:T(8,128)(2,1)} %fusion.15.in_ref, bf16[384,1600]{1,0:T(8,128)(2,1)} %pad.30.down_ref), custom_call_target="tpu_custom_call" | custom-call | bytes 105000000 | tf_op jit(solution)/shard_map/ffn/pallas_call | solution.py:498
  245.9 35.4 %sum_half.2 = f32[128,1600]{1,0:T(8,128)} custom-call(bf16[16,128,1600]{2,1,0:T(8,128)(2,1)} %bitcast.151), custom_call_target="tpu_custom_call" | custom-call | bytes 150000000 | tf_op jit(solution)/shard_map/sum_half/pallas_call | solution.py:440
  287.1 5.9 convolution_convert_fusion.grad_ref
  300.7 6.3 collective-permute-start.2
  314.1 7.8 %fusion.16 = bf16[128,1600]{0,1:T(8,128)(2,1)} fusion(bf16[128,1600]{1,0:T(8,128)(2,1)S(1)} %copy-done.88, bf16[1600,3840]{1,0:T(8,128)(2,1)} %param.23), kind=kOutput, calls=%fused_computation.23 | convolution fusion | flops 655564800 | bytes 6144000 | tf_op jit(solution)/shard_map/dot_general | solution.py:1277
  321.8 7.5 %attend_back.1 = (bf16[5,5,64,128]{3,2,1,0:T(8,128)(2,1)}, bf16[32,128,640]{2,1,0:T(8,128)(2,1)}) custom-call(s32[2]{0:T(128)} %pad_add_fusion.steps_ref, bf16[5,5,64,128]{3,2,1,0:T(8,128)(2,1)} %bitcast.161, bf16[32,128,640]{2,1,0:T(8,128)(2,1)} %get-tuple-element.69.kv_ref, s32[1,128]{1,0:T(1,128)} %bitcast.175, ...), custom_call_target="tpu_custom_call" | custom-call | bytes 60000000 | tf_op jit(solution)/shard_map/attend_back/pallas_call | solution.py:651
  329.4 72.0 %sum_half.3 = f32[128,640]{1,0:T(8,128)} custom-call(bf16[32,128,640]{2,1,0:T(8,128)(2,1)} %get-tuple-element.94.refs_0_), custom_call_target="tpu_custom_call" | custom-call | bytes 150000000 | tf_op jit(solution)/shard_map/sum_half/pallas_call | solution.py:440
  417.5 5.9 collective-permute-start.4
  428.6 24.2 %all-to-all-done = bf16[16,128,2,120]{1,3,2,0:T(8,128)(2,1)} async-done(((bf16[16,128,2,120]{1,3,2,0:T(8,128)(2,1)}), bf16[16,128,2,120]{1,3,2,0:T(8,128)(2,1)}, u32[]{:S(2)}, u32[]{:S(2)}) %all-to-all-start) | async-done | bytes 983072 | tf_op jit(solution)/shard_map/all_to_all | solution.py:1083
  465.6 15.3 %ssm_back.1 = (bf16[128,3200]{1,0:T(8,128)(2,1)S(1)}, bf16[128,3200]{1,0:T(8,128)(2,1)S(1)}, f32[8,3200]{1,0:T(8,128)S(1)}, f32[8,3200]{1,0:T(8,128)S(1)}, f32[1...) custom-call(f32[128,6400]{1,0:T(8,128)} %copy-done.2, ...), custom_call_target="tpu_custom_call" | custom-call | bytes 60000000 | tf_op jit(solution)/shard_map/ssm_back/pallas_call | solution.py:1031
  509.2 5.8 collective-permute-start.7
  527.9 9.8 %all-to-all-start.1 = ((bf16[16,128,2,200]{1,3,2,0:T(8,128)(2,1)}), bf16[16,128,2,200]{1,3,2,0:T(8,128)(2,1)}, u32[]{:S(2)}, u32[]{:S(2)}) async-start(bf16[16,128,2,200]{1,3,2,0:T(8,128)(2,1)} %copy.197), calls=%async_computation.2 | async-start | bytes 3276800 | tf_op jit(solution)/shard_map/all_to_all | solution.py:1083
  537.7 10.6 %fusion.66 = f32[128,1600]{1,0:T(8,128)S(1)} fusion(bf16[128,6400]{1,0:T(8,128)(2,1)S(1)} %pad_maximum_fusion, bf16[1600,6400]{1,0:T(8,128)(2,1)} %param.24), kind=kOutput, calls=%fused_computation.164 | convolution fusion | flops 2621440000 | bytes 22937600 | tf_op jit(solution)/shard_map/dot_general | solution.py:1370
  548.4 5.7 fusion.12
  560.1 6.5 concatenate.37
  566.6 13.2 %all-to-all-done.1 = bf16[16,128,2,200]{1,3,2,0:T(8,128)(2,1)} async-done(((bf16[16,128,2,200]{1,3,2,0:T(8,128)(2,1)}), bf16[16,128,2,200]{1,3,2,0:T(8,128)(2,1)}, u32[]{:S(2)}, u32[]{:S(2)}) %all-to-all-start.1) | async-done | bytes 1638432 | tf_op jit(solution)/shard_map/all_to_all | solution.py:1083
  591.5 56.6 %total_of.1 = f32[32,8,1600]{2,1,0:T(8,128)S(1)} custom-call(f32[32,8,1600]{2,1,0:T(8,128)S(1)} %bitcast.138), custom_call_target="tpu_custom_call" | custom-call | bytes 120000000 | tf_op jit(solution)/shard_map/total_of/pallas_call | solution.py:321
  (420 shorter events, 189.4 us)
Async XLA Ops:
  7.2 57.6 %all-gather.9.cloned.1.call-start = ((), (), s32[]{:S(2)}) async-start(), calls=%async_computation.4 | async-start | bytes 7241728 | tf_op jit(solution)/shard_map/all_gather | solution.py:1058
  9.3 122.0 %all-gather.17.cloned.1.call-start = ((), (), s32[]{:S(2)}) async-start(), calls=%async_computation.9 | async-start | bytes 3379200 | tf_op jit(solution)/shard_map/all_gather | solution.py:1187
  25.2 3.6 collective-permute-start
  38.8 26.0 %copy-start.61 = (f32[1,50]{1,0:T(1,128)}, f32[1,50]{1,0:T(1,128)S(1)}, u32[]{:S(2)}) copy-start(f32[1,50]{1,0:T(1,128)S(1)} %get-tuple-element.67) | copy-start | bytes 604
  38.8 126.2 %all-gather.11.cloned.1.call-start = ((), (), s32[]{:S(2)}) async-start(), calls=%async_computation.5 | async-start | bytes 7241728 | tf_op jit(solution)/shard_map/all_gather | solution.py:1058
  39.5 420.7 %all-gather.19.cloned.1.call-start = ((), (), s32[]{:S(2)}) async-start(), calls=%async_computation.10 | async-start | bytes 3379200 | tf_op jit(solution)/shard_map/all_gather | solution.py:1319
  51.0 82.9 %copy-start.21 = (f32[128,128]{1,0:T(8,128)}, f32[128,128]{1,0:T(8,128)S(1)}, u32[]{:S(2)}) copy-start(f32[128,128]{1,0:T(8,128)S(1)} %fusion.50.same_ref) | copy-start | bytes 196612
  149.7 133.5 %copy-start.65 = (f32[128,1600]{1,0:T(8,128)}, f32[128,1600]{1,0:T(8,128)S(1)}, u32[]{:S(2)}) copy-start(f32[128,1600]{1,0:T(8,128)S(1)} %get-tuple-element.222) | copy-start | bytes 2457604
  245.9 37.4 %copy-start.73 = (f32[128,1600]{1,0:T(8,128)S(1)}, f32[128,1600]{1,0:T(8,128)}, u32[]{:S(2)}) copy-start(f32[128,1600]{1,0:T(8,128)} %copy.185) | copy-start | bytes 2457604
  245.9 37.4 %copy-start.83 = (bf16[128,1600]{1,0:T(8,128)(2,1)S(1)}, bf16[128,1600]{1,0:T(8,128)(2,1)}, u32[]{:S(2)}) copy-start(bf16[128,1600]{1,0:T(8,128)(2,1)} %copy.179) | copy-start | bytes 1228804
  296.0 205.6 %all-gather.15.cloned.1.call-start = ((), (), s32[]{:S(2)}) async-start(), calls=%async_computation.8 | async-start | bytes 7241728 | tf_op jit(solution)/shard_map/all_gather | solution.py:1058
  296.6 218.5 %all-gather.13.cloned.1.call-start = ((), (), s32[]{:S(2)}) async-start(), calls=%async_computation.7 | async-start | bytes 7241728 | tf_op jit(solution)/shard_map/all_gather | solution.py:1058
  300.7 100.7 %collective-permute-start.2 = (bf16[344,1600]{1,0:T(8,128)(2,1)}, bf16[344,1600]{1,0:T(8,128)(2,1)}, u32[]{:S(2)}, u32[]{:S(2)}) collective-permute-start(bf16[344,1600]{1,0:T(8,128)(2,1)} %select_convert_fusion), channel_id=1, source_target_pairs={{0,16},{1,17},{2,18},{3,19},{4,20},{5,21},{6,22},{7,23},{8,24},{9,... | collective-permute-start | bytes 3302408 | tf_op jit(solution)/shard_map/ppermute | solution.py:1075
  309.7 97.6 %all-to-all-start.2 = ((bf16[16,128,2,100]{1,2,3,0:T(2,128)(2,1)}), bf16[16,128,2,100]{1,2,3,0:T(2,128)(2,1)S(1)}, u32[]{:S(2)}, u32[]{:S(2)}) async-start(bf16[16,128,2,100]{1,2,3,0:T(2,128)(2,1)} %copy.211), calls=%async_computation.3 | async-start | bytes 1638400 | tf_op jit(solution)/shard_map/all_to_all | solution.py:1083
  407.3 45.5 %all-to-all-start = ((bf16[16,128,2,120]{1,3,2,0:T(8,128)(2,1)}), bf16[16,128,2,120]{1,3,2,0:T(8,128)(2,1)}, u32[]{:S(2)}, u32[]{:S(2)}) async-start(bf16[16,128,2,120]{1,3,2,0:T(8,128)(2,1)} %copy.194), calls=%async_computation.1 | async-start | bytes 1966080 | tf_op jit(solution)/shard_map/all_to_all | solution.py:1083
  411.6 247.6 %reduce-scatter.2.cloned.1.call-start = ((), (), s32[]{:S(2)}) async-start(), calls=%async_computation.6 | async-start | bytes 7241728 | tf_op jit(solution)/shard_map/reduce_scatter | solution.py:1062
  417.5 77.7 %collective-permute-start.4 = (bf16[172,1600]{1,0:T(8,128)(2,1)}, bf16[172,1600]{1,0:T(8,128)(2,1)}, u32[]{:S(2)}, u32[]{:S(2)}) collective-permute-start(bf16[172,1600]{1,0:T(8,128)(2,1)} %get-tuple-element.108), channel_id=1, source_target_pairs={{0,0},{1,2},{2,4},{3,6},{4,8},{5,10},{6,12},{7,14},{8,16},{9,18},{... | collective-permute-start | bytes 1651208 | tf_op jit(solution)/shard_map/ppermute | solution.py:1292
  423.4 71.8 %collective-permute-start.5 = (bf16[172,1600]{1,0:T(8,128)(2,1)}, bf16[172,1600]{1,0:T(8,128)(2,1)}, u32[]{:S(2)}, u32[]{:S(2)}) collective-permute-start(bf16[172,1600]{1,0:T(8,128)(2,1)} %get-tuple-element.110), channel_id=1, source_target_pairs={{0,1},{1,3},{2,5},{3,7},{4,9},{5,11},{6,13},{7,15},{8,17},{9,19},{... | collective-permute-start | bytes 1651208 | tf_op jit(solution)/shard_map/ppermute | solution.py:1292
  493.9 7.5 %collective-permute-start.1 = (bf16[3,3200]{1,0:T(4,128)(2,1)S(1)}, bf16[3,3200]{1,0:T(4,128)(2,1)S(1)}, u32[]{:S(2)}, u32[]{:S(2)}) collective-permute-start(bf16[3,3200]{1,0:T(4,128)(2,1)S(1)} %slice.266), channel_id=1, source_target_pairs={{1,0},{2,1},{3,2},{4,3},{5,4},{6,5},{7,6},{8,7},{9,8},{10,9},{11,1... | collective-permute-start | bytes 57608 | tf_op jit(solution)/shard_map/ppermute | solution.py:1050
  509.2 145.9 %collective-permute-start.7 = (bf16[100,1600]{1,0:T(8,128)(2,1)}, bf16[100,1600]{1,0:T(8,128)(2,1)}, u32[]{:S(2)}, u32[]{:S(2)}) collective-permute-start(bf16[100,1600]{1,0:T(8,128)(2,1)} %get-tuple-element.106), channel_id=1, source_target_pairs={{0,16},{1,17},{2,18},{3,19},{4,20},{5,21},{6,22},{7,23},{8,24},{9,... | collective-permute-start | bytes 960008 | tf_op jit(solution)/shard_map/ppermute | solution.py:1075
  523.8 131.3 %collective-permute-start.6 = (bf16[120,1600]{1,0:T(8,128)(2,1)}, bf16[120,1600]{1,0:T(8,128)(2,1)}, u32[]{:S(2)}, u32[]{:S(2)}) collective-permute-start(bf16[120,1600]{1,0:T(8,128)(2,1)} %get-tuple-element.98), channel_id=1, source_target_pairs={{0,16},{1,17},{2,18},{3,19},{4,20},{5,21},{6,22},{7,23},{8,24},{9,... | collective-permute-start | bytes 1152008 | tf_op jit(solution)/shard_map/ppermute | solution.py:1075
  527.9 51.9 %all-to-all-start.1 = ((bf16[16,128,2,200]{1,3,2,0:T(8,128)(2,1)}), bf16[16,128,2,200]{1,3,2,0:T(8,128)(2,1)}, u32[]{:S(2)}, u32[]{:S(2)}) async-start(bf16[16,128,2,200]{1,3,2,0:T(8,128)(2,1)} %copy.197), calls=%async_computation.2 | async-start | bytes 3276800 | tf_op jit(solution)/shard_map/all_to_all | solution.py:1083
  560.1 26.3 %slice-start = ((s8[6815744]{0:T(1024)(128)(4,1)}), s8[2621440]{0:T(1024)(128)(4,1)S(1)}, s32[]{:S(2)}) async-start(s8[6815744]{0:T(1024)(128)(4,1)} %bitcast.148), calls=%async_computation.11 | async-start | bytes 5242880
  589.4 62.8 %collective-permute-start.3 = (bf16[200,1600]{1,0:T(8,128)(2,1)}, bf16[200,1600]{1,0:T(8,128)(2,1)}, u32[]{:S(2)}, u32[]{:S(2)}) collective-permute-start(bf16[200,1600]{1,0:T(8,128)(2,1)} %get-tuple-element.245), channel_id=1, source_target_pairs={{0,16},{1,17},{2,18},{3,19},{4,20},{5,21},{6,22},{7,23},{8,24},{9,... | collective-permute-start | bytes 1920008 | tf_op jit(solution)/shard_map/ppermute | solution.py:1075
  (119 other events, 598.9 us)
Sparse Core Ops, SparseCore 0:
  10.2 45.0 all-gather.8
  58.8 63.8 all-gather.16
  124.2 40.7 all-gather.10
  296.1 93.8 all-gather.18
  391.4 78.5 all-gather.14
  471.5 42.4 all-gather.12
  516.3 108.7 reduce-scatter.1

commit v5 on v4

--- a/solution.py
+++ b/solution.py
@@ -314,14 +314,15 @@
         copy.wait_send()
 
 
-def total_of(terms, devices, collective_id):
+def total_of(terms, devices, collective_id, *early):
     pairs = devices // 2
     half_shape = (pairs,) + terms.shape[1:]
     semaphores = pltpu.SemaphoreType.DMA((4, pairs))
     return pl.pallas_call(
-        partial(total_kernel, devices),
+        lambda terms, *refs: total_kernel(devices, terms, *refs[len(early) :]),
         out_shape=jax.ShapeDtypeStruct(terms.shape, terms.dtype),
-        in_specs=[pl.BlockSpec(memory_space=pltpu.VMEM)],
+        in_specs=[pl.BlockSpec(memory_space=pltpu.VMEM)]
+        + [pl.BlockSpec(memory_space=pl.ANY)] * len(early),
         out_specs=pl.BlockSpec(memory_space=pltpu.VMEM),
         scratch_shapes=[pltpu.VMEM(half_shape, terms.dtype)] * 3 + [semaphores] * 4,
         compiler_params=pltpu.CompilerParams(
@@ -329,7 +330,7 @@
         ),
         cost_estimate=cost(40),
         name="total_of",
-    )(terms)
+    )(terms, *early)
 
 
 def sum_kernel(arrays, half, *refs):
@@ -432,15 +433,15 @@
         copy.wait_send()
 
 
-def sum_half(terms, arrays, half, collective_id):
+def sum_half(terms, arrays, half, collective_id, *early):
     rows, columns = terms.shape[1:]
     pairs = half // 2
     block = (rows, columns)
     semaphores = pltpu.SemaphoreType.DMA((arrays, 3, pairs))
     return pl.pallas_call(
-        partial(sum_kernel, arrays, half),
+        lambda terms, *refs: sum_kernel(arrays, half, terms, *refs[len(early) :]),
         out_shape=jax.ShapeDtypeStruct(block, jnp.float32),
-        in_specs=[pl.BlockSpec(memory_space=pl.ANY)],
+        in_specs=[pl.BlockSpec(memory_space=pl.ANY)] * (1 + len(early)),
         out_specs=pl.BlockSpec(memory_space=pltpu.VMEM),
         scratch_shapes=[
             pltpu.VMEM((arrays, pairs) + block, terms.dtype),
@@ -458,7 +459,7 @@
         ),
         cost_estimate=cost(50),
         name="sum_half",
-    )(terms)
+    )(terms, *early)
 
 
 def ffn_kernel(x_ref, cot_ref, in_ref, down_ref, out_ref, grad_in_ref, grad_w_ref, grad_d_ref):
@@ -1062,6 +1063,14 @@
     return lax.psum_scatter(x, "seq", scatter_dimension=0, axis_index_groups=groups, tiled=True)
 
 
+def behind(x, late):
+    return x + (0.0 * late.reshape(-1)[0].astype(jnp.float32)).astype(x.dtype)
+
+
+def corner(x):
+    return x[:16, :128]
+
+
 def after(x, late):
     return lax.optimization_barrier((x, late))[0]
 
@@ -1082,7 +1091,7 @@
     packed = jnp.transpose(packed, (2, 0, 1, 3))
     packed = lax.all_to_all(packed, "seq", 0, 0, axis_index_groups=groups, tiled=True)
     if late is not None:
-        packed = after(packed, late)
+        packed = behind(packed, late)
     packed = packed.reshape(half * rows, 2, -1)
     out, at = [], 0
     for width in widths:
@@ -1284,9 +1293,11 @@
         steps, queries, kv_all, first[None, :], attn_full, log_sum, out_grad, half
     )
     def complete(keep, sent, late):
-        return keep + after(sent, late).astype(jnp.float32)
-
-    grad_kv = sum_half(kv_terms, 2, half, 1)
+        return keep + behind(sent.astype(jnp.float32), late)
+
+    gated_columns = swapped([gated], half, groups)[0]
+    grad_kv = sum_half(kv_terms, 2, half, 1, corner(gated_columns[0]))
+    out_sum = summed_rows(after(out_terms, grad_kv), groups)
     grad_gate_up = complete(gate_keep, gate_sent, grad_queries)
     down_sent = [
         lax.ppermute(
@@ -1300,24 +1311,10 @@
     qkv_grad = jnp.concatenate(
         [grad_queries.reshape(model_width, row_count).T, grad_kv.astype(jnp.bfloat16)], 1
     )
-    gated_columns = swapped([gated], half, groups, grad_kv)[0]
-    attn_columns = swapped([jnp.concatenate([qkv_grad, attended], 1)], half, groups)[0]
-    attn_grad_rows = gathered(attn_grad_low, groups)
-    ssm_grad_rows = gathered(ssm_grad_low, groups)
-    attn_terms = []
-    for k in range(2):
-        block = attn_columns[k]
-        width = block.shape[1]
-        column = (k * half + place) * width + jnp.arange(width, dtype=jnp.int32)
-        attn_terms.append(
-            jnp.where(
-                (column < qkv_cols)[:, None],
-                jnp.dot(block.T, normed_rows, preferred_element_type=jnp.float32),
-                jnp.dot(block.T, attn_grad_rows, preferred_element_type=jnp.float32),
-            )
-        )
     held_grads = lax.all_gather(held_grad(ssm_proj, grad_gated, carry_weight, c_proj), "seq")
-    later_grad = jnp.sum(per_channel(weight_after) * held_grads.astype(jnp.float32), axis=0)
+    later_grad = jnp.sum(
+        per_channel(behind(weight_after, grad_kv)) * held_grads.astype(jnp.float32), axis=0
+    )
     grad_decay_all = jnp.sum((later_grad * held_in).reshape(STATE, sheads, SHEAD), axis=(0, 2))
     grad_all = jnp.pad((grad_decay_all * decay_all[0])[None, :], ((0, 0), (0, 128 - sheads)))
     conv_grad, z_grad, end_rows, grad_tail, grad_b, grad_c, grad_raw, grad_conv, grad_heads = (
@@ -1344,8 +1341,24 @@
             grad_all,
         )
     )
+    attn_columns = swapped(
+        [jnp.concatenate([qkv_grad, attended], 1)], half, groups, grad_raw
+    )[0]
+    attn_grad_rows = gathered(attn_grad_low, groups)
+    ssm_grad_rows = gathered(ssm_grad_low, groups)
+    attn_terms = []
+    for k in range(2):
+        block = attn_columns[k]
+        width = block.shape[1]
+        column = (k * half + place) * width + jnp.arange(width, dtype=jnp.int32)
+        attn_terms.append(
+            jnp.where(
+                (column < qkv_cols)[:, None],
+                jnp.dot(block.T, normed_rows, preferred_element_type=jnp.float32),
+                jnp.dot(block.T, attn_grad_rows, preferred_element_type=jnp.float32),
+            )
+        )
     grad_step_bias, grad_decay, grad_skip = grad_heads[0], grad_heads[1], grad_heads[2]
-    out_sum = summed_rows(after(out_terms, grad_raw), groups)
     grad_ffn_down = sum(after(sent, grad_raw).astype(jnp.float32) for sent in down_sent)
     tail_back = from_behind(grad_tail[8 - CONV + 1 :].astype(jnp.bfloat16), "seq", -1)
     end_rows = end_rows[8 - CONV + 1 :] + tail_back.astype(jnp.float32)
@@ -1364,7 +1377,6 @@
         [conv_grad[: row_count - CONV + 1], end_rows.astype(jnp.bfloat16)], 0
     )
     proj_grad = jnp.concatenate([conv_grad, z_grad], 1)
-    proj_grad = after(proj_grad, attn_send)
     ssm_columns = swapped([proj_grad], half, groups)[0]
     grad_normed = jnp.dot(qkv_grad, attn_weight[:, :qkv_cols].T, preferred_element_type=jnp.float32)
     grad_normed = grad_normed + jnp.dot(proj_grad, ssm_weight.T, preferred_element_type=jnp.float32)
@@ -1401,7 +1413,14 @@
     packed = after(
         packed, (attn_send, ssm_down_send, ssm_send, grad_ffn_down)
     )
-    packed = total_of(packed.reshape(devices, share, model_width), devices, 4)
+    packed = total_of(
+        packed.reshape(devices, share, model_width),
+        devices,
+        4,
+        corner(ssm_send),
+        corner(attn_send),
+        corner(ssm_down_send),
+    )
     packed = packed.reshape(devices * share, model_width)
     at = [sum(counts[:i]) for i in range(len(counts))]
     gains = packed[at[3] : at[4]]

time: 676 us -> 667 us (0.987)
  waiting for transfers between devices: 53.6 us -> 43.5 us
  starting transfers between devices: 42.9 us -> 50.2 us
    all_to_all x3, waiting for transfers between devices: 37.4 us -> 0.01 us  [swapped(): lax.all_to_all(packed, 'seq', 0, 0, axis_index_groups=groups, tiled=True)]
    ppermute x4, waiting for transfers between devices: 0.01 us -> 24.1 us  [exchanged(): return (keep, lax.ppermute(send, 'seq', pairs), send)]
    all_to_all x3, starting transfers between devices: 18.5 us -> 28.2 us  [swapped(): lax.all_to_all(packed, 'seq', 0, 0, axis_index_groups=groups, tiled=True)]
    unnamed x256 -> x246, local copies, waits for them, and re-layouts: 28.8 us -> 26.8 us
  transfers between devices with their start and end apart: 18 -> 18, of which waited for: 3 -> 2; matrix products, arithmetic and copies ran while one was open for 28% -> 28% of each run, Pallas kernels for 32% -> 32%
where the time goes in v5:
time: 667 us; the launch traced here: 661 us
  Pallas kernels  326 us (49%)
  matrix products  95.6 us (14%)
  local copies, waits for them, and re-layouts  76.4 us (11%)
  starting transfers between devices  50.2 us (8%)
  other arithmetic  47.4 us (7%)
  waiting for transfers between devices  43.5 us (7%)
  between operations  21.6 us (3%)
    pallas_call x1, Pallas kernels, total_of(): pl.pallas_call(lambda terms, *refs: total_kernel(devices, terms, *refs[le...  79.9 us
    pallas_call x2, Pallas kernels, sum_half(): pl.pallas_call(lambda terms, *refs: sum_kernel(arrays, half, terms, *refs...  79.4 us
    pallas_call x1, Pallas kernels, gather_both(): pl.pallas_call(partial(gather_both_kernel, count, half), out_shape=[jax.S...  50.1 us
    pallas_call x1, Pallas kernels, ffn(): pl.pallas_call(ffn_kernel, grid=(rows // block,), out_shape=[jax.ShapeDty...  43.2 us
    pallas_call x1, Pallas kernels, gather_half(): pl.pallas_call(partial(gather_kernel, count, half), out_shape=jax.ShapeDt...  35.1 us
    all_to_all x3, starting transfers between devices, swapped(): lax.all_to_all(packed, 'seq', 0, 0, axis_index_groups=groups, tiled=True)  28.2 us
    unnamed x246, local copies, waits for them, and re-layouts  26.8 us
    ppermute x4, waiting for transfers between devices, exchanged(): return (keep, lax.ppermute(send, 'seq', pairs), send)  24.1 us
  transfers between devices with their start and end apart: 18, of which 2 were waited for; matrix products, arithmetic and copies ran while one was open for 28% of the time, Pallas kernels for 32%

profile of v5, /device:TPU:0, one launch (start us, length us, event | category | flops | bytes accessed | tf_op | source)
XLA Modules:
  0.0 661.0 jit_solution(17717540953876974851)
XLA Ops:
  14.4 10.1 %fusion.64.proj_ref = f32[128,6400]{1,0:T(8,128)S(1)} fusion(bf16[128,1600]{1,0:T(8,128)(2,1)} %multiply_convert_fusion.1, bf16[1600,6400]{1,0:T(8,128)(2,1)} %param.24), kind=kOutput, calls=%fused_computation.163 | convolution fusion | flops 2621440000 | bytes 24166400 | tf_op jit(solution)/shard_map/dot_general | solution.py:1168
  55.5 5.4 fusion.22
  61.6 50.1 %gather_both.1 = (bf16[32,128,640]{2,1,0:T(8,128)(2,1)}, f32[32,8,128]{2,1,0:T(8,128)}) custom-call(bf16[128,640]{1,0:T(8,128)(2,1)} %fusion.27.refs_0_, f32[8,128]{1,0:T(8,128)} %broadcast_in_dim.193.refs_1_), custom_call_target="tpu_custom_call" | custom-call | bytes 150000000 | tf_op jit(solution)/shard_map/gather_both/pallas_call | solution.py:225
  114.8 5.6 attend.1
  132.0 5.9 ssm_output.1
  137.9 6.8 %multiply_reduce_fusion.10 = (f32[128]{0:T(128)S(1)}, f32[128,1600]{0,1:T(8,128)S(1)}) fusion(bf16[128,3200]{1,0:T(8,128)(2,1)S(1)} %get-tuple-element.72, bf16[3200,1600]{0,1:T(8,128)(2,1)} %param.30), kind=kOutput, calls=%fused_computation.71 | convolution fusion | flops 1311129472 | bytes 11878912 | tf_op jit(solution)/shard_map/dot_general | solution.py:1245
  148.6 17.5 %all-gather.11.cloned.1.call-done = bf16[2048,1600]{1,0:T(8,128)(2,1)} async-done(((bf16[128,1600]{1,0:T(8,128)(2,1)}), bf16[2048,1600]{1,0:T(8,128)(2,1)}) %all-gather.11.cloned.1.call-update) | async-done | bytes 6553616 | tf_op jit(solution)/shard_map/all_gather | solution.py:1059
  166.1 35.1 %gather_half.1 = bf16[16,128,1600]{2,1,0:T(8,128)(2,1)} custom-call(bf16[128,1600]{1,0:T(8,128)(2,1)} %multiply_convert_fusion.refs_0_), custom_call_target="tpu_custom_call" | custom-call | bytes 120000000 | tf_op jit(solution)/shard_map/gather_half/pallas_call | solution.py:139
  201.2 43.2 %ffn.1 = (bf16[2048,1600]{1,0:T(8,128)(2,1)}, bf16[2048,1600]{1,0:T(8,128)(2,1)}, f32[768,1600]{1,0:T(8,128)}, f32[384,1600]{1,0:T(8,128)}) custom-call(bf16[2048,1600]{1,0:T(8,128)(2,1)} %bitcast.158, bf16[2048,1600]{1,0:T(8,128)(2,1)} %all-gather.9.cloned.1.call-done.cot_ref, bf16[1600,768]{1,0:T(8,128)(2,1)} %fusion.15.in_ref, bf16[384,1600]{1,0:T(8,128)(2,1)} %pad.30.down_ref), custom_call_target="tpu_custom_call" | custom-call | bytes 105000000 | tf_op jit(solution)/shard_map/ffn/pallas_call | solution.py:499
  244.4 34.8 %sum_half.2 = f32[128,1600]{1,0:T(8,128)} custom-call(bf16[16,128,1600]{2,1,0:T(8,128)(2,1)} %bitcast.159), custom_call_target="tpu_custom_call" | custom-call | bytes 150000000 | tf_op jit(solution)/shard_map/sum_half/pallas_call | solution.py:441
  285.1 5.9 convolution_convert_fusion.grad_ref
  298.7 6.5 collective-permute-start.1
  315.5 7.9 %fusion.16 = bf16[128,1600]{0,1:T(8,128)(2,1)} fusion(bf16[128,1600]{1,0:T(8,128)(2,1)} %get-tuple-element.219, bf16[1600,3840]{1,0:T(8,128)(2,1)} %param.23), kind=kOutput, calls=%fused_computation.23 | convolution fusion | flops 655564800 | bytes 6160384 | tf_op jit(solution)/shard_map/dot_general | solution.py:1286
  323.4 7.5 %attend_back.1 = (bf16[5,5,64,128]{3,2,1,0:T(8,128)(2,1)}, bf16[32,128,640]{2,1,0:T(8,128)(2,1)}) custom-call(s32[2]{0:T(128)} %pad_add_fusion.steps_ref, bf16[5,5,64,128]{3,2,1,0:T(8,128)(2,1)} %bitcast.172, bf16[32,128,640]{2,1,0:T(8,128)(2,1)} %get-tuple-element.63.kv_ref, s32[1,128]{1,0:T(1,128)} %bitcast.187, ...), custom_call_target="tpu_custom_call" | custom-call | bytes 60000000 | tf_op jit(solution)/shard_map/attend_back/pallas_call | solution.py:652
  336.5 24.1 %collective-permute-done.1 = bf16[344,1600]{1,0:T(8,128)(2,1)} collective-permute-done((bf16[344,1600]{1,0:T(8,128)(2,1)}, bf16[344,1600]{1,0:T(8,128)(2,1)}, u32[]{:S(2)}, u32[]{:S(2)}) %collective-permute-start.1) | collective-permute-done | bytes 1100832 | tf_op jit(solution)/shard_map/ppermute | solution.py:1084
  366.6 44.6 %sum_half.3 = f32[128,640]{1,0:T(8,128)} custom-call(bf16[32,128,640]{2,1,0:T(8,128)(2,1)} %get-tuple-element.78.terms, bf16[16,100]{1,0:T(8,128)(2,1)} %slice_bitcast_fusion.18.refs_0_), custom_call_target="tpu_custom_call" | custom-call | bytes 150000000 | tf_op jit(solution)/shard_map/sum_half/pallas_call | solution.py:441
  420.2 6.0 collective-permute-start.3
  433.9 15.3 %ssm_back.1 = (bf16[128,3200]{1,0:T(8,128)(2,1)S(1)}, bf16[128,3200]{1,0:T(8,128)(2,1)S(1)}, f32[8,3200]{1,0:T(8,128)S(1)}, f32[8,3200]{1,0:T(8,128)S(1)}, f32[1...) custom-call(f32[128,6400]{1,0:T(8,128)} %copy-done.2, ...), custom_call_target="tpu_custom_call" | custom-call | bytes 60000000 | tf_op jit(solution)/shard_map/ssm_back/pallas_call | solution.py:1032
  463.3 5.4 fusion.43
  478.7 19.4 %all-to-all-start.2 = ((bf16[16,128,2,200]{1,3,2,0:T(8,128)(2,1)}), bf16[16,128,2,200]{1,3,2,0:T(8,128)(2,1)S(1)}, u32[]{:S(2)}, u32[]{:S(2)}) async-start(bf16[16,128,2,200]{1,3,2,0:T(8,128)(2,1)} %copy.212), calls=%async_computation.3 | async-start | bytes 3276800 | tf_op jit(solution)/shard_map/all_to_all | solution.py:1092
  498.1 10.7 %fusion.66 = f32[128,1600]{1,0:T(8,128)S(1)} fusion(bf16[128,6400]{1,0:T(8,128)(2,1)S(1)} %pad_maximum_fusion, bf16[1600,6400]{1,0:T(8,128)(2,1)} %param.24), kind=kOutput, calls=%fused_computation.165 | convolution fusion | flops 2621440000 | bytes 22937600 | tf_op jit(solution)/shard_map/dot_general | solution.py:1382
  508.9 5.8 fusion.12
  521.5 6.4 concatenate.36
  558.9 79.9 %total_of.1 = f32[32,8,1600]{2,1,0:T(8,128)S(1)} custom-call(f32[32,8,1600]{2,1,0:T(8,128)S(1)} %bitcast.143, bf16[16,128]{1,0:T(8,128)(2,1)S(1)} %slice.244.refs_0_, bf16[16,128]{1,0:T(8,128)(2,1)S(1)} %slice.209.refs_1_, bf16[16,128]{1,0:T(8,128)(2,1)S(1)} %slice.210.refs_2_), custom_call_target="tpu_custom_call" | custom-call | bytes 120000000 | tf_op jit(solution)/shard_map/total_of/pallas_call | solution.py:321
  (421 shorter events, 179.5 us)
Async XLA Ops:
  7.2 53.7 %all-gather.9.cloned.1.call-start = ((), (), s32[]{:S(2)}) async-start(), calls=%async_computation.4 | async-start | bytes 7241728 | tf_op jit(solution)/shard_map/all_gather | solution.py:1059
  9.3 119.7 %all-gather.17.cloned.1.call-start = ((), (), s32[]{:S(2)}) async-start(), calls=%async_computation.9 | async-start | bytes 3379200 | tf_op jit(solution)/shard_map/all_gather | solution.py:1196
  25.2 3.6 collective-permute-start
  38.7 127.3 %all-gather.11.cloned.1.call-start = ((), (), s32[]{:S(2)}) async-start(), calls=%async_computation.5 | async-start | bytes 7241728 | tf_op jit(solution)/shard_map/all_gather | solution.py:1059
  39.5 389.6 %all-gather.19.cloned.1.call-start = ((), (), s32[]{:S(2)}) async-start(), calls=%async_computation.10 | async-start | bytes 3379200 | tf_op jit(solution)/shard_map/all_gather | solution.py:1314
  47.2 84.7 %copy-start.21 = (f32[128,128]{1,0:T(8,128)}, f32[128,128]{1,0:T(8,128)S(1)}, u32[]{:S(2)}) copy-start(f32[128,128]{1,0:T(8,128)S(1)} %fusion.50.same_ref) | copy-start | bytes 196612
  147.6 133.6 %copy-start.61 = (f32[128,1600]{1,0:T(8,128)}, f32[128,1600]{1,0:T(8,128)S(1)}, u32[]{:S(2)}) copy-start(f32[128,1600]{1,0:T(8,128)S(1)} %get-tuple-element.210) | copy-start | bytes 2457604
  294.0 244.2 %all-gather.15.cloned.1.call-start = ((), (), s32[]{:S(2)}) async-start(), calls=%async_computation.8 | async-start | bytes 7241728 | tf_op jit(solution)/shard_map/all_gather | solution.py:1059
  294.6 252.7 %all-gather.13.cloned.1.call-start = ((), (), s32[]{:S(2)}) async-start(), calls=%async_computation.7 | async-start | bytes 7241728 | tf_op jit(solution)/shard_map/all_gather | solution.py:1059
  298.7 62.0 %collective-permute-start.1 = (bf16[344,1600]{1,0:T(8,128)(2,1)}, bf16[344,1600]{1,0:T(8,128)(2,1)}, u32[]{:S(2)}, u32[]{:S(2)}) collective-permute-start(bf16[344,1600]{1,0:T(8,128)(2,1)} %select_convert_fusion), channel_id=1, source_target_pairs={{0,16},{1,17},{2,18},{3,19},{4,20},{5,21},{6,22},{7,23},{8,24},{9,... | collective-permute-start | bytes 3302408 | tf_op jit(solution)/shard_map/ppermute | solution.py:1084
  309.0 56.0 %all-to-all-start = ((bf16[16,128,2,100]{1,2,3,0:T(2,128)(2,1)}), bf16[16,128,2,100]{1,2,3,0:T(2,128)(2,1)S(1)}, u32[]{:S(2)}, u32[]{:S(2)}) async-start(bf16[16,128,2,100]{1,2,3,0:T(2,128)(2,1)} %copy.192), calls=%async_computation | async-start | bytes 1638400 | tf_op jit(solution)/shard_map/all_to_all | solution.py:1092
  366.0 45.3 %copy-start.75 = (bf16[16,128,2,100]{3,1,0,2:T(8,128)(2,1)}, bf16[16,128,2,100]{3,1,0,2:T(8,128)(2,1)S(1)}, u32[]{:S(2)}) copy-start(bf16[16,128,2,100]{3,1,0,2:T(8,128)(2,1)S(1)} %copy.193) | copy-start | bytes 2457604
  366.6 45.8 %copy-start.82 = (bf16[5,5,64,128]{3,2,1,0:T(8,128)(2,1)S(1)}, bf16[5,5,64,128]{3,2,1,0:T(8,128)(2,1)}, u32[]{:S(2)}) copy-start(bf16[5,5,64,128]{3,2,1,0:T(8,128)(2,1)} %copy-done.81) | copy-start | bytes 1228804
  414.6 47.2 %all-to-all-start.1 = ((bf16[16,128,2,120]{1,3,2,0:T(8,128)(2,1)}), bf16[16,128,2,120]{1,3,2,0:T(8,128)(2,1)}, u32[]{:S(2)}, u32[]{:S(2)}) async-start(bf16[16,128,2,120]{1,3,2,0:T(8,128)(2,1)} %copy.209), calls=%async_computation.2 | async-start | bytes 1966080 | tf_op jit(solution)/shard_map/all_to_all | solution.py:1092
  419.1 232.6 %reduce-scatter.2.cloned.1.call-start = ((), (), s32[]{:S(2)}) async-start(), calls=%async_computation.6 | async-start | bytes 7241728 | tf_op jit(solution)/shard_map/reduce_scatter | solution.py:1063
  420.2 34.1 %collective-permute-start.3 = (bf16[172,1600]{1,0:T(8,128)(2,1)}, bf16[172,1600]{1,0:T(8,128)(2,1)}, u32[]{:S(2)}, u32[]{:S(2)}) collective-permute-start(bf16[172,1600]{1,0:T(8,128)(2,1)} %get-tuple-element.98), channel_id=1, source_target_pairs={{0,0},{1,2},{2,4},{3,6},{4,8},{5,10},{6,12},{7,14},{8,16},{9,18},{... | collective-permute-start | bytes 1651208 | tf_op jit(solution)/shard_map/ppermute | solution.py:1303
  428.7 25.6 %collective-permute-start.4 = (bf16[172,1600]{1,0:T(8,128)(2,1)}, bf16[172,1600]{1,0:T(8,128)(2,1)}, u32[]{:S(2)}, u32[]{:S(2)}) collective-permute-start(bf16[172,1600]{1,0:T(8,128)(2,1)} %get-tuple-element.100), channel_id=1, source_target_pairs={{0,1},{1,3},{2,5},{3,7},{4,9},{5,11},{6,13},{7,15},{8,17},{9,19},{... | collective-permute-start | bytes 1651208 | tf_op jit(solution)/shard_map/ppermute | solution.py:1303
  455.3 20.5 %collective-permute-start.2 = (bf16[3,3200]{1,0:T(4,128)(2,1)S(1)}, bf16[3,3200]{1,0:T(4,128)(2,1)S(1)}, u32[]{:S(2)}, u32[]{:S(2)}) collective-permute-start(bf16[3,3200]{1,0:T(4,128)(2,1)S(1)} %slice.315), channel_id=1, source_target_pairs={{1,0},{2,1},{3,2},{4,3},{5,4},{6,5},{7,6},{8,7},{9,8},{10,9},{11,1... | collective-permute-start | bytes 57608 | tf_op jit(solution)/shard_map/ppermute | solution.py:1051
  478.7 49.2 %all-to-all-start.2 = ((bf16[16,128,2,200]{1,3,2,0:T(8,128)(2,1)}), bf16[16,128,2,200]{1,3,2,0:T(8,128)(2,1)S(1)}, u32[]{:S(2)}, u32[]{:S(2)}) async-start(bf16[16,128,2,200]{1,3,2,0:T(8,128)(2,1)} %copy.212), calls=%async_computation.3 | async-start | bytes 3276800 | tf_op jit(solution)/shard_map/all_to_all | solution.py:1092
  536.7 103.3 %collective-permute-start.6 = (bf16[200,1600]{1,0:T(8,128)(2,1)}, bf16[200,1600]{1,0:T(8,128)(2,1)}, u32[]{:S(2)}, u32[]{:S(2)}) collective-permute-start(bf16[200,1600]{1,0:T(8,128)(2,1)} %get-tuple-element.236), channel_id=1, source_target_pairs={{0,16},{1,17},{2,18},{3,19},{4,20},{5,21},{6,22},{7,23},{8,24},{9,... | collective-permute-start | bytes 1920008 | tf_op jit(solution)/shard_map/ppermute | solution.py:1084
  546.0 101.1 %collective-permute-start.7 = (bf16[100,1600]{1,0:T(8,128)(2,1)}, bf16[100,1600]{1,0:T(8,128)(2,1)}, u32[]{:S(2)}, u32[]{:S(2)}) collective-permute-start(bf16[100,1600]{1,0:T(8,128)(2,1)} %get-tuple-element.96), channel_id=1, source_target_pairs={{0,16},{1,17},{2,18},{3,19},{4,20},{5,21},{6,22},{7,23},{8,24},{9,... | collective-permute-start | bytes 960008 | tf_op jit(solution)/shard_map/ppermute | solution.py:1084
  555.5 93.9 %collective-permute-start.5 = (bf16[120,1600]{1,0:T(8,128)(2,1)}, bf16[120,1600]{1,0:T(8,128)(2,1)}, u32[]{:S(2)}, u32[]{:S(2)}) collective-permute-start(bf16[120,1600]{1,0:T(8,128)(2,1)} %get-tuple-element.95), channel_id=1, source_target_pairs={{0,16},{1,17},{2,18},{3,19},{4,20},{5,21},{6,22},{7,23},{8,24},{9,... | collective-permute-start | bytes 1152008 | tf_op jit(solution)/shard_map/ppermute | solution.py:1084
  558.9 81.1 %copy-start.85 = (f32[200,1600]{1,0:T(8,128)S(1)}, f32[200,1600]{1,0:T(8,128)}, u32[]{:S(2)}) copy-start(f32[200,1600]{1,0:T(8,128)} %copy-done.84) | copy-start | bytes 3840004
  558.9 81.1 %copy-start.86 = (f32[200,1600]{1,0:T(8,128)S(1)}, f32[200,1600]{1,0:T(8,128)}, u32[]{:S(2)}) copy-start(f32[200,1600]{1,0:T(8,128)} %get-tuple-element.237) | copy-start | bytes 3840004
  (114 other events, 609.6 us)
Sparse Core Ops, SparseCore 0:
  10.2 45.0 all-gather.8
  58.8 63.9 all-gather.16
  125.0 41.0 all-gather.10
  294.1 90.5 all-gather.18
  386.2 83.6 all-gather.14
  471.4 54.9 all-gather.12
  528.7 107.8 reduce-scatter.1

commit v6 on v5

--- a/solution.py
+++ b/solution.py
@@ -1366,6 +1366,13 @@
     attn_keep, attn_sent, attn_send = exchanged(
         attn_terms[0], attn_terms[1], side, half, tail_back
     )
+    conv_grad = jnp.concatenate(
+        [conv_grad[: row_count - CONV + 1], end_rows.astype(jnp.bfloat16)], 0
+    )
+    proj_grad = jnp.concatenate([conv_grad, z_grad], 1)
+    proj_grad = behind(proj_grad, attn_send)
+    ssm_columns = swapped([proj_grad], half, groups)[0]
+    gated_columns = [behind(block, ssm_columns[0]) for block in gated_columns]
     ssm_down_keep, ssm_down_sent, ssm_down_send = exchanged(
         jnp.dot(gated_columns[0].T, ssm_grad_rows, preferred_element_type=jnp.float32),
         jnp.dot(gated_columns[1].T, ssm_grad_rows, preferred_element_type=jnp.float32),
@@ -1373,11 +1380,6 @@
         half,
         tail_back,
     )
-    conv_grad = jnp.concatenate(
-        [conv_grad[: row_count - CONV + 1], end_rows.astype(jnp.bfloat16)], 0
-    )
-    proj_grad = jnp.concatenate([conv_grad, z_grad], 1)
-    ssm_columns = swapped([proj_grad], half, groups)[0]
     grad_normed = jnp.dot(qkv_grad, attn_weight[:, :qkv_cols].T, preferred_element_type=jnp.float32)
     grad_normed = grad_normed + jnp.dot(proj_grad, ssm_weight.T, preferred_element_type=jnp.float32)
     grad_normed = grad_normed + jnp.dot(
@@ -1439,7 +1441,7 @@
     )
     grad_ssm = complete(ssm_keep, ssm_sent, little)
     late = grad_ssm[0]
-    layer_out = (hidden1 + after(out_sum, late).astype(jnp.float32)).astype(jnp.bfloat16)
+    layer_out = (hidden1 + behind(out_sum.astype(jnp.float32), late)).astype(jnp.bfloat16)
     shares = (
         complete(attn_keep, attn_sent, late).T,
         grad_ssm.T,

time: 667 us -> 668 us (level)
  Pallas kernels: 326 us -> 310 us
  local copies, waits for them, and re-layouts: 76.4 us -> 84.4 us
    ppermute x4, starting transfers between devices: 11 us -> 26.6 us  [exchanged(): return (keep, lax.ppermute(send, 'seq', pairs), send)]
    pallas_call x1, Pallas kernels: 79.9 us -> 64.3 us  [total_of(): pl.pallas_call(lambda terms, *refs: total_kernel(devices, terms, *refs[le...]
    all_to_all x3, starting transfers between devices: 28.2 us -> 13.1 us  [swapped(): lax.all_to_all(packed, 'seq', 0, 0, axis_index_groups=groups, tiled=True)]
    unnamed x246 -> x244, local copies, waits for them, and re-layouts: 26.8 us -> 27.4 us
  transfers between devices with their start and end apart: 18 -> 18, of which waited for: 2 -> 3; matrix products, arithmetic and copies ran while one was open for 28% -> 30% of each run, Pallas kernels for 32% -> 30%
where the time goes in v6:
time: 668 us; the launch traced here: 662 us
  Pallas kernels  310 us (46%)
  matrix products  95.2 us (14%)
  local copies, waits for them, and re-layouts  84.4 us (13%)
  starting transfers between devices  50.9 us (8%)
  other arithmetic  50 us (7%)
  waiting for transfers between devices  48.1 us (7%)
  between operations  22.7 us (3%)
    pallas_call x2, Pallas kernels, sum_half(): pl.pallas_call(lambda terms, *refs: sum_kernel(arrays, half, terms, *refs...  79.4 us
    pallas_call x1, Pallas kernels, total_of(): pl.pallas_call(lambda terms, *refs: total_kernel(devices, terms, *refs[le...  64.3 us
    pallas_call x1, Pallas kernels, gather_both(): pl.pallas_call(partial(gather_both_kernel, count, half), out_shape=[jax.S...  50.1 us
    pallas_call x1, Pallas kernels, ffn(): pl.pallas_call(ffn_kernel, grid=(rows // block,), out_shape=[jax.ShapeDty...  43.3 us
    pallas_call x1, Pallas kernels, gather_half(): pl.pallas_call(partial(gather_kernel, count, half), out_shape=jax.ShapeDt...  35.1 us
    unnamed x244, local copies, waits for them, and re-layouts  27.4 us
    ppermute x4, starting transfers between devices, exchanged(): return (keep, lax.ppermute(send, 'seq', pairs), send)  26.6 us
    ppermute x4, waiting for transfers between devices, exchanged(): return (keep, lax.ppermute(send, 'seq', pairs), send)  24 us
  transfers between devices with their start and end apart: 18, of which 3 were waited for; matrix products, arithmetic and copies ran while one was open for 30% of the time, Pallas kernels for 30%

profile of v6, /device:TPU:0, one launch (start us, length us, event | category | flops | bytes accessed | tf_op | source)
XLA Modules:
  0.0 661.7 jit_solution(6651884188970067775)
XLA Ops:
  14.4 10.1 %fusion.80.proj_ref = f32[128,6400]{1,0:T(8,128)S(1)} fusion(bf16[128,1600]{1,0:T(8,128)(2,1)} %multiply_convert_fusion.1, bf16[1600,6400]{1,0:T(8,128)(2,1)} %param.24), kind=kOutput, calls=%fused_computation.178 | convolution fusion | flops 2621440000 | bytes 24166400 | tf_op jit(solution)/shard_map/dot_general | solution.py:1168
  55.7 5.4 fusion.22
  61.8 50.1 %gather_both.1 = (bf16[32,128,640]{2,1,0:T(8,128)(2,1)}, f32[32,8,128]{2,1,0:T(8,128)}) custom-call(bf16[128,640]{1,0:T(8,128)(2,1)} %fusion.33.refs_0_, f32[8,128]{1,0:T(8,128)} %broadcast_in_dim.193.refs_1_), custom_call_target="tpu_custom_call" | custom-call | bytes 150000000 | tf_op jit(solution)/shard_map/gather_both/pallas_call | solution.py:225
  115.0 5.2 attend.1
  121.5 5.4 multiply_reduce_fusion.11
  131.8 5.9 ssm_output.1
  137.7 6.8 %multiply_reduce_fusion.10 = (f32[128]{0:T(128)S(1)}, f32[128,1600]{0,1:T(8,128)S(1)}) fusion(bf16[128,3200]{1,0:T(8,128)(2,1)S(1)} %get-tuple-element.72, bf16[3200,1600]{0,1:T(8,128)(2,1)} %param.30), kind=kOutput, calls=%fused_computation.80 | convolution fusion | flops 1311129472 | bytes 11878912 | tf_op jit(solution)/shard_map/dot_general | solution.py:1245
  148.4 17.7 %all-gather.11.cloned.1.call-done = bf16[2048,1600]{1,0:T(8,128)(2,1)} async-done(((bf16[128,1600]{1,0:T(8,128)(2,1)}), bf16[2048,1600]{1,0:T(8,128)(2,1)}) %all-gather.11.cloned.1.call-update) | async-done | bytes 6553616 | tf_op jit(solution)/shard_map/all_gather | solution.py:1059
  166.1 35.1 %gather_half.1 = bf16[16,128,1600]{2,1,0:T(8,128)(2,1)} custom-call(bf16[128,1600]{1,0:T(8,128)(2,1)} %multiply_convert_fusion.refs_0_), custom_call_target="tpu_custom_call" | custom-call | bytes 120000000 | tf_op jit(solution)/shard_map/gather_half/pallas_call | solution.py:139
  201.2 43.3 %ffn.1 = (bf16[2048,1600]{1,0:T(8,128)(2,1)}, bf16[2048,1600]{1,0:T(8,128)(2,1)}, f32[768,1600]{1,0:T(8,128)}, f32[384,1600]{1,0:T(8,128)}) custom-call(bf16[2048,1600]{1,0:T(8,128)(2,1)} %bitcast.163, bf16[2048,1600]{1,0:T(8,128)(2,1)} %all-gather.9.cloned.1.call-done.cot_ref, bf16[1600,768]{1,0:T(8,128)(2,1)} %fusion.15.in_ref, bf16[384,1600]{1,0:T(8,128)(2,1)} %pad.30.down_ref), custom_call_target="tpu_custom_call" | custom-call | bytes 105000000 | tf_op jit(solution)/shard_map/ffn/pallas_call | solution.py:499
  244.5 34.8 %sum_half.2 = f32[128,1600]{1,0:T(8,128)} custom-call(bf16[16,128,1600]{2,1,0:T(8,128)(2,1)} %bitcast.164), custom_call_target="tpu_custom_call" | custom-call | bytes 150000000 | tf_op jit(solution)/shard_map/sum_half/pallas_call | solution.py:441
  285.2 5.9 convolution_convert_fusion.grad_ref
  298.8 6.4 collective-permute-start.1
  315.6 7.9 %fusion.16 = bf16[128,1600]{0,1:T(8,128)(2,1)} fusion(bf16[128,1600]{1,0:T(8,128)(2,1)} %get-tuple-element.219, bf16[1600,3840]{1,0:T(8,128)(2,1)} %param.23), kind=kOutput, calls=%fused_computation.23 | convolution fusion | flops 655564800 | bytes 6160384 | tf_op jit(solution)/shard_map/dot_general | solution.py:1286
  323.5 7.6 %attend_back.1 = (bf16[5,5,64,128]{3,2,1,0:T(8,128)(2,1)}, bf16[32,128,640]{2,1,0:T(8,128)(2,1)}) custom-call(s32[2]{0:T(128)} %pad_add_fusion.steps_ref, bf16[5,5,64,128]{3,2,1,0:T(8,128)(2,1)} %bitcast.178, bf16[32,128,640]{2,1,0:T(8,128)(2,1)} %get-tuple-element.63.kv_ref, s32[1,128]{1,0:T(1,128)} %bitcast.193, ...), custom_call_target="tpu_custom_call" | custom-call | bytes 60000000 | tf_op jit(solution)/shard_map/attend_back/pallas_call | solution.py:652
  336.7 24.0 %collective-permute-done.1 = bf16[344,1600]{1,0:T(8,128)(2,1)} collective-permute-done((bf16[344,1600]{1,0:T(8,128)(2,1)}, bf16[344,1600]{1,0:T(8,128)(2,1)}, u32[]{:S(2)}, u32[]{:S(2)}) %collective-permute-start.1) | collective-permute-done | bytes 1100832 | tf_op jit(solution)/shard_map/ppermute | solution.py:1084
  366.6 44.6 %sum_half.3 = f32[128,640]{1,0:T(8,128)} custom-call(bf16[32,128,640]{2,1,0:T(8,128)(2,1)} %get-tuple-element.78.terms, bf16[16,100]{1,0:T(8,128)(2,1)} %slice_bitcast_fusion.12.refs_0_), custom_call_target="tpu_custom_call" | custom-call | bytes 150000000 | tf_op jit(solution)/shard_map/sum_half/pallas_call | solution.py:441
  420.3 6.0 collective-permute-start.4
  434.0 15.3 %ssm_back.1 = (bf16[128,3200]{1,0:T(8,128)(2,1)S(1)}, bf16[128,3200]{1,0:T(8,128)(2,1)S(1)}, f32[8,3200]{1,0:T(8,128)S(1)}, f32[8,3200]{1,0:T(8,128)S(1)}, f32[1...) custom-call(f32[128,6400]{1,0:T(8,128)} %copy-done.2, ...), custom_call_target="tpu_custom_call" | custom-call | bytes 60000000 | tf_op jit(solution)/shard_map/ssm_back/pallas_call | solution.py:1032
  490.0 17.3 %collective-permute-start.6 = (bf16[120,1600]{1,0:T(8,128)(2,1)}, bf16[120,1600]{1,0:T(8,128)(2,1)}, u32[]{:S(2)}, u32[]{:S(2)}) collective-permute-start(bf16[120,1600]{1,0:T(8,128)(2,1)} %get-tuple-element.91), channel_id=1, source_target_pairs={{0,16},{1,17},{2,18},{3,19},{4,20},{5,21},{6,22},{7,23},{8,24},{9,... | collective-permute-start | bytes 1152008 | tf_op jit(solution)/shard_map/ppermute | solution.py:1084
  515.5 10.4 %fusion.28 = f32[128,1600]{1,0:T(8,128)S(1)} fusion(bf16[1600,6400]{1,0:T(8,128)(2,1)} %param.24, bf16[128,3200]{1,0:T(8,128)(2,1)S(1)} %copy-done.14, bf16[3,3200]{1,0:T(4,128)(2,1)S(1)} %add_convert_fusion.1, bf16[125,3200]{1,0:T(8,128)(2,1)S(1)} %bitcast.154, bf16[]{:T(256)} %bitcast.40), kind=kOutput, calls=%fused_computation.36 | convolution fusion | flops 2627993600 | bytes 22937602 | tf_op jit(solution)/shard_map/dot_general | solution.py:1384
  525.9 5.8 fusion.12
  536.8 6.4 concatenate.47
  573.0 64.3 %total_of.1 = f32[32,8,1600]{2,1,0:T(8,128)S(1)} custom-call(f32[32,8,1600]{2,1,0:T(8,128)S(1)} %bitcast.147, bf16[16,128]{1,0:T(8,128)(2,1)S(1)} %slice.256.refs_0_, bf16[16,128]{1,0:T(8,128)(2,1)S(1)} %slice.219.refs_1_, bf16[16,128]{1,0:T(8,128)(2,1)S(1)} %slice.220.refs_2_), custom_call_target="tpu_custom_call" | custom-call | bytes 120000000 | tf_op jit(solution)/shard_map/total_of/pallas_call | solution.py:321
  (427 shorter events, 197.4 us)
Async XLA Ops:
  7.2 54.0 %all-gather.9.cloned.1.call-start = ((), (), s32[]{:S(2)}) async-start(), calls=%async_computation.4 | async-start | bytes 7241728 | tf_op jit(solution)/shard_map/all_gather | solution.py:1059
  9.3 119.5 %all-gather.17.cloned.1.call-start = ((), (), s32[]{:S(2)}) async-start(), calls=%async_computation.9 | async-start | bytes 3379200 | tf_op jit(solution)/shard_map/all_gather | solution.py:1196
  25.2 3.6 collective-permute-start
  38.7 127.4 %all-gather.11.cloned.1.call-start = ((), (), s32[]{:S(2)}) async-start(), calls=%async_computation.5 | async-start | bytes 7241728 | tf_op jit(solution)/shard_map/all_gather | solution.py:1059
  39.5 389.6 %all-gather.19.cloned.1.call-start = ((), (), s32[]{:S(2)}) async-start(), calls=%async_computation.10 | async-start | bytes 3379200 | tf_op jit(solution)/shard_map/all_gather | solution.py:1314
  47.4 84.3 %copy-start.21 = (f32[128,128]{1,0:T(8,128)}, f32[128,128]{1,0:T(8,128)S(1)}, u32[]{:S(2)}) copy-start(f32[128,128]{1,0:T(8,128)S(1)} %fusion.64.same_ref) | copy-start | bytes 196612
  147.4 133.9 %copy-start.61 = (f32[128,1600]{1,0:T(8,128)}, f32[128,1600]{1,0:T(8,128)S(1)}, u32[]{:S(2)}) copy-start(f32[128,1600]{1,0:T(8,128)S(1)} %get-tuple-element.210) | copy-start | bytes 2457604
  244.5 36.8 %copy-start.66 = (f32[128,1600]{1,0:T(8,128)S(1)}, f32[128,1600]{1,0:T(8,128)}, u32[]{:S(2)}) copy-start(f32[128,1600]{1,0:T(8,128)} %copy.192) | copy-start | bytes 2457604
  244.5 36.8 %copy-start.78 = (bf16[128,1600]{1,0:T(8,128)(2,1)S(1)}, bf16[128,1600]{1,0:T(8,128)(2,1)}, u32[]{:S(2)}) copy-start(bf16[128,1600]{1,0:T(8,128)(2,1)} %copy.186) | copy-start | bytes 1228804
  294.1 186.0 %all-gather.13.cloned.1.call-start = ((), (), s32[]{:S(2)}) async-start(), calls=%async_computation.7 | async-start | bytes 7241728 | tf_op jit(solution)/shard_map/all_gather | solution.py:1059
  294.7 267.8 %all-gather.15.cloned.1.call-start = ((), (), s32[]{:S(2)}) async-start(), calls=%async_computation.8 | async-start | bytes 7241728 | tf_op jit(solution)/shard_map/all_gather | solution.py:1059
  298.8 61.9 %collective-permute-start.1 = (bf16[344,1600]{1,0:T(8,128)(2,1)}, bf16[344,1600]{1,0:T(8,128)(2,1)}, u32[]{:S(2)}, u32[]{:S(2)}) collective-permute-start(bf16[344,1600]{1,0:T(8,128)(2,1)} %select_convert_fusion), channel_id=1, source_target_pairs={{0,16},{1,17},{2,18},{3,19},{4,20},{5,21},{6,22},{7,23},{8,24},{9,... | collective-permute-start | bytes 3302408 | tf_op jit(solution)/shard_map/ppermute | solution.py:1084
  309.0 56.0 %all-to-all-start = ((bf16[16,128,2,100]{1,2,3,0:T(2,128)(2,1)}), bf16[16,128,2,100]{1,2,3,0:T(2,128)(2,1)S(1)}, u32[]{:S(2)}, u32[]{:S(2)}) async-start(bf16[16,128,2,100]{1,2,3,0:T(2,128)(2,1)} %copy.198), calls=%async_computation | async-start | bytes 1638400 | tf_op jit(solution)/shard_map/all_to_all | solution.py:1092
  366.0 45.3 %copy-start.76 = (bf16[16,128,2,100]{3,1,0,2:T(8,128)(2,1)}, bf16[16,128,2,100]{3,1,0,2:T(8,128)(2,1)S(1)}, u32[]{:S(2)}) copy-start(bf16[16,128,2,100]{3,1,0,2:T(8,128)(2,1)S(1)} %copy.199) | copy-start | bytes 2457604
  366.6 45.8 %copy-start.83 = (bf16[5,5,64,128]{3,2,1,0:T(8,128)(2,1)S(1)}, bf16[5,5,64,128]{3,2,1,0:T(8,128)(2,1)}, u32[]{:S(2)}) copy-start(bf16[5,5,64,128]{3,2,1,0:T(8,128)(2,1)} %copy-done.82) | copy-start | bytes 1228804
  414.6 47.2 %all-to-all-start.1 = ((bf16[16,128,2,120]{1,3,2,0:T(8,128)(2,1)}), bf16[16,128,2,120]{1,3,2,0:T(8,128)(2,1)}, u32[]{:S(2)}, u32[]{:S(2)}) async-start(bf16[16,128,2,120]{1,3,2,0:T(8,128)(2,1)} %copy.206), calls=%async_computation.2 | async-start | bytes 1966080 | tf_op jit(solution)/shard_map/all_to_all | solution.py:1092
  419.1 227.6 %reduce-scatter.2.cloned.1.call-start = ((), (), s32[]{:S(2)}) async-start(), calls=%async_computation.6 | async-start | bytes 7241728 | tf_op jit(solution)/shard_map/reduce_scatter | solution.py:1063
  420.3 34.1 %collective-permute-start.4 = (bf16[172,1600]{1,0:T(8,128)(2,1)}, bf16[172,1600]{1,0:T(8,128)(2,1)}, u32[]{:S(2)}, u32[]{:S(2)}) collective-permute-start(bf16[172,1600]{1,0:T(8,128)(2,1)} %get-tuple-element.98), channel_id=1, source_target_pairs={{0,0},{1,2},{2,4},{3,6},{4,8},{5,10},{6,12},{7,14},{8,16},{9,18},{... | collective-permute-start | bytes 1651208 | tf_op jit(solution)/shard_map/ppermute | solution.py:1303
  428.8 25.6 %collective-permute-start.5 = (bf16[172,1600]{1,0:T(8,128)(2,1)}, bf16[172,1600]{1,0:T(8,128)(2,1)}, u32[]{:S(2)}, u32[]{:S(2)}) collective-permute-start(bf16[172,1600]{1,0:T(8,128)(2,1)} %get-tuple-element.100), channel_id=1, source_target_pairs={{0,1},{1,3},{2,5},{3,7},{4,9},{5,11},{6,13},{7,15},{8,17},{9,19},{... | collective-permute-start | bytes 1651208 | tf_op jit(solution)/shard_map/ppermute | solution.py:1303
  456.5 20.3 %collective-permute-start.2 = (bf16[3,3200]{1,0:T(4,128)(2,1)S(1)}, bf16[3,3200]{1,0:T(4,128)(2,1)S(1)}, u32[]{:S(2)}, u32[]{:S(2)}) collective-permute-start(bf16[3,3200]{1,0:T(4,128)(2,1)S(1)} %slice.333), channel_id=1, source_target_pairs={{1,0},{2,1},{3,2},{4,3},{5,4},{6,5},{7,6},{8,7},{9,8},{10,9},{11,1... | collective-permute-start | bytes 57608 | tf_op jit(solution)/shard_map/ppermute | solution.py:1051
  490.0 162.6 %collective-permute-start.6 = (bf16[120,1600]{1,0:T(8,128)(2,1)}, bf16[120,1600]{1,0:T(8,128)(2,1)}, u32[]{:S(2)}, u32[]{:S(2)}) collective-permute-start(bf16[120,1600]{1,0:T(8,128)(2,1)} %get-tuple-element.91), channel_id=1, source_target_pairs={{0,16},{1,17},{2,18},{3,19},{4,20},{5,21},{6,22},{7,23},{8,24},{9,... | collective-permute-start | bytes 1152008 | tf_op jit(solution)/shard_map/ppermute | solution.py:1084
  511.3 36.5 %all-to-all-start.2 = ((bf16[16,128,2,200]{1,3,2,0:T(8,128)(2,1)}), bf16[16,128,2,200]{1,3,2,0:T(8,128)(2,1)S(1)}, u32[]{:S(2)}, u32[]{:S(2)}) async-start(bf16[16,128,2,200]{1,3,2,0:T(8,128)(2,1)} %copy.208), calls=%async_computation.3 | async-start | bytes 3276800 | tf_op jit(solution)/shard_map/all_to_all | solution.py:1092
  556.8 85.8 %collective-permute-start.3 = (bf16[200,1600]{1,0:T(8,128)(2,1)}, bf16[200,1600]{1,0:T(8,128)(2,1)}, u32[]{:S(2)}, u32[]{:S(2)}) collective-permute-start(bf16[200,1600]{1,0:T(8,128)(2,1)} %get-tuple-element.233), channel_id=1, source_target_pairs={{0,16},{1,17},{2,18},{3,19},{4,20},{5,21},{6,22},{7,23},{8,24},{9,... | collective-permute-start | bytes 1920008 | tf_op jit(solution)/shard_map/ppermute | solution.py:1084
  570.4 80.3 %collective-permute-start.7 = (bf16[100,1600]{1,0:T(8,128)(2,1)}, bf16[100,1600]{1,0:T(8,128)(2,1)}, u32[]{:S(2)}, u32[]{:S(2)}) collective-permute-start(bf16[100,1600]{1,0:T(8,128)(2,1)} %get-tuple-element.96), channel_id=1, source_target_pairs={{0,16},{1,17},{2,18},{3,19},{4,20},{5,21},{6,22},{7,23},{8,24},{9,... | collective-permute-start | bytes 960008 | tf_op jit(solution)/shard_map/ppermute | solution.py:1084
  (113 other events, 545.4 us)
Sparse Core Ops, SparseCore 0:
  10.2 45.0 all-gather.8
  58.8 64.0 all-gather.16
  125.0 41.0 all-gather.10
  294.2 90.4 all-gather.18
  386.2 83.6 all-gather.12
  471.4 38.8 all-gather.14
  512.6 113.0 reduce-scatter.1
